TPU v7x, 128 devices: a whole 4x4x4 slice. The times are simulated.
128 devices in a mesh: dp: 16 (over z, y_lo, core), tensor: 8 (over x, y_hi).
Axes of the slice: x: 4, y: 4 (y_hi: 2, y_lo: 2; y = y_hi * 2 + y_lo), z: 4, core: 2. Of those that a mesh axis runs over, the one named last changes fastest.
Arguments:
- activations: bfloat16 [3072, 4096], P('dp'), may hold values from -6 to 6
- cotangents: bfloat16 [4, 3072, 4096], P(None, 'dp'), may hold values from -6 to 6
- gate_weight: bfloat16 [4096, 7168], P('dp', 'tensor'), may hold values from -0.09375 to 0.09375
- up_weight: bfloat16 [4096, 7168], P('dp', 'tensor'), may hold values from -0.09375 to 0.09375
- down_weight: bfloat16 [4096, 7168], P('dp', 'tensor'), may hold values from -0.046875 to 0.046875
Outputs:
- input_grad: float32 [3072, 4096], P('dp', 'tensor')
- gate_grad: float32 [4096, 7168], P('dp', 'tensor')
- up_grad: float32 [4096, 7168], P('dp', 'tensor')
- down_grad: float32 [4096, 7168], P('dp', 'tensor')
All inputs are finite; a program needn't handle non-finite values.
Results may differ from a plain program's by a relative error of at most 0.0042.
Values may be sent and summed in bfloat16 or wider, within the bound.
No kernel may reach another device: no remote copies, remote signals or barrier semaphores. Data moves between devices by JAX's collectives and lax.ppermute only.
A program may use at most 192 MiB of HBM per device.

v0:
```python
import jax
import jax.numpy as jnp
from jax import lax
from jax.sharding import PartitionSpec as P

FF = 14336


def local(activations, cotangents, gate_weight, up_weight, down_weight):
    unit_count = gate_weight.shape[1]
    first_unit = lax.axis_index("tensor") * unit_count
    band_index = (
        1
        + (first_unit >= FF // 8).astype(jnp.int32)
        + (first_unit >= FF // 4).astype(jnp.int32)
        + (first_unit >= FF // 2).astype(jnp.int32)
    )
    summed = jnp.zeros(activations.shape, jnp.float32)
    for later in range(4):
        included = (later + 1 >= band_index).astype(jnp.float32)
        summed = summed + included * cotangents[later].astype(jnp.float32)
    carried = summed.astype(jnp.bfloat16)
    token_cols, carried_cols = (
        lax.all_to_all(activations, "dp", split_axis=1, concat_axis=0, tiled=True),
        lax.all_to_all(carried, "dp", split_axis=1, concat_axis=0, tiled=True),
    )
    over_rows = (((0,), (0,)), ((), ()))
    over_units = (((1,), (1,)), ((), ()))
    full_gate, full_up, full_down = (
        lax.all_gather(gate_weight, "dp", axis=0, tiled=True),
        lax.all_gather(up_weight, "dp", axis=0, tiled=True),
        lax.all_gather(down_weight, "dp", axis=0, tiled=True),
    )
    gate_pre = jnp.dot(activations, full_gate, preferred_element_type=jnp.float32)
    up_pre = jnp.dot(activations, full_up, preferred_element_type=jnp.float32)
    hidden_grad = jnp.dot(carried, full_down, preferred_element_type=jnp.float32)
    sigmoid_gate = jax.nn.sigmoid(gate_pre)
    silu_gate = gate_pre * sigmoid_gate
    hidden = (silu_gate * up_pre).astype(jnp.bfloat16)
    up_delta = (hidden_grad * silu_gate).astype(jnp.bfloat16)
    gate_delta = (
        hidden_grad * up_pre * sigmoid_gate * (1.0 + gate_pre * (1.0 - sigmoid_gate))
    ).astype(jnp.bfloat16)
    all_gate, all_up, all_hidden = (
        lax.all_gather(gate_delta, "dp", axis=0, tiled=True),
        lax.all_gather(up_delta, "dp", axis=0, tiled=True),
        lax.all_gather(hidden, "dp", axis=0, tiled=True),
    )
    gate_grad = lax.dot_general(token_cols, all_gate, over_rows, preferred_element_type=jnp.float32)
    up_grad = lax.dot_general(token_cols, all_up, over_rows, preferred_element_type=jnp.float32)
    down_grad = lax.dot_general(
        carried_cols, all_hidden, over_rows, preferred_element_type=jnp.float32
    )
    partial_input = lax.dot_general(
        gate_delta, full_gate, over_units, preferred_element_type=jnp.float32
    ) + lax.dot_general(up_delta, full_up, over_units, preferred_element_type=jnp.float32)
    input_grad = lax.psum_scatter(partial_input, "tensor", scatter_dimension=1, tiled=True)
    return (input_grad, gate_grad, up_grad, down_grad)


def solution(mesh):
    return jax.shard_map(
        local,
        mesh=mesh,
        in_specs=(
            P("dp", None),
            P(None, "dp", None),
            P("dp", "tensor"),
            P("dp", "tensor"),
            P("dp", "tensor"),
        ),
        out_specs=(P("dp", "tensor"), P("dp", "tensor"), P("dp", "tensor"), P("dp", "tensor")),
        check_vma=False,
    )
```

profile of v0, /device:TPU:1, one launch (start us, length us, event | category | flops | bytes accessed | tf_op | source)
XLA Modules:
  0.0 403.4 jit_solution(3829597105975033289)
XLA Ops:
  7.2 0.0 all-gather.7.cloned.1.call-start
  7.2 0.7 all-gather.7.cloned.1.call-update
  7.9 0.0 all-gather.11.cloned.1.call-start
  7.9 0.7 all-gather.11.cloned.1.call-update
  8.6 0.0 all-gather.9.cloned.1.call-start
  8.7 0.7 all-gather.9.cloned.1.call-update
  9.4 0.0 all-gather.13.cloned.1.call-start
  9.4 4.0 add_convert_fusion
  13.5 0.0 copy-start.1
  13.5 47.1 %all-gather.7.cloned.1.call-done = bf16[4096,896]{1,0:T(8,128)(2,1)} async-done(((bf16[256,896]{1,0:T(8,128)(2,1)}), bf16[4096,896]{1,0:T(8,128)(2,1)}) %all-gather.7.cloned.1.call-update) | async-done | bytes 7340048 | tf_op jit(solution)/shard_map/all_gather | solution.py:32
  60.6 5.7 %fusion = f32[192,896]{1,0:T(8,128)} fusion(bf16[4096,896]{1,0:T(8,128)(2,1)} %all-gather.7.cloned.1.call-done, bf16[1,192,4096]{2,1,0:T(8,128)(2,1)S(1)} %add_convert_fusion), kind=kOutput, calls=%fused_computation.3 | convolution fusion | flops 1409286144 | bytes 9601024 | tf_op jit(solution)/shard_map/dot_general | solution.py:36
  66.3 44.2 %all-gather.11.cloned.1.call-done = bf16[4096,896]{1,0:T(8,128)(2,1)} async-done(((bf16[256,896]{1,0:T(8,128)(2,1)}), bf16[4096,896]{1,0:T(8,128)(2,1)}) %all-gather.11.cloned.1.call-update) | async-done | bytes 7340048 | tf_op jit(solution)/shard_map/all_gather | solution.py:30
  110.5 0.0 copy-done.1
  110.5 5.7 %fusion.3 = f32[192,896]{1,0:T(8,128)} fusion(bf16[192,4096]{1,0:T(8,128)(2,1)S(1)} %copy-done.1, bf16[4096,896]{1,0:T(8,128)(2,1)} %all-gather.11.cloned.1.call-done), kind=kOutput, calls=%fused_computation.12 | convolution fusion | flops 1409286144 | bytes 9601024 | tf_op jit(solution)/shard_map/dot_general | solution.py:34
  116.3 44.2 %all-gather.9.cloned.1.call-done = bf16[4096,896]{1,0:T(8,128)(2,1)} async-done(((bf16[256,896]{1,0:T(8,128)(2,1)}), bf16[4096,896]{1,0:T(8,128)(2,1)}) %all-gather.9.cloned.1.call-update) | async-done | bytes 7340048 | tf_op jit(solution)/shard_map/all_gather | solution.py:31
  160.5 6.3 %multiply_convert_fusion = (bf16[192,896]{1,0:T(8,128)(2,1)}, bf16[192,896]{1,0:T(8,128)(2,1)}, bf16[192,896]{1,0:T(8,128)(2,1)}) fusion(f32[192,896]{1,0:T(8,128)} %fusion.3, f32[192,896]{1,0:T(8,128)} %fusion, bf16[192,4096]{1,0:T(8,128)(2,1)S(1)} %copy-done.1, bf16[4096,896]{1,0:T(8,128)(2,1)} %all-gather.9.cloned.1.call-done), kind=kOutput, calls=%fused_computation.7 | convolution fusion | flops 1411866624 | bytes 11321344 | tf_op jit(solution)/shard_map/dot_general | solution.py:35
  166.7 0.0 all-gather.13.cloned.1.call-update
  166.8 0.0 all-gather.15.cloned.1.call-start
  166.8 0.5 all-gather.15.cloned.1.call-update
  167.4 0.0 all-gather.17.cloned.1.call-start
  167.4 0.5 all-gather.17.cloned.1.call-update
  167.9 0.0 copy-start.2
  167.9 0.0 reduce-scatter.2.cloned.1.call-start
  168.0 0.0 copy-start
  168.0 5.9 %fusion.4 = f32[192,4096]{1,0:T(8,128)S(1)} fusion(bf16[192,896]{1,0:T(8,128)(2,1)} %get-tuple-element.21, bf16[4096,896]{1,0:T(8,128)(2,1)} %all-gather.11.cloned.1.call-done), kind=kOutput, calls=%fused_computation.13 | convolution fusion | flops 1409286144 | bytes 10829824 | tf_op jit(solution)/shard_map/dot_general | solution.py:54
  173.9 0.0 copy-done.2
  173.9 0.0 copy-done
  173.9 4.2 %convolution_add_fusion = f32[192,4096]{1,0:T(8,128)} fusion(f32[192,4096]{1,0:T(8,128)S(1)} %fusion.4, bf16[192,896]{1,0:T(8,128)(2,1)S(1)} %copy-done.2, bf16[4096,896]{1,0:T(8,128)(2,1)S(1)} %copy-done), kind=kOutput, calls=%fused_computation | convolution fusion | flops 1410072576 | bytes 13975552 | tf_op jit(solution)/shard_map/dot_general | solution.py:56
  178.2 0.0 reduce-scatter.2.cloned.1.call-update
  178.2 1.3 copy.24
  179.5 5.3 %all-to-all-start = ((bf16[192,16,256]{2,0,1:T(8,128)(2,1)}), bf16[192,16,256]{2,0,1:T(8,128)(2,1)S(1)}, u32[]{:S(2)}, u32[]{:S(2)}) async-start(bf16[192,16,256]{2,0,1:T(8,128)(2,1)} %bitcast.34), calls=%async_computation.1 | async-start | bytes 3145728 | tf_op jit(solution)/shard_map/all_to_all | solution.py:24
  184.8 0.4 copy.22
  185.2 1.8 copy.18
  187.0 31.7 %all-to-all-done = bf16[192,16,256]{2,0,1:T(8,128)(2,1)S(1)} async-done(((bf16[192,16,256]{2,0,1:T(8,128)(2,1)}), bf16[192,16,256]{2,0,1:T(8,128)(2,1)S(1)}, u32[]{:S(2)}, u32[]{:S(2)}) %all-to-all-start) | async-done | bytes 1572896 | tf_op jit(solution)/shard_map/all_to_all | solution.py:24
  218.7 5.1 %all-to-all-start.1 = ((bf16[192,16,256]{2,0,1:T(8,128)(2,1)}), bf16[192,16,256]{2,0,1:T(8,128)(2,1)}, u32[]{:S(2)}, u32[]{:S(2)}) async-start(bf16[192,16,256]{2,0,1:T(8,128)(2,1)} %copy.18), calls=%async_computation.2 | async-start | bytes 3145728 | tf_op jit(solution)/shard_map/all_to_all | solution.py:25
  223.8 1.2 all-gather.13.cloned.1.call-done
  225.0 4.2 %convolution_bitcast_fusion.1 = f32[256,896]{0,1:T(8,128)S(1)} fusion(bf16[3072,896]{1,0:T(8,128)(2,1)} %all-gather.13.cloned.1.call-done, bf16[3072,256]{1,0:T(8,128)(2,1)S(1)} %bitcast.35), kind=kOutput, calls=%fused_computation.6 | convolution fusion | flops 1409286144 | bytes 7995392 | tf_op jit(solution)/shard_map/dot_general | solution.py:49
  229.1 1.2 copy.19
  230.4 41.8 %all-gather.15.cloned.1.call-done = bf16[3072,896]{1,0:T(8,128)(2,1)} async-done(((bf16[192,896]{1,0:T(8,128)(2,1)}), bf16[3072,896]{1,0:T(8,128)(2,1)}) %all-gather.15.cloned.1.call-update) | async-done | bytes 5505040 | tf_op jit(solution)/shard_map/all_gather | solution.py:46
  272.2 4.2 %convolution_bitcast_fusion = f32[256,896]{0,1:T(8,128)S(1)} fusion(bf16[3072,896]{1,0:T(8,128)(2,1)} %all-gather.15.cloned.1.call-done, bf16[3072,256]{1,0:T(8,128)(2,1)S(1)} %bitcast.36), kind=kOutput, calls=%fused_computation.5 | convolution fusion | flops 1409286144 | bytes 7995392 | tf_op jit(solution)/shard_map/dot_general | solution.py:50
  276.3 1.2 copy.20
  277.6 0.0 all-to-all-done.1
  277.6 36.7 %all-gather.17.cloned.1.call-done = bf16[3072,896]{1,0:T(8,128)(2,1)} async-done(((bf16[192,896]{1,0:T(8,128)(2,1)}), bf16[3072,896]{1,0:T(8,128)(2,1)}) %all-gather.17.cloned.1.call-update) | async-done | bytes 5505040 | tf_op jit(solution)/shard_map/all_gather | solution.py:47
  314.2 5.8 %fusion.5 = f32[256,896]{1,0:T(8,128)} fusion(bf16[3072,256]{1,0:T(8,128)(2,1)} %bitcast.7, bf16[3072,896]{1,0:T(8,128)(2,1)} %all-gather.17.cloned.1.call-done), kind=kOutput, calls=%fused_computation.14 | convolution fusion | flops 1409286144 | bytes 7995392 | tf_op jit(solution)/shard_map/dot_general | solution.py:51
  320.0 76.5 %reduce-scatter.2.cloned.1.call-done = f32[192,512]{1,0:T(8,128)} async-done(((f32[192,4096]{1,0:T(8,128)}), f32[192,512]{1,0:T(8,128)}) %reduce-scatter.2.cloned.1.call-update) | async-done | bytes 393232 | tf_op jit(solution)/shard_map/reduce_scatter | solution.py:57
Async XLA Ops:
  7.2 53.4 %all-gather.7.cloned.1.call-start = ((), (), s32[]{:S(2)}) async-start(), calls=%async_computation.3 | async-start | bytes 7798784 | tf_op jit(solution)/shard_map/all_gather | solution.py:32
  7.9 102.6 %all-gather.11.cloned.1.call-start = ((), (), s32[]{:S(2)}) async-start(), calls=%async_computation.5 | async-start | bytes 7798784 | tf_op jit(solution)/shard_map/all_gather | solution.py:30
  8.6 151.8 %all-gather.9.cloned.1.call-start = ((), (), s32[]{:S(2)}) async-start(), calls=%async_computation.4 | async-start | bytes 7798784 | tf_op jit(solution)/shard_map/all_gather | solution.py:31
  9.4 215.6 %all-gather.13.cloned.1.call-start = ((), (), s32[]{:S(2)}) async-start(), calls=%async_computation.7 | async-start | bytes 5849088 | tf_op jit(solution)/shard_map/all_gather | solution.py:45
  13.5 97.1 %copy-start.1 = (bf16[192,4096]{1,0:T(8,128)(2,1)S(1)}, bf16[192,4096]{1,0:T(8,128)(2,1)}, u32[]{:S(2)}) copy-start(bf16[192,4096]{1,0:T(8,128)(2,1)} %param.5) | copy-start | bytes 4718596
  166.8 105.4 %all-gather.15.cloned.1.call-start = ((), (), s32[]{:S(2)}) async-start(), calls=%async_computation.8 | async-start | bytes 5849088 | tf_op jit(solution)/shard_map/all_gather | solution.py:46
  167.4 146.9 %all-gather.17.cloned.1.call-start = ((), (), s32[]{:S(2)}) async-start(), calls=%async_computation.9 | async-start | bytes 5849088 | tf_op jit(solution)/shard_map/all_gather | solution.py:47
  167.9 6.0 %copy-start.2 = (bf16[192,896]{1,0:T(8,128)(2,1)S(1)}, bf16[192,896]{1,0:T(8,128)(2,1)}, u32[]{:S(2)}) copy-start(bf16[192,896]{1,0:T(8,128)(2,1)} %get-tuple-element.22) | copy-start | bytes 1032196
  167.9 228.6 %reduce-scatter.2.cloned.1.call-start = ((), (), s32[]{:S(2)}) async-start(), calls=%async_computation.6 | async-start | bytes 3538944 | tf_op jit(solution)/shard_map/reduce_scatter | solution.py:57
  168.0 6.0 %copy-start = (bf16[4096,896]{1,0:T(8,128)(2,1)S(1)}, bf16[4096,896]{1,0:T(8,128)(2,1)}, u32[]{:S(2)}) copy-start(bf16[4096,896]{1,0:T(8,128)(2,1)} %all-gather.9.cloned.1.call-done) | copy-start | bytes 22020100
  179.5 39.2 %all-to-all-start = ((bf16[192,16,256]{2,0,1:T(8,128)(2,1)}), bf16[192,16,256]{2,0,1:T(8,128)(2,1)S(1)}, u32[]{:S(2)}, u32[]{:S(2)}) async-start(bf16[192,16,256]{2,0,1:T(8,128)(2,1)} %bitcast.34), calls=%async_computation.1 | async-start | bytes 3145728 | tf_op jit(solution)/shard_map/all_to_all | solution.py:24
  218.7 58.9 %all-to-all-start.1 = ((bf16[192,16,256]{2,0,1:T(8,128)(2,1)}), bf16[192,16,256]{2,0,1:T(8,128)(2,1)}, u32[]{:S(2)}, u32[]{:S(2)}) async-start(bf16[192,16,256]{2,0,1:T(8,128)(2,1)} %copy.18), calls=%async_computation.2 | async-start | bytes 3145728 | tf_op jit(solution)/shard_map/all_to_all | solution.py:25
Sparse Core Ops, SparseCore 0:
  9.7 50.8 all-gather.6
  62.3 48.1 all-gather.10
  112.2 48.1 all-gather.8
  166.9 58.0 all-gather.12
  226.5 45.6 all-gather.14
  273.7 40.4 all-gather.16
  318.7 77.7 reduce-scatter.1
where the time goes:
time: 404 us; the launch traced here: 403 us
  waiting for transfers between devices  327 us (81%)
  matrix products  42 us (10%)
  between operations  14.2 us (4%)
  starting transfers between devices  10.6 us (3%)
  local copies, waits for them, and re-layouts  6 us (1%)
    reduce_scatter x1, waiting for transfers between devices, local(): lax.psum_scatter(partial_input, 'tensor', scatter_dimension=1, tiled=True)  76.5 us
    all_gather x1, waiting for transfers between devices, local(): lax.all_gather(down_weight, 'dp', axis=0, tiled=True)  47.1 us
    all_gather x1, waiting for transfers between devices, local(): lax.all_gather(up_weight, 'dp', axis=0, tiled=True)  44.2 us
    all_gather x1, waiting for transfers between devices, local(): lax.all_gather(gate_weight, 'dp', axis=0, tiled=True)  44.2 us
    all_gather x1, waiting for transfers between devices, local(): lax.all_gather(up_delta, 'dp', axis=0, tiled=True)  41.8 us
    all_gather x1, waiting for transfers between devices, local(): lax.all_gather(hidden, 'dp', axis=0, tiled=True)  36.7 us
    all_to_all x1, waiting for transfers between devices, local(): lax.all_to_all(activations, 'dp', split_axis=1, concat_axis=0, tiled=True)  31.7 us
  transfers between devices with their start and end apart: 9, of which 8 were waited for; matrix products, arithmetic and copies ran while one was open for 11% of the time, Pallas kernels for 0%

commit v1 on v0

v1 whole, which is shorter than its diff:
```python
import functools

import jax
import jax.numpy as jnp
from jax import lax
from jax.experimental import pallas as pl
from jax.experimental.pallas import tpu as pltpu
from jax.sharding import PartitionSpec as P

FF = 14336
F32 = jnp.float32
BF16 = jnp.bfloat16
VMEM = pl.BlockSpec(memory_space=pltpu.VMEM)
SMEM = pl.BlockSpec(memory_space=pltpu.SMEM)
PARAMS = pltpu.CompilerParams(vmem_limit_bytes=32 * 1024 * 1024)


def _split(device):
    dp, tensor = divmod(device, 8)
    return dp // 4, (dp // 2) % 2, dp % 2, tensor // 2, tensor % 2


def _join(z, yl, c, x, yh):
    return ((z % 4) * 4 + yl * 2 + c) * 8 + (x % 4) * 2 + yh


def _move(value, where):
    pairs = [(d, _join(*where(*_split(d)))) for d in range(128)]
    return lax.ppermute(value, ("dp", "tensor"), pairs)


def z_shift(value, by):
    return _move(value, lambda z, yl, c, x, yh: (z + by, yl, c, x, yh))


def x_shift(value, by):
    return _move(value, lambda z, yl, c, x, yh: (z, yl, c, x + by, yh))


def core_swap(value):
    return _move(value, lambda z, yl, c, x, yh: (z, yl, 1 - c, x, yh))


def y_swap(value):
    return _move(value, lambda z, yl, c, x, yh: (z, 1 - yl, c, x, yh))


def y_cross(value):
    return _move(value, lambda z, yl, c, x, yh: (z, 1 - yl, c, x, 1 - yh))


def after(value, *others):
    return lax.optimization_barrier((value, *others))[0]


def cost(flops, bytes_accessed):
    return pl.CostEstimate(flops=flops, bytes_accessed=bytes_accessed, transcendentals=0)


def _columns(source, block):
    return pl.ds(pl.multiple_of(source[block] * 256, 256), 256)


def _place(block, kept, far, sibling, sibling_far, value):
    (kept, far, sibling, sibling_far)[block // 4][block % 4] = value


def arrange_kernel(source, x, *outs):
    for block in range(16):
        _place(block, *outs, x[:, _columns(source, block)])


def carry_kernel(source, included, x, *outs):
    for block in range(16):
        columns = _columns(source, block)
        total = jnp.zeros((x.shape[1], 256), F32)
        for later in range(4):
            total = total + included[later].astype(F32) * x[later, :, columns].astype(F32)
        _place(block, *outs, total.astype(BF16))


def arrange(kernel, scalars, array):
    rows = 48
    block = (rows, 4096) if array.ndim == 2 else (4, rows, 4096)
    index = (lambda i, *_: (i, 0)) if array.ndim == 2 else (lambda i, *_: (0, i, 0))
    return pl.pallas_call(
        kernel,
        grid_spec=pltpu.PrefetchScalarGridSpec(
            num_scalar_prefetch=len(scalars),
            grid=(192 // rows,),
            in_specs=[pl.BlockSpec(block, index)],
            out_specs=[pl.BlockSpec((4, rows, 256), lambda i, *_: (0, i, 0))] * 4,
        ),
        out_shape=[jax.ShapeDtypeStruct((4, 192, 256), BF16)] * 4,
        compiler_params=PARAMS,
        cost_estimate=cost(0, array.size * 2 + 192 * 4096 * 2),
    )(*scalars, array)


def spread(kept, far, sibling, sibling_far):
    other = y_swap(far)
    from_sibling, from_sibling_far = core_swap(sibling), core_swap(sibling_far)
    return (kept, other, from_sibling, y_cross(from_sibling_far))


def turned(pieces):
    return jnp.concatenate(pieces, axis=1).transpose(0, 2, 1).reshape(1024, 768)


def pre_kernel(t0, t1, t2, t3, w0, w1, w2a, w2b, w3, keep, send, left, right):
    right[0:256] = w0[...]
    right[256:512] = w1[...]
    right[512:640] = w2a[...]
    right[640:768] = w2b[...]
    right[768:1024] = w3[...]
    for out, first, second in ((send, t2, t3), (keep, t0, t1)):
        for k in range(4):
            left[0:192, k * 256 : (k + 1) * 256] = first[k]
            left[192:384, k * 256 : (k + 1) * 256] = second[k]
        out[...] = jnp.dot(left[...], right[...], preferred_element_type=F32)


def partial_pre(pieces, rows):
    return pl.pallas_call(
        pre_kernel,
        in_specs=[VMEM] * 9,
        out_specs=[VMEM] * 2,
        out_shape=[jax.ShapeDtypeStruct((384, 896), F32)] * 2,
        scratch_shapes=[pltpu.VMEM((384, 1024), BF16), pltpu.VMEM((1024, 896), BF16)],
        compiler_params=PARAMS,
        cost_estimate=cost(2 * 768 * 1024 * 896, 6_000_000),
    )(*pieces, *rows)


def gather_rows(block, behind=None):
    if behind is not None:
        block = after(block, behind)
    nxt, prev = z_shift(block, -1), z_shift(block, 1)
    return (block, nxt, z_shift(nxt[:128], -1), z_shift(prev[128:], 1), prev)


def add_over_rows(pieces, rows):
    keep, send = partial_pre(pieces, rows)
    half = keep + core_swap(send)
    other = y_swap(half.astype(BF16)).astype(F32)
    return half + jnp.concatenate([other[192:], other[:192]], axis=0)


def grad_kernel(tokens, mine, theirs, g0, g1, g2a, g2b, g3, right):
    right[0:384] = mine[...]
    right[384:768] = theirs[...]
    for k in range(4):
        block = jnp.dot(
            tokens[k * 256 : (k + 1) * 256, :], right[...], preferred_element_type=F32
        )
        if k == 2:
            g2a[...] = block[:128].astype(BF16)
            g2b[...] = block[128:].astype(BF16)
        else:
            (g0, g1, None, g3)[k][...] = block


def weight_gradient(tokens, units):
    full = jax.ShapeDtypeStruct((256, 896), F32)
    half = jax.ShapeDtypeStruct((128, 896), BF16)
    blocks = pl.pallas_call(
        grad_kernel,
        in_specs=[VMEM] * 3,
        out_specs=[VMEM] * 5,
        out_shape=[full, full, half, half, full],
        scratch_shapes=[pltpu.VMEM((768, 896), BF16)],
        compiler_params=PARAMS,
        cost_estimate=cost(2 * 768 * 1024 * 896, 6_000_000),
    )(tokens, *units)
    return scatter_ring(blocks, z_shift)


def input_kernel(order, *refs):
    gm, gs, um, us = refs[:4]
    gate_rows, up_rows = refs[4:9], refs[9:14]
    j0, j1, j2a, j2b, j3, gate, up = refs[14:]
    for rows, whole in ((gate_rows, gate), (up_rows, up)):
        whole[0] = rows[0][...]
        whole[1] = rows[1][...]
        whole[2, 0:128] = rows[2][...]
        whole[2, 128:256] = rows[3][...]
        whole[3] = rows[4][...]
    over_units = (((1,), (1,)), ((), ()))
    for j in range(4):
        k = order[j]
        for part, (gd, ud) in enumerate(((gm, um), (gs, us))):
            block = lax.dot_general(
                gd[...], gate[k], over_units, preferred_element_type=F32
            ) + lax.dot_general(ud[...], up[k], over_units, preferred_element_type=F32)
            if j == 2:
                (j2a, j2b)[part][...] = block.astype(BF16)
            else:
                (j0, j1, None, j3)[j][part * 384 : (part + 1) * 384, :] = block


def input_partial(order, gate_delta, up_delta, gate_rows, up_rows):
    full = jax.ShapeDtypeStruct((768, 256), F32)
    half = jax.ShapeDtypeStruct((384, 256), BF16)
    return pl.pallas_call(
        input_kernel,
        in_specs=[SMEM] + [VMEM] * 14,
        out_specs=[VMEM] * 5,
        out_shape=[full, full, half, half, full],
        scratch_shapes=[pltpu.VMEM((4, 256, 896), BF16)] * 2,
        compiler_params=PARAMS,
        cost_estimate=cost(4 * 768 * 1024 * 896, 10_000_000),
    )(order, *gate_delta, *up_delta, *gate_rows, *up_rows)


def scatter_ring(blocks, shift):
    b0, b1, b2a, b2b, b3 = blocks
    half = b2a.shape[0]
    low, high = shift(b2a, 1), shift(b2b, -1)
    ahead = jnp.concatenate(
        [(b1[:half] + low.astype(F32)).astype(BF16), b1[half:].astype(BF16)], axis=0
    )
    behind = jnp.concatenate(
        [b3[:half].astype(BF16), (b3[half:] + high.astype(F32)).astype(BF16)], axis=0
    )
    return b0 + shift(ahead, 1).astype(F32) + shift(behind, -1).astype(F32)


def local(activations, cotangents, gate_weight, up_weight, down_weight):
    dp, tensor = lax.axis_index("dp"), lax.axis_index("tensor")
    z, yl, c = dp // 4, (dp // 2) % 2, dp % 2
    x, yh = tensor // 2, tensor % 2
    source = jnp.stack(
        [
            ((z + k) % 4) * 4 + (yl ^ far) * 2 + (c ^ sibling)
            for sibling in range(2)
            for far in range(2)
            for k in range(4)
        ]
    ).astype(jnp.int32)
    first_unit = tensor * gate_weight.shape[1]
    band_index = (
        1
        + (first_unit >= FF // 8).astype(jnp.int32)
        + (first_unit >= FF // 4).astype(jnp.int32)
        + (first_unit >= FF // 2).astype(jnp.int32)
    )
    included = jnp.stack([(k + 1 >= band_index).astype(jnp.int32) for k in range(4)])

    gate_rows = gather_rows(gate_weight)
    up_rows = gather_rows(up_weight)
    down_rows = gather_rows(down_weight, gate_rows[1])

    tokens = spread(*arrange(arrange_kernel, (source,), activations))
    cotangent = spread(*arrange(carry_kernel, (source, included), cotangents))
    tokens_turned, cotangent_turned = turned(tokens), turned(cotangent)

    gate_pre = add_over_rows(tokens, gate_rows)
    up_pre = add_over_rows(tokens, up_rows)
    sigmoid_gate = jax.nn.sigmoid(gate_pre)
    silu_gate = gate_pre * sigmoid_gate
    hidden = (silu_gate * up_pre).astype(BF16)
    hidden, gate_pre, up_pre = lax.optimization_barrier((hidden, gate_pre, up_pre))
    down_grad = weight_gradient(cotangent_turned, (hidden, core_swap(hidden)))

    hidden_grad = add_over_rows(cotangent, down_rows)
    sigmoid_gate = jax.nn.sigmoid(gate_pre)
    silu_gate = gate_pre * sigmoid_gate
    gate_mine = (
        hidden_grad * up_pre * sigmoid_gate * (1.0 + gate_pre * (1.0 - sigmoid_gate))
    ).astype(BF16)
    up_mine = (hidden_grad * silu_gate).astype(BF16)
    gate_delta = (gate_mine, core_swap(gate_mine))
    up_delta = (up_mine, core_swap(up_mine))

    gate_grad = weight_gradient(tokens_turned, gate_delta)
    up_grad = weight_gradient(tokens_turned, up_delta)

    order = jnp.stack([(x + j - z) % 4 for j in range(4)]).astype(jnp.int32)
    along_x = input_partial(order, gate_delta, up_delta, gate_rows, up_rows)
    columns = scatter_ring(along_x, x_shift).reshape(2, 2, 192, 256)
    halves = []
    for j in range(2):
        moved = []
        for i in range(2):
            block = lax.dynamic_index_in_dim(columns[j], (i + yh + yl) % 2, 0, keepdims=False)
            moved.append(
                _move(block, lambda z, yl, c, x, yh, i=i, j=j: (z, yh ^ i, c ^ j, x, yl))
            )
        halves.append(moved[0] + moved[1])
    input_grad = jnp.where(
        c == 0,
        jnp.concatenate([halves[0], halves[1]], axis=1),
        jnp.concatenate([halves[1], halves[0]], axis=1),
    )
    return (input_grad, gate_grad, up_grad, down_grad)


def solution(mesh):
    return jax.shard_map(
        local,
        mesh=mesh,
        in_specs=(
            P("dp", None),
            P(None, "dp", None),
            P("dp", "tensor"),
            P("dp", "tensor"),
            P("dp", "tensor"),
        ),
        out_specs=(P("dp", "tensor"), P("dp", "tensor"), P("dp", "tensor"), P("dp", "tensor")),
        check_vma=False,
    )
```

time: 404 us -> 193 us (0.48)
  waiting for transfers between devices: 327 us -> 62.9 us
  starting transfers between devices: 10.6 us -> 73.7 us
  matrix products: 42 us -> 0 us
  Pallas kernels: 0 us -> 23.7 us
  between operations: 14.2 us -> 1.64 us
  other arithmetic: 4.01 us -> 15.8 us
  local copies, waits for them, and re-layouts: 6 us -> 12.8 us
    all_gather x6 -> x0, waiting for transfers between devices: 215 us -> none  [the longest x1 47.1 us: local(): lax.all_gather(down_weight, 'dp', axis=0, tiled=True)]
    reduce_scatter x1 -> x0, waiting for transfers between devices: 76.5 us -> none  [local(): lax.psum_scatter(partial_input, 'tensor', scatter_dimension=1, tiled=True)]
    ppermute x0 -> x49, starting transfers between devices: none -> 73.7 us  [_move(): return lax.ppermute(value, ('dp', 'tensor'), pairs)]
    ppermute x0 -> x49, waiting for transfers between devices: none -> 62.9 us  [_move(): return lax.ppermute(value, ('dp', 'tensor'), pairs)]
    dot_general x8 -> x0, matrix products: 42 us -> none  [the longest x1 6.27 us: local(): up_pre = jnp.dot(activations, full_up, preferred_element_type=jnp.float32)]
    all_to_all x2 -> x0, waiting for transfers between devices: 31.7 us -> none  [the longest x1 31.7 us: local(): lax.all_to_all(activations, 'dp', split_axis=1, concat_axis=0, tiled=True)]
    pallas_call x0 -> x9, Pallas kernels: none -> 23.7 us  [the longest x3 7.48 us: partial_pre(): pl.pallas_call(pre_kernel, in_specs=[VMEM] * 9, out_specs=[VMEM] * 2, out...]
    all_to_all x2 -> x0, starting transfers between devices: 10.3 us -> none  [the longest x1 5.25 us: local(): lax.all_to_all(activations, 'dp', split_axis=1, concat_axis=0, tiled=True)]
  transfers between devices with their start and end apart: 9 -> 49, of which waited for: 8 -> 14; matrix products, arithmetic and copies ran while one was open for 11% -> 12% of each run, Pallas kernels for 0% -> 10%
where the time goes in v1:
time: 193 us; the launch traced here: 190 us
  starting transfers between devices  73.7 us (38%)
  waiting for transfers between devices  62.9 us (33%)
  Pallas kernels  23.7 us (12%)
  other arithmetic  15.8 us (8%)
  local copies, waits for them, and re-layouts  12.8 us (7%)
    ppermute x49, starting transfers between devices, _move(): return lax.ppermute(value, ('dp', 'tensor'), pairs)  73.7 us
    ppermute x49, waiting for transfers between devices, _move(): return lax.ppermute(value, ('dp', 'tensor'), pairs)  62.9 us
    pallas_call x3, Pallas kernels, partial_pre(): pl.pallas_call(pre_kernel, in_specs=[VMEM] * 9, out_specs=[VMEM] * 2, out...  7.48 us
    pallas_call x3, Pallas kernels, weight_gradient(): pl.pallas_call(grad_kernel, in_specs=[VMEM] * 3, out_specs=[VMEM] * 5, ou...  6.92 us
    convert_element_type x3, other arithmetic, add_over_rows(): other = y_swap(half.astype(BF16)).astype(F32)  5.73 us
    pallas_call x1, Pallas kernels, input_partial(): pl.pallas_call(input_kernel, in_specs=[SMEM] + [VMEM] * 14, out_specs=[VM...  4.79 us
    pallas_call x2, Pallas kernels, arrange(): pl.pallas_call(kernel, grid_spec=pltpu.PrefetchScalarGridSpec(num_scalar_...  4.48 us
    unnamed x62, local copies, waits for them, and re-layouts  4.31 us
  transfers between devices with their start and end apart: 49, of which 14 were waited for; matrix products, arithmetic and copies ran while one was open for 12% of the time, Pallas kernels for 10%

profile of v1, /device:TPU:1, one launch (start us, length us, event | category | flops | bytes accessed | tf_op | source)
XLA Modules:
  0.0 190.5 jit_solution(5967655854821160147)
XLA Ops:
  0.9 1.4 copy-done.1
  2.3 2.1 %shard_map.86 = (bf16[4,192,256]{2,1,0:T(8,128)(2,1)S(1)}, bf16[4,192,256]{2,1,0:T(8,128)(2,1)}, bf16[4,192,256]{2,1,0:T(8,128)(2,1)}, bf16[4,192,256]{2,1,0:T(8,128)(2,1)S(1)}) custom-call(s32[16]{0:T(128)S(1)} %stack.108.source, bf16[192,4096]{1,0:T(8,128)(2,1)S(1)} %copy-done.1), custom_call_target="tpu_custom_call" | custom-call | bytes 3145728 | tf_op jit(solution)/shard_map/pallas_call | solution.py:86
  4.4 1.4 collective-permute-start.13
  5.8 3.8 %collective-permute-start.4 = (bf16[256,896]{1,0:T(8,128)(2,1)S(1)}, bf16[256,896]{1,0:T(8,128)(2,1)S(1)}, u32[]{:S(2)}, u32[]{:S(2)}) collective-permute-start(bf16[256,896]{1,0:T(8,128)(2,1)S(1)} %copy-done.15), channel_id=1, source_target_pairs={{0,96},{1,97},{2,98},{3,99},{4,100},{5,101},{6,102},{7,103},{8,104... | collective-permute-start | bytes 1376264 | tf_op jit(solution)/shard_map/ppermute | solution.py:29
  9.7 1.3 collective-permute-start.11
  11.6 3.0 %collective-permute-start.20 = (bf16[256,896]{1,0:T(8,128)(2,1)}, bf16[256,896]{1,0:T(8,128)(2,1)S(1)}, u32[]{:S(2)}, u32[]{:S(2)}) collective-permute-start(bf16[256,896]{1,0:T(8,128)(2,1)} %refs_9_.1), channel_id=1, source_target_pairs={{0,96},{1,97},{2,98},{3,99},{4,100},{5,101},{6,102},{7,103},{8,104... | collective-permute-start | bytes 1376264 | tf_op jit(solution)/shard_map/ppermute | solution.py:29
  14.5 5.0 %collective-permute-done.4.w1.refs_5_ = bf16[256,896]{1,0:T(8,128)(2,1)S(1)} collective-permute-done((bf16[256,896]{1,0:T(8,128)(2,1)S(1)}, bf16[256,896]{1,0:T(8,128)(2,1)S(1)}, u32[]{:S(2)}, u32[]{:S(2)}) %collective-permute-start.4) | collective-permute-done | bytes 458784 | tf_op jit(solution)/shard_map/ppermute | solution.py:29
  19.9 2.7 %collective-permute-done.16.w3.refs_8_ = bf16[256,896]{1,0:T(8,128)(2,1)S(1)} collective-permute-done((bf16[256,896]{1,0:T(8,128)(2,1)S(1)}, bf16[256,896]{1,0:T(8,128)(2,1)S(1)}, u32[]{:S(2)}, u32[]{:S(2)}) %collective-permute-start.16) | collective-permute-done | bytes 458784 | tf_op jit(solution)/shard_map/ppermute | solution.py:29
  22.6 2.7 %collective-permute-start.14 = (bf16[4,192,256]{2,1,0:T(8,128)(2,1)}, bf16[4,192,256]{2,1,0:T(8,128)(2,1)S(1)}, u32[]{:S(2)}, u32[]{:S(2)}) collective-permute-start(bf16[4,192,256]{2,1,0:T(8,128)(2,1)} %collective-permute-done.13), channel_id=1, source_target_pairs={{0,17},{1,16},{2,19},{3,18},{4,21},{5,20},{6,23},{7,22},{8,25},{9,... | collective-permute-start | bytes 1179656 | tf_op jit(solution)/shard_map/ppermute | solution.py:29
  25.9 1.1 collective-permute-start.17
  27.1 2.8 %copy-done = bf16[4,192,4096]{2,1,0:T(8,128)(2,1)S(1)} copy-done((bf16[4,192,4096]{2,1,0:T(8,128)(2,1)S(1)}, bf16[4,192,4096]{2,1,0:T(8,128)(2,1)}, u32[]{:S(2)}) %copy-start) | copy-done | bytes 6291480
  29.8 2.4 %shard_map.84 = (bf16[4,192,256]{2,1,0:T(8,128)(2,1)S(1)}, bf16[4,192,256]{2,1,0:T(8,128)(2,1)S(1)}, bf16[4,192,256]{2,1,0:T(8,128)(2,1)S(1)}, bf16[4,192,256]{2,1,0:T(8,128)(2,1)S(1)}) custom-call(s32[16]{0:T(128)S(1)} %stack.108.source, s32[4]{0:T(128)S(1)} %add_convert_fusion.8.included, bf16[4,192,4096]{2,1,0:T(8,128)(2,1)S(1)} %copy-done), custom_call_target="tpu_custom_call" | custom-call | bytes 7864320 | tf_op jit(solution)/shard_map/pallas_call | solution.py:86
  32.2 2.1 %collective-permute-start.2 = (bf16[4,192,256]{2,1,0:T(8,128)(2,1)S(1)}, bf16[4,192,256]{2,1,0:T(8,128)(2,1)S(1)}, u32[]{:S(2)}, u32[]{:S(2)}) collective-permute-start(bf16[4,192,256]{2,1,0:T(8,128)(2,1)S(1)} %get-tuple-element.45), channel_id=1, source_target_pairs={{0,8},{1,9},{2,10},{3,11},{4,12},{5,13},{6,14},{7,15},{8,0},{9,1},... | collective-permute-start | bytes 1179656 | tf_op jit(solution)/shard_map/ppermute | solution.py:29
  34.3 1.8 collective-permute-start.5
  36.1 1.6 collective-permute-start.21
  38.9 1.8 shard_map.87
  40.7 2.8 %collective-permute-start.18 = (f32[384,896]{1,0:T(8,128)S(1)}, f32[384,896]{1,0:T(8,128)S(1)}, u32[]{:S(2)}, u32[]{:S(2)}) collective-permute-start(f32[384,896]{1,0:T(8,128)S(1)} %get-tuple-element.54), channel_id=1, source_target_pairs={{0,8},{1,9},{2,10},{3,11},{4,12},{5,13},{6,14},{7,15},{8,0},{9,1},... | collective-permute-start | bytes 4128776 | tf_op jit(solution)/shard_map/ppermute | solution.py:29
  43.5 5.7 %collective-permute-done.21.w2a.refs_11_ = bf16[128,896]{1,0:T(8,128)(2,1)S(1)} collective-permute-done((bf16[128,896]{1,0:T(8,128)(2,1)S(1)}, bf16[128,896]{1,0:T(8,128)(2,1)S(1)}, u32[]{:S(2)}, u32[]{:S(2)}) %collective-permute-start.21) | collective-permute-done | bytes 229408 | tf_op jit(solution)/shard_map/ppermute | solution.py:29
  49.3 3.0 %collective-permute-start.1 = (bf16[4,192,256]{2,1,0:T(8,128)(2,1)S(1)}, bf16[4,192,256]{2,1,0:T(8,128)(2,1)S(1)}, u32[]{:S(2)}, u32[]{:S(2)}) collective-permute-start(bf16[4,192,256]{2,1,0:T(8,128)(2,1)S(1)} %get-tuple-element.44), channel_id=1, source_target_pairs={{0,8},{1,9},{2,10},{3,11},{4,12},{5,13},{6,14},{7,15},{8,0},{9,1},... | collective-permute-start | bytes 1179656 | tf_op jit(solution)/shard_map/ppermute | solution.py:29
  52.3 1.9 collective-permute-start.3
  54.2 3.0 %shard_map.88 = (f32[384,896]{1,0:T(8,128)S(1)}, f32[384,896]{1,0:T(8,128)S(1)}) custom-call(bf16[4,192,256]{2,1,0:T(8,128)(2,1)S(1)} %get-tuple-element.49.t0, bf16[4,192,256]{2,1,0:T(8,128)(2,1)S(1)} %collective-permute-done.11.t1, bf16[4,192,256]{2,1,0:T(8,128)(2,1)S(1)} %collective-permute-done.12.t2, ...), custom_call_target="tpu_custom_call" | custom-call | flops 1409286144 | bytes 6000000 | tf_op jit(solution)/shard_map/pallas_call | solution.py:124
  57.9 2.5 %collective-permute-start.6 = (bf16[128,896]{1,0:T(8,128)(2,1)S(1)}, bf16[128,896]{1,0:T(8,128)(2,1)S(1)}, u32[]{:S(2)}, u32[]{:S(2)}) collective-permute-start(bf16[128,896]{1,0:T(8,128)(2,1)S(1)} %slice.132), channel_id=1, source_target_pairs={{0,96},{1,97},{2,98},{3,99},{4,100},{5,101},{6,102},{7,103},{8,104... | collective-permute-start | bytes 688136 | tf_op jit(solution)/shard_map/ppermute | solution.py:29
  60.4 3.8 %collective-permute-done.3.t3 = bf16[4,192,256]{2,1,0:T(8,128)(2,1)S(1)} collective-permute-done((bf16[4,192,256]{2,1,0:T(8,128)(2,1)S(1)}, bf16[4,192,256]{2,1,0:T(8,128)(2,1)S(1)}, u32[]{:S(2)}, u32[]{:S(2)}) %collective-permute-start.3) | collective-permute-done | bytes 393248 | tf_op jit(solution)/shard_map/ppermute | solution.py:29
  64.2 2.3 %collective-permute-done.8.w2b = bf16[128,896]{1,0:T(8,128)(2,1)S(1)} collective-permute-done((bf16[128,896]{1,0:T(8,128)(2,1)S(1)}, bf16[128,896]{1,0:T(8,128)(2,1)S(1)}, u32[]{:S(2)}, u32[]{:S(2)}) %collective-permute-start.8) | collective-permute-done | bytes 229408 | tf_op jit(solution)/shard_map/ppermute | solution.py:29
  66.5 2.7 %shard_map.85 = (f32[384,896]{1,0:T(8,128)S(1)}, f32[384,896]{1,0:T(8,128)}) custom-call(bf16[4,192,256]{2,1,0:T(8,128)(2,1)S(1)} %get-tuple-element.42.t0, bf16[4,192,256]{2,1,0:T(8,128)(2,1)S(1)} %collective-permute-done.t1, bf16[4,192,256]{2,1,0:T(8,128)(2,1)S(1)} %collective-permute-done.1.t2, bf16[4,192,256]{2,1,0:T(8,128)(2,1)S(1)} %collective-permute-done.3.t3, ...), custom_call_target="tpu_custom_call" | custom-call | flops 1409286144 | bytes 6000000 | tf_op jit(solution)/shard_map/pallas_call | solution.py:124
  69.2 5.1 %collective-permute-start.9 = (f32[384,896]{1,0:T(8,128)}, f32[384,896]{1,0:T(8,128)}, u32[]{:S(2)}, u32[]{:S(2)}) collective-permute-start(f32[384,896]{1,0:T(8,128)} %get-tuple-element.48), channel_id=1, source_target_pairs={{0,8},{1,9},{2,10},{3,11},{4,12},{5,13},{6,14},{7,15},{8,0},{9,1},... | collective-permute-start | bytes 4128776 | tf_op jit(solution)/shard_map/ppermute | solution.py:29
  74.3 1.5 fusion.1
  75.7 1.5 fusion.2
  77.2 1.5 collective-permute-start.25
  78.7 2.8 %fusion = (bf16[384,896]{1,0:T(8,128)(2,1)}, f32[384,896]{1,0:T(8,128)}) fusion(f32[384,896]{1,0:T(8,128)S(1)} %get-tuple-element.47, f32[384,896]{1,0:T(8,128)} %collective-permute-done.9), kind=kLoop, calls=%fused_computation.44 | loop fusion | flops 688128 | bytes 4816896 | tf_op jit(solution)/shard_map/convert_element_type | solution.py:145
  81.5 11.6 %collective-permute-done.19 = bf16[384,896]{1,0:T(8,128)(2,1)} collective-permute-done((bf16[384,896]{1,0:T(8,128)(2,1)}, bf16[384,896]{1,0:T(8,128)(2,1)}, u32[]{:S(2)}, u32[]{:S(2)}) %collective-permute-start.19) | collective-permute-done | bytes 688160 | tf_op jit(solution)/shard_map/ppermute | solution.py:29
  93.1 1.2 fusion.6
  94.3 13.6 %collective-permute-done.25 = bf16[384,896]{1,0:T(8,128)(2,1)} collective-permute-done((bf16[384,896]{1,0:T(8,128)(2,1)}, bf16[384,896]{1,0:T(8,128)(2,1)}, u32[]{:S(2)}, u32[]{:S(2)}) %collective-permute-start.25) | collective-permute-done | bytes 688160 | tf_op jit(solution)/shard_map/ppermute | solution.py:29
  107.8 1.2 fusion.5
  109.0 1.9 %multiply_convert_fusion.2 = (bf16[384,896]{1,0:T(8,128)(2,1)}, f32[384,896]{1,0:T(8,128)}, f32[384,896]{1,0:T(8,128)}) fusion(f32[384,896]{1,0:T(8,128)S(1)} %copy-done.28, f32[192,896]{1,0:T(8,128)S(1)} %get-tuple-element.98, f32[192,896]{1,0:T(8,128)S(1)} %get-tuple-element.97, f32[384,896]{1,0:T(8,128)S(1)} %copy-done.29, ...), kind=kLoop, calls=%fused_computation.8 | loop fusion | flops 3440640 | bytes 8945664 | tf_op jit(solution)/shard_map/convert_element_type | solution.py:261
  111.0 1.2 collective-permute-start.44
  112.2 1.3 maximum_bitcast_fusion
  113.5 1.8 copy.9
  115.4 1.3 maximum_bitcast_fusion.1
  116.6 1.7 copy.10
  118.3 4.2 %collective-permute-done.10 = bf16[384,896]{1,0:T(8,128)(2,1)} collective-permute-done((bf16[384,896]{1,0:T(8,128)(2,1)}, bf16[384,896]{1,0:T(8,128)(2,1)}, u32[]{:S(2)}, u32[]{:S(2)}) %collective-permute-start.10) | collective-permute-done | bytes 688160 | tf_op jit(solution)/shard_map/ppermute | solution.py:29
  122.6 1.2 fusion.4
  123.8 3.3 %shard_map.92 = (f32[256,896]{1,0:T(8,128)S(1)}, f32[256,896]{1,0:T(8,128)S(1)}, bf16[128,896]{1,0:T(8,128)(2,1)S(1)}, bf16[128,896]{1,0:T(8,128)(2,1)S(1)}, f32[256,896]{1,0:T(8,128)S(1)}) custom-call(bf16[1024,768]{1,0:T(8,128)(2,1)S(1)} %bitcast.42, bf16[384,896]{1,0:T(8,128)(2,1)} %get-tuple-element.74.mine, bf16[384,896]{1,0:T(8,128)(2,1)} %collective-permute-done.44.theirs), custom_call_target="tpu_custom_call" | custom-call | flops 1409286144 | bytes 6000000 | tf_op jit(solution)/shard_map/pallas_call | solution.py:166
  129.0 1.8 collective-permute-start.45
  130.8 2.7 %collective-permute-done.47 = bf16[128,896]{1,0:T(8,128)(2,1)S(1)} collective-permute-done((bf16[128,896]{1,0:T(8,128)(2,1)S(1)}, bf16[128,896]{1,0:T(8,128)(2,1)S(1)}, u32[]{:S(2)}, u32[]{:S(2)}) %collective-permute-start.47) | collective-permute-done | bytes 229408 | tf_op jit(solution)/shard_map/ppermute | solution.py:29
  133.7 1.6 collective-permute-start.48
  135.3 1.8 collective-permute-done.45
  137.8 4.8 %shard_map.89 = (f32[768,256]{1,0:T(8,128)S(1)}, f32[768,256]{1,0:T(8,128)S(1)}, bf16[384,256]{1,0:T(8,128)(2,1)S(1)}, bf16[384,256]{1,0:T(8,128)(2,1)S(1)}, f32[768,256]{1,0:T(8,128)S(1)}) custom-call(s32[4]{0:T(128)S(1)} %pad_add_fusion.order, bf16[384,896]{1,0:T(8,128)(2,1)S(1)} %get-tuple-element.90.refs_0_.mine, ...), custom_call_target="tpu_custom_call" | custom-call | flops 2818572288 | bytes 10000000 | tf_op jit(solution)/shard_map/pallas_call | solution.py:204
  142.6 2.5 %collective-permute-start.30 = (bf16[384,256]{1,0:T(8,128)(2,1)S(1)}, bf16[384,256]{1,0:T(8,128)(2,1)S(1)}, u32[]{:S(2)}, u32[]{:S(2)}) collective-permute-start(bf16[384,256]{1,0:T(8,128)(2,1)S(1)} %get-tuple-element.63), channel_id=1, source_target_pairs={{0,6},{1,7},{2,0},{3,1},{4,2},{5,3},{6,4},{7,5},{8,14},{9,15},{10,... | collective-permute-start | bytes 589832 | tf_op jit(solution)/shard_map/ppermute | solution.py:29
  145.5 1.8 shard_map.90
  147.3 2.3 %collective-permute-start.38 = (bf16[128,896]{1,0:T(8,128)(2,1)S(1)}, bf16[128,896]{1,0:T(8,128)(2,1)S(1)}, u32[]{:S(2)}, u32[]{:S(2)}) collective-permute-start(bf16[128,896]{1,0:T(8,128)(2,1)S(1)} %get-tuple-element.68), channel_id=1, source_target_pairs={{0,96},{1,97},{2,98},{3,99},{4,100},{5,101},{6,102},{7,103},{8,104... | collective-permute-start | bytes 688136 | tf_op jit(solution)/shard_map/ppermute | solution.py:29
  149.6 1.8 shard_map.91
  151.7 2.7 %collective-permute-start.42 = (bf16[128,896]{1,0:T(8,128)(2,1)S(1)}, bf16[128,896]{1,0:T(8,128)(2,1)S(1)}, u32[]{:S(2)}, u32[]{:S(2)}) collective-permute-start(bf16[128,896]{1,0:T(8,128)(2,1)S(1)} %get-tuple-element.73), channel_id=1, source_target_pairs={{0,96},{1,97},{2,98},{3,99},{4,100},{5,101},{6,102},{7,103},{8,104... | collective-permute-start | bytes 688136 | tf_op jit(solution)/shard_map/ppermute | solution.py:29
  154.7 3.0 %collective-permute-done.36 = bf16[128,896]{1,0:T(8,128)(2,1)S(1)} collective-permute-done((bf16[128,896]{1,0:T(8,128)(2,1)S(1)}, bf16[128,896]{1,0:T(8,128)(2,1)S(1)}, u32[]{:S(2)}, u32[]{:S(2)}) %collective-permute-start.36) | collective-permute-done | bytes 229408 | tf_op jit(solution)/shard_map/ppermute | solution.py:29
  157.7 2.7 %collective-permute-start.31 = (bf16[768,256]{1,0:T(8,128)(2,1)S(1)}, bf16[768,256]{1,0:T(8,128)(2,1)S(1)}, u32[]{:S(2)}, u32[]{:S(2)}) collective-permute-start(bf16[768,256]{1,0:T(8,128)(2,1)S(1)} %pad_maximum_fusion.7), channel_id=1, source_target_pairs={{0,6},{1,7},{2,0},{3,1},{4,2},{5,3},{6,4},{7,5},{8,14},{9,15},{10,... | collective-permute-start | bytes 1179656 | tf_op jit(solution)/shard_map/ppermute | solution.py:29
  160.6 2.7 %collective-permute-done.40 = bf16[128,896]{1,0:T(8,128)(2,1)S(1)} collective-permute-done((bf16[128,896]{1,0:T(8,128)(2,1)S(1)}, bf16[128,896]{1,0:T(8,128)(2,1)S(1)}, u32[]{:S(2)}, u32[]{:S(2)}) %collective-permute-start.40) | collective-permute-done | bytes 229408 | tf_op jit(solution)/shard_map/ppermute | solution.py:29
  163.5 1.5 collective-permute-start.37
  165.0 1.2 collective-permute-start.43
  168.5 7.3 %collective-permute-start.34 = (f32[192,256]{1,0:T(8,128)S(1)}, f32[192,256]{1,0:T(8,128)S(1)}, u32[]{:S(2)}, u32[]{:S(2)}) collective-permute-start(f32[192,256]{1,0:T(8,128)S(1)} %get-tuple-element.102), channel_id=1, source_target_pairs={{0,8},{1,24},{2,10},{3,26},{4,12},{5,28},{6,14},{7,30},{8,0},{9,16... | collective-permute-start | bytes 589832 | tf_op jit(solution)/shard_map/ppermute | solution.py:29
  175.9 4.3 %collective-permute-start.35 = (f32[192,256]{1,0:T(8,128)S(1)}, f32[192,256]{1,0:T(8,128)S(1)}, u32[]{:S(2)}, u32[]{:S(2)}) collective-permute-start(f32[192,256]{1,0:T(8,128)S(1)} %get-tuple-element.101), channel_id=1, source_target_pairs={{0,24},{1,8},{2,26},{3,10},{4,28},{5,12},{6,30},{7,14},{8,16},{9,0... | collective-permute-start | bytes 589832 | tf_op jit(solution)/shard_map/ppermute | solution.py:29
  180.8 1.0 convert_add_fusion.2
  181.9 3.9 %collective-permute-start.33 = (f32[192,256]{1,0:T(8,128)S(1)}, f32[192,256]{1,0:T(8,128)S(1)}, u32[]{:S(2)}, u32[]{:S(2)}) collective-permute-start(f32[192,256]{1,0:T(8,128)S(1)} %get-tuple-element.99), channel_id=1, source_target_pairs={{0,16},{1,0},{2,18},{3,2},{4,20},{5,4},{6,22},{7,6},{8,24},{9,8},{... | collective-permute-start | bytes 589832 | tf_op jit(solution)/shard_map/ppermute | solution.py:29
  185.7 1.0 convert_add_fusion.1
  186.8 2.8 %collective-permute-done.33 = f32[192,256]{1,0:T(8,128)S(1)} collective-permute-done((f32[192,256]{1,0:T(8,128)S(1)}, f32[192,256]{1,0:T(8,128)S(1)}, u32[]{:S(2)}, u32[]{:S(2)}) %collective-permute-start.33) | collective-permute-done | bytes 196640 | tf_op jit(solution)/shard_map/ppermute | solution.py:29
  (160 shorter events, 11.3 us)
Async XLA Ops:
  4.4 7.2 %collective-permute-start.13 = (bf16[4,192,256]{2,1,0:T(8,128)(2,1)S(1)}, bf16[4,192,256]{2,1,0:T(8,128)(2,1)}, u32[]{:S(2)}, u32[]{:S(2)}) collective-permute-start(bf16[4,192,256]{2,1,0:T(8,128)(2,1)S(1)} %get-tuple-element.52), channel_id=1, source_target_pairs={{0,8},{1,9},{2,10},{3,11},{4,12},{5,13},{6,14},{7,15},{8,0},{9,1},... | collective-permute-start | bytes 1179656 | tf_op jit(solution)/shard_map/ppermute | solution.py:29
  5.8 13.7 %collective-permute-start.4 = (bf16[256,896]{1,0:T(8,128)(2,1)S(1)}, bf16[256,896]{1,0:T(8,128)(2,1)S(1)}, u32[]{:S(2)}, u32[]{:S(2)}) collective-permute-start(bf16[256,896]{1,0:T(8,128)(2,1)S(1)} %copy-done.15), channel_id=1, source_target_pairs={{0,96},{1,97},{2,98},{3,99},{4,100},{5,101},{6,102},{7,103},{8,104... | collective-permute-start | bytes 1376264 | tf_op jit(solution)/shard_map/ppermute | solution.py:29
  9.7 13.0 %collective-permute-start.16 = (bf16[256,896]{1,0:T(8,128)(2,1)S(1)}, bf16[256,896]{1,0:T(8,128)(2,1)S(1)}, u32[]{:S(2)}, u32[]{:S(2)}) collective-permute-start(bf16[256,896]{1,0:T(8,128)(2,1)S(1)} %copy-done.15), channel_id=1, source_target_pairs={{0,32},{1,33},{2,34},{3,35},{4,36},{5,37},{6,38},{7,39},{8,40},{9,... | collective-permute-start | bytes 1376264 | tf_op jit(solution)/shard_map/ppermute | solution.py:29
  9.7 15.8 %collective-permute-start.11 = (bf16[4,192,256]{2,1,0:T(8,128)(2,1)}, bf16[4,192,256]{2,1,0:T(8,128)(2,1)S(1)}, u32[]{:S(2)}, u32[]{:S(2)}) collective-permute-start(bf16[4,192,256]{2,1,0:T(8,128)(2,1)} %get-tuple-element.50), channel_id=1, source_target_pairs={{0,16},{1,17},{2,18},{3,19},{4,20},{5,21},{6,22},{7,23},{8,24},{9,... | collective-permute-start | bytes 1179656 | tf_op jit(solution)/shard_map/ppermute | solution.py:29
  11.0 15.0 %collective-permute-start.12 = (bf16[4,192,256]{2,1,0:T(8,128)(2,1)}, bf16[4,192,256]{2,1,0:T(8,128)(2,1)S(1)}, u32[]{:S(2)}, u32[]{:S(2)}) collective-permute-start(bf16[4,192,256]{2,1,0:T(8,128)(2,1)} %get-tuple-element.51), channel_id=1, source_target_pairs={{0,8},{1,9},{2,10},{3,11},{4,12},{5,13},{6,14},{7,15},{8,0},{9,1},... | collective-permute-start | bytes 1179656 | tf_op jit(solution)/shard_map/ppermute | solution.py:29
  11.6 20.6 %collective-permute-start.20 = (bf16[256,896]{1,0:T(8,128)(2,1)}, bf16[256,896]{1,0:T(8,128)(2,1)S(1)}, u32[]{:S(2)}, u32[]{:S(2)}) collective-permute-start(bf16[256,896]{1,0:T(8,128)(2,1)} %refs_9_.1), channel_id=1, source_target_pairs={{0,96},{1,97},{2,98},{3,99},{4,100},{5,101},{6,102},{7,103},{8,104... | collective-permute-start | bytes 1376264 | tf_op jit(solution)/shard_map/ppermute | solution.py:29
  19.5 19.3 %copy-start.8 = (bf16[256,896]{1,0:T(8,128)(2,1)}, bf16[256,896]{1,0:T(8,128)(2,1)S(1)}, u32[]{:S(2)}) copy-start(bf16[256,896]{1,0:T(8,128)(2,1)S(1)} %collective-permute-done.4.w1.refs_5_) | copy-start | bytes 1376260
  19.6 14.8 %collective-permute-start.22 = (bf16[256,896]{1,0:T(8,128)(2,1)}, bf16[256,896]{1,0:T(8,128)(2,1)}, u32[]{:S(2)}, u32[]{:S(2)}) collective-permute-start(bf16[256,896]{1,0:T(8,128)(2,1)} %refs_9_.1), channel_id=1, source_target_pairs={{0,32},{1,33},{2,34},{3,35},{4,36},{5,37},{6,38},{7,39},{8,40},{9,... | collective-permute-start | bytes 1376264 | tf_op jit(solution)/shard_map/ppermute | solution.py:29
  22.6 16.2 %copy-start.10 = (bf16[256,896]{1,0:T(8,128)(2,1)}, bf16[256,896]{1,0:T(8,128)(2,1)S(1)}, u32[]{:S(2)}) copy-start(bf16[256,896]{1,0:T(8,128)(2,1)S(1)} %collective-permute-done.16.w3.refs_8_) | copy-start | bytes 1376260
  22.6 16.1 %collective-permute-start.14 = (bf16[4,192,256]{2,1,0:T(8,128)(2,1)}, bf16[4,192,256]{2,1,0:T(8,128)(2,1)S(1)}, u32[]{:S(2)}, u32[]{:S(2)}) collective-permute-start(bf16[4,192,256]{2,1,0:T(8,128)(2,1)} %collective-permute-done.13), channel_id=1, source_target_pairs={{0,17},{1,16},{2,19},{3,18},{4,21},{5,20},{6,23},{7,22},{8,25},{9,... | collective-permute-start | bytes 1179656 | tf_op jit(solution)/shard_map/ppermute | solution.py:29
  25.4 10.7 %collective-permute-start.15 = (bf16[128,896]{1,0:T(8,128)(2,1)S(1)}, bf16[128,896]{1,0:T(8,128)(2,1)S(1)}, u32[]{:S(2)}, u32[]{:S(2)}) collective-permute-start(bf16[128,896]{1,0:T(8,128)(2,1)S(1)} %slice.136), channel_id=1, source_target_pairs={{0,96},{1,97},{2,98},{3,99},{4,100},{5,101},{6,102},{7,103},{8,104... | collective-permute-start | bytes 688136 | tf_op jit(solution)/shard_map/ppermute | solution.py:29
  25.9 12.7 %collective-permute-start.17 = (bf16[128,896]{1,0:T(8,128)(2,1)S(1)}, bf16[128,896]{1,0:T(8,128)(2,1)S(1)}, u32[]{:S(2)}, u32[]{:S(2)}) collective-permute-start(bf16[128,896]{1,0:T(8,128)(2,1)S(1)} %slice.137), channel_id=1, source_target_pairs={{0,32},{1,33},{2,34},{3,35},{4,36},{5,37},{6,38},{7,39},{8,40},{9,... | collective-permute-start | bytes 688136 | tf_op jit(solution)/shard_map/ppermute | solution.py:29
  29.8 4.5 %copy-start.14 = (bf16[256,896]{1,0:T(8,128)(2,1)S(1)}, bf16[256,896]{1,0:T(8,128)(2,1)}, u32[]{:S(2)}) copy-start(bf16[256,896]{1,0:T(8,128)(2,1)} %w0.2) | copy-start | bytes 1376260
  29.8 9.0 %copy-start.16 = (bf16[256,896]{1,0:T(8,128)(2,1)S(1)}, bf16[256,896]{1,0:T(8,128)(2,1)}, u32[]{:S(2)}) copy-start(bf16[256,896]{1,0:T(8,128)(2,1)} %refs_4_.1) | copy-start | bytes 1376260
  32.2 22.0 %copy-start.12 = (bf16[256,896]{1,0:T(8,128)(2,1)}, bf16[256,896]{1,0:T(8,128)(2,1)S(1)}, u32[]{:S(2)}) copy-start(bf16[256,896]{1,0:T(8,128)(2,1)S(1)} %collective-permute-done.20.w1.refs_10_) | copy-start | bytes 1376260
  32.2 8.5 %collective-permute-start.2 = (bf16[4,192,256]{2,1,0:T(8,128)(2,1)S(1)}, bf16[4,192,256]{2,1,0:T(8,128)(2,1)S(1)}, u32[]{:S(2)}, u32[]{:S(2)}) collective-permute-start(bf16[4,192,256]{2,1,0:T(8,128)(2,1)S(1)} %get-tuple-element.45), channel_id=1, source_target_pairs={{0,8},{1,9},{2,10},{3,11},{4,12},{5,13},{6,14},{7,15},{8,0},{9,1},... | collective-permute-start | bytes 1179656 | tf_op jit(solution)/shard_map/ppermute | solution.py:29
  34.3 18.0 %collective-permute-start.5 = (bf16[256,896]{1,0:T(8,128)(2,1)S(1)}, bf16[256,896]{1,0:T(8,128)(2,1)S(1)}, u32[]{:S(2)}, u32[]{:S(2)}) collective-permute-start(bf16[256,896]{1,0:T(8,128)(2,1)S(1)} %copy-done.14), channel_id=1, source_target_pairs={{0,96},{1,97},{2,98},{3,99},{4,100},{5,101},{6,102},{7,103},{8,104... | collective-permute-start | bytes 1376264 | tf_op jit(solution)/shard_map/ppermute | solution.py:29
  36.1 4.6 %copy-start.18 = (bf16[128,896]{1,0:T(8,128)(2,1)}, bf16[128,896]{1,0:T(8,128)(2,1)S(1)}, u32[]{:S(2)}) copy-start(bf16[128,896]{1,0:T(8,128)(2,1)S(1)} %collective-permute-done.15.w2a.refs_6_) | copy-start | bytes 688132
  36.1 13.2 %collective-permute-start.21 = (bf16[128,896]{1,0:T(8,128)(2,1)S(1)}, bf16[128,896]{1,0:T(8,128)(2,1)S(1)}, u32[]{:S(2)}, u32[]{:S(2)}) collective-permute-start(bf16[128,896]{1,0:T(8,128)(2,1)S(1)} %slice.140), channel_id=1, source_target_pairs={{0,96},{1,97},{2,98},{3,99},{4,100},{5,101},{6,102},{7,103},{8,104... | collective-permute-start | bytes 688136 | tf_op jit(solution)/shard_map/ppermute | solution.py:29
  38.7 10.6 %collective-permute-start.23 = (bf16[128,896]{1,0:T(8,128)(2,1)S(1)}, bf16[128,896]{1,0:T(8,128)(2,1)S(1)}, u32[]{:S(2)}, u32[]{:S(2)}) collective-permute-start(bf16[128,896]{1,0:T(8,128)(2,1)S(1)} %slice.141), channel_id=1, source_target_pairs={{0,32},{1,33},{2,34},{3,35},{4,36},{5,37},{6,38},{7,39},{8,40},{9,... | collective-permute-start | bytes 688136 | tf_op jit(solution)/shard_map/ppermute | solution.py:29
  38.8 18.4 %collective-permute-start.7 = (bf16[256,896]{1,0:T(8,128)(2,1)S(1)}, bf16[256,896]{1,0:T(8,128)(2,1)S(1)}, u32[]{:S(2)}, u32[]{:S(2)}) collective-permute-start(bf16[256,896]{1,0:T(8,128)(2,1)S(1)} %copy-done.14), channel_id=1, source_target_pairs={{0,32},{1,33},{2,34},{3,35},{4,36},{5,37},{6,38},{7,39},{8,40},{9,... | collective-permute-start | bytes 1376264 | tf_op jit(solution)/shard_map/ppermute | solution.py:29
  40.7 33.5 %collective-permute-start.18 = (f32[384,896]{1,0:T(8,128)S(1)}, f32[384,896]{1,0:T(8,128)S(1)}, u32[]{:S(2)}, u32[]{:S(2)}) collective-permute-start(f32[384,896]{1,0:T(8,128)S(1)} %get-tuple-element.54), channel_id=1, source_target_pairs={{0,8},{1,9},{2,10},{3,11},{4,12},{5,13},{6,14},{7,15},{8,0},{9,1},... | collective-permute-start | bytes 4128776 | tf_op jit(solution)/shard_map/ppermute | solution.py:29
  49.3 7.9 %copy-start.22 = (bf16[128,896]{1,0:T(8,128)(2,1)}, bf16[128,896]{1,0:T(8,128)(2,1)S(1)}, u32[]{:S(2)}) copy-start(bf16[128,896]{1,0:T(8,128)(2,1)S(1)} %collective-permute-done.21.w2a.refs_11_) | copy-start | bytes 688132
  49.3 8.6 %collective-permute-start = (bf16[4,192,256]{2,1,0:T(8,128)(2,1)S(1)}, bf16[4,192,256]{2,1,0:T(8,128)(2,1)S(1)}, u32[]{:S(2)}, u32[]{:S(2)}) collective-permute-start(bf16[4,192,256]{2,1,0:T(8,128)(2,1)S(1)} %get-tuple-element.43), channel_id=1, source_target_pairs={{0,16},{1,17},{2,18},{3,19},{4,20},{5,21},{6,22},{7,23},{8,24},{9,... | collective-permute-start | bytes 1179656 | tf_op jit(solution)/shard_map/ppermute | solution.py:29
  49.3 7.9 %copy-start.24 = (bf16[128,896]{1,0:T(8,128)(2,1)}, bf16[128,896]{1,0:T(8,128)(2,1)S(1)}, u32[]{:S(2)}) copy-start(bf16[128,896]{1,0:T(8,128)(2,1)S(1)} %collective-permute-done.23.w2b.refs_12_) | copy-start | bytes 688132
  49.3 11.1 %collective-permute-start.1 = (bf16[4,192,256]{2,1,0:T(8,128)(2,1)S(1)}, bf16[4,192,256]{2,1,0:T(8,128)(2,1)S(1)}, u32[]{:S(2)}, u32[]{:S(2)}) collective-permute-start(bf16[4,192,256]{2,1,0:T(8,128)(2,1)S(1)} %get-tuple-element.44), channel_id=1, source_target_pairs={{0,8},{1,9},{2,10},{3,11},{4,12},{5,13},{6,14},{7,15},{8,0},{9,1},... | collective-permute-start | bytes 1179656 | tf_op jit(solution)/shard_map/ppermute | solution.py:29
  52.3 11.9 %collective-permute-start.3 = (bf16[4,192,256]{2,1,0:T(8,128)(2,1)S(1)}, bf16[4,192,256]{2,1,0:T(8,128)(2,1)S(1)}, u32[]{:S(2)}, u32[]{:S(2)}) collective-permute-start(bf16[4,192,256]{2,1,0:T(8,128)(2,1)S(1)} %collective-permute-done.2), channel_id=1, source_target_pairs={{0,17},{1,16},{2,19},{3,18},{4,21},{5,20},{6,23},{7,22},{8,25},{9,... | collective-permute-start | bytes 1179656 | tf_op jit(solution)/shard_map/ppermute | solution.py:29
  57.2 18.5 %collective-permute-start.24 = (f32[384,896]{1,0:T(8,128)S(1)}, f32[384,896]{1,0:T(8,128)S(1)}, u32[]{:S(2)}, u32[]{:S(2)}) collective-permute-start(f32[384,896]{1,0:T(8,128)S(1)} %get-tuple-element.56), channel_id=1, source_target_pairs={{0,8},{1,9},{2,10},{3,11},{4,12},{5,13},{6,14},{7,15},{8,0},{9,1},... | collective-permute-start | bytes 4128776 | tf_op jit(solution)/shard_map/ppermute | solution.py:29
  57.9 11.3 %copy-start.2 = (bf16[4,192,256]{2,1,0:T(8,128)(2,1)}, bf16[4,192,256]{2,1,0:T(8,128)(2,1)S(1)}, u32[]{:S(2)}) copy-start(bf16[4,192,256]{2,1,0:T(8,128)(2,1)S(1)} %collective-permute-done.t1) | copy-start | bytes 1179652
  57.9 6.3 %collective-permute-start.6 = (bf16[128,896]{1,0:T(8,128)(2,1)S(1)}, bf16[128,896]{1,0:T(8,128)(2,1)S(1)}, u32[]{:S(2)}, u32[]{:S(2)}) collective-permute-start(bf16[128,896]{1,0:T(8,128)(2,1)S(1)} %slice.132), channel_id=1, source_target_pairs={{0,96},{1,97},{2,98},{3,99},{4,100},{5,101},{6,102},{7,103},{8,104... | collective-permute-start | bytes 688136 | tf_op jit(solution)/shard_map/ppermute | solution.py:29
  60.4 8.8 %copy-start.4 = (bf16[4,192,256]{2,1,0:T(8,128)(2,1)}, bf16[4,192,256]{2,1,0:T(8,128)(2,1)S(1)}, u32[]{:S(2)}) copy-start(bf16[4,192,256]{2,1,0:T(8,128)(2,1)S(1)} %collective-permute-done.1.t2) | copy-start | bytes 1179652
  60.4 6.1 %collective-permute-start.8 = (bf16[128,896]{1,0:T(8,128)(2,1)S(1)}, bf16[128,896]{1,0:T(8,128)(2,1)S(1)}, u32[]{:S(2)}, u32[]{:S(2)}) collective-permute-start(bf16[128,896]{1,0:T(8,128)(2,1)S(1)} %slice.133), channel_id=1, source_target_pairs={{0,32},{1,33},{2,34},{3,35},{4,36},{5,37},{6,38},{7,39},{8,40},{9,... | collective-permute-start | bytes 688136 | tf_op jit(solution)/shard_map/ppermute | solution.py:29
  64.2 5.0 %copy-start.6 = (bf16[4,192,256]{2,1,0:T(8,128)(2,1)}, bf16[4,192,256]{2,1,0:T(8,128)(2,1)S(1)}, u32[]{:S(2)}) copy-start(bf16[4,192,256]{2,1,0:T(8,128)(2,1)S(1)} %collective-permute-done.3.t3) | copy-start | bytes 1179652
  69.2 9.5 %collective-permute-start.9 = (f32[384,896]{1,0:T(8,128)}, f32[384,896]{1,0:T(8,128)}, u32[]{:S(2)}, u32[]{:S(2)}) collective-permute-start(f32[384,896]{1,0:T(8,128)} %get-tuple-element.48), channel_id=1, source_target_pairs={{0,8},{1,9},{2,10},{3,11},{4,12},{5,13},{6,14},{7,15},{8,0},{9,1},... | collective-permute-start | bytes 4128776 | tf_op jit(solution)/shard_map/ppermute | solution.py:29
  75.7 17.4 %collective-permute-start.19 = (bf16[384,896]{1,0:T(8,128)(2,1)}, bf16[384,896]{1,0:T(8,128)(2,1)}, u32[]{:S(2)}, u32[]{:S(2)}) collective-permute-start(bf16[384,896]{1,0:T(8,128)(2,1)} %get-tuple-element.85), channel_id=1, source_target_pairs={{0,16},{1,17},{2,18},{3,19},{4,20},{5,21},{6,22},{7,23},{8,24},{9,... | collective-permute-start | bytes 2064392 | tf_op jit(solution)/shard_map/ppermute | solution.py:29
  77.2 30.6 %collective-permute-start.25 = (bf16[384,896]{1,0:T(8,128)(2,1)}, bf16[384,896]{1,0:T(8,128)(2,1)}, u32[]{:S(2)}, u32[]{:S(2)}) collective-permute-start(bf16[384,896]{1,0:T(8,128)(2,1)} %get-tuple-element.87), channel_id=1, source_target_pairs={{0,16},{1,17},{2,18},{3,19},{4,20},{5,21},{6,22},{7,23},{8,24},{9,... | collective-permute-start | bytes 2064392 | tf_op jit(solution)/shard_map/ppermute | solution.py:29
  81.5 41.1 %collective-permute-start.10 = (bf16[384,896]{1,0:T(8,128)(2,1)}, bf16[384,896]{1,0:T(8,128)(2,1)}, u32[]{:S(2)}, u32[]{:S(2)}) collective-permute-start(bf16[384,896]{1,0:T(8,128)(2,1)} %get-tuple-element.80), channel_id=1, source_target_pairs={{0,16},{1,17},{2,18},{3,19},{4,20},{5,21},{6,22},{7,23},{8,24},{9,... | collective-permute-start | bytes 2064392 | tf_op jit(solution)/shard_map/ppermute | solution.py:29
  94.3 14.7 %copy-start.28 = (f32[384,896]{1,0:T(8,128)S(1)}, f32[384,896]{1,0:T(8,128)}, u32[]{:S(2)}) copy-start(f32[384,896]{1,0:T(8,128)} %get-tuple-element.86) | copy-start | bytes 4128772
  94.3 14.7 %copy-start.29 = (f32[384,896]{1,0:T(8,128)S(1)}, f32[384,896]{1,0:T(8,128)}, u32[]{:S(2)}) copy-start(f32[384,896]{1,0:T(8,128)} %get-tuple-element.88) | copy-start | bytes 4128772
  111.0 12.8 %collective-permute-start.44 = (bf16[384,896]{1,0:T(8,128)(2,1)}, bf16[384,896]{1,0:T(8,128)(2,1)}, u32[]{:S(2)}, u32[]{:S(2)}) collective-permute-start(bf16[384,896]{1,0:T(8,128)(2,1)} %get-tuple-element.74.mine), channel_id=1, source_target_pairs={{0,8},{1,9},{2,10},{3,11},{4,12},{5,13},{6,14},{7,15},{8,0},{9,1},... | collective-permute-start | bytes 2064392 | tf_op jit(solution)/shard_map/ppermute | solution.py:29
  127.1 6.4 %collective-permute-start.47 = (bf16[128,896]{1,0:T(8,128)(2,1)S(1)}, bf16[128,896]{1,0:T(8,128)(2,1)S(1)}, u32[]{:S(2)}, u32[]{:S(2)}) collective-permute-start(bf16[128,896]{1,0:T(8,128)(2,1)S(1)} %get-tuple-element.79), channel_id=1, source_target_pairs={{0,96},{1,97},{2,98},{3,99},{4,100},{5,101},{6,102},{7,103},{8,104... | collective-permute-start | bytes 688136 | tf_op jit(solution)/shard_map/ppermute | solution.py:29
  127.9 9.7 %collective-permute-start.26 = (bf16[384,896]{1,0:T(8,128)(2,1)S(1)}, bf16[384,896]{1,0:T(8,128)(2,1)S(1)}, u32[]{:S(2)}, u32[]{:S(2)}) collective-permute-start(bf16[384,896]{1,0:T(8,128)(2,1)S(1)} %get-tuple-element.90.refs_0_.mine), channel_id=1, source_target_pairs={{0,8},{1,9},{2,10},{3,11},{4,12},{5,13},{6,14},{7,15},{8,0},{9,1},... | collective-permute-start | bytes 2064392 | tf_op jit(solution)/shard_map/ppermute | solution.py:29
  128.8 8.9 %collective-permute-start.27 = (bf16[384,896]{1,0:T(8,128)(2,1)S(1)}, bf16[384,896]{1,0:T(8,128)(2,1)S(1)}, u32[]{:S(2)}, u32[]{:S(2)}) collective-permute-start(bf16[384,896]{1,0:T(8,128)(2,1)S(1)} %get-tuple-element.89.refs_2_.mine), channel_id=1, source_target_pairs={{0,8},{1,9},{2,10},{3,11},{4,12},{5,13},{6,14},{7,15},{8,0},{9,1},... | collective-permute-start | bytes 2064392 | tf_op jit(solution)/shard_map/ppermute | solution.py:29
  129.0 8.0 %collective-permute-start.45 = (bf16[128,896]{1,0:T(8,128)(2,1)S(1)}, bf16[128,896]{1,0:T(8,128)(2,1)S(1)}, u32[]{:S(2)}, u32[]{:S(2)}) collective-permute-start(bf16[128,896]{1,0:T(8,128)(2,1)S(1)} %get-tuple-element.77), channel_id=1, source_target_pairs={{0,32},{1,33},{2,34},{3,35},{4,36},{5,37},{6,38},{7,39},{8,40},{9,... | collective-permute-start | bytes 688136 | tf_op jit(solution)/shard_map/ppermute | solution.py:29
  133.5 4.2 %copy-start.9 = (bf16[256,896]{1,0:T(8,128)(2,1)S(1)}, bf16[256,896]{1,0:T(8,128)(2,1)}, u32[]{:S(2)}) copy-start(bf16[256,896]{1,0:T(8,128)(2,1)} %copy-done.8) | copy-start | bytes 1376260
  133.6 4.2 %copy-start.11 = (bf16[256,896]{1,0:T(8,128)(2,1)S(1)}, bf16[256,896]{1,0:T(8,128)(2,1)}, u32[]{:S(2)}) copy-start(bf16[256,896]{1,0:T(8,128)(2,1)} %copy-done.10) | copy-start | bytes 1376260
  133.7 29.8 %collective-permute-start.48 = (bf16[256,896]{1,0:T(8,128)(2,1)S(1)}, bf16[256,896]{1,0:T(8,128)(2,1)S(1)}, u32[]{:S(2)}, u32[]{:S(2)}) collective-permute-start(bf16[256,896]{1,0:T(8,128)(2,1)S(1)} %pad_maximum_fusion.5), channel_id=1, source_target_pairs={{0,96},{1,97},{2,98},{3,99},{4,100},{5,101},{6,102},{7,103},{8,104... | collective-permute-start | bytes 1376264 | tf_op jit(solution)/shard_map/ppermute | solution.py:29
  137.1 27.9 %collective-permute-start.46 = (bf16[256,896]{1,0:T(8,128)(2,1)S(1)}, bf16[256,896]{1,0:T(8,128)(2,1)S(1)}, u32[]{:S(2)}, u32[]{:S(2)}) collective-permute-start(bf16[256,896]{1,0:T(8,128)(2,1)S(1)} %pad_maximum_fusion.4), channel_id=1, source_target_pairs={{0,32},{1,33},{2,34},{3,35},{4,36},{5,37},{6,38},{7,39},{8,40},{9,... | collective-permute-start | bytes 1376264 | tf_op jit(solution)/shard_map/ppermute | solution.py:29
  142.6 8.9 %collective-permute-start.30 = (bf16[384,256]{1,0:T(8,128)(2,1)S(1)}, bf16[384,256]{1,0:T(8,128)(2,1)S(1)}, u32[]{:S(2)}, u32[]{:S(2)}) collective-permute-start(bf16[384,256]{1,0:T(8,128)(2,1)S(1)} %get-tuple-element.63), channel_id=1, source_target_pairs={{0,6},{1,7},{2,0},{3,1},{4,2},{5,3},{6,4},{7,5},{8,14},{9,15},{10,... | collective-permute-start | bytes 589832 | tf_op jit(solution)/shard_map/ppermute | solution.py:29
  145.2 6.5 %collective-permute-start.28 = (bf16[384,256]{1,0:T(8,128)(2,1)S(1)}, bf16[384,256]{1,0:T(8,128)(2,1)S(1)}, u32[]{:S(2)}, u32[]{:S(2)}) collective-permute-start(bf16[384,256]{1,0:T(8,128)(2,1)S(1)} %get-tuple-element.61), channel_id=1, source_target_pairs={{0,2},{1,3},{2,4},{3,5},{4,6},{5,7},{6,0},{7,1},{8,10},{9,11},{10,... | collective-permute-start | bytes 589832 | tf_op jit(solution)/shard_map/ppermute | solution.py:29
  147.3 7.2 %collective-permute-start.38 = (bf16[128,896]{1,0:T(8,128)(2,1)S(1)}, bf16[128,896]{1,0:T(8,128)(2,1)S(1)}, u32[]{:S(2)}, u32[]{:S(2)}) collective-permute-start(bf16[128,896]{1,0:T(8,128)(2,1)S(1)} %get-tuple-element.68), channel_id=1, source_target_pairs={{0,96},{1,97},{2,98},{3,99},{4,100},{5,101},{6,102},{7,103},{8,104... | collective-permute-start | bytes 688136 | tf_op jit(solution)/shard_map/ppermute | solution.py:29
  151.5 6.2 %collective-permute-start.36 = (bf16[128,896]{1,0:T(8,128)(2,1)S(1)}, bf16[128,896]{1,0:T(8,128)(2,1)S(1)}, u32[]{:S(2)}, u32[]{:S(2)}) collective-permute-start(bf16[128,896]{1,0:T(8,128)(2,1)S(1)} %get-tuple-element.66), channel_id=1, source_target_pairs={{0,32},{1,33},{2,34},{3,35},{4,36},{5,37},{6,38},{7,39},{8,40},{9,... | collective-permute-start | bytes 688136 | tf_op jit(solution)/shard_map/ppermute | solution.py:29
  151.7 8.7 %collective-permute-start.42 = (bf16[128,896]{1,0:T(8,128)(2,1)S(1)}, bf16[128,896]{1,0:T(8,128)(2,1)S(1)}, u32[]{:S(2)}, u32[]{:S(2)}) collective-permute-start(bf16[128,896]{1,0:T(8,128)(2,1)S(1)} %get-tuple-element.73), channel_id=1, source_target_pairs={{0,96},{1,97},{2,98},{3,99},{4,100},{5,101},{6,102},{7,103},{8,104... | collective-permute-start | bytes 688136 | tf_op jit(solution)/shard_map/ppermute | solution.py:29
  154.5 8.8 %collective-permute-start.40 = (bf16[128,896]{1,0:T(8,128)(2,1)S(1)}, bf16[128,896]{1,0:T(8,128)(2,1)S(1)}, u32[]{:S(2)}, u32[]{:S(2)}) collective-permute-start(bf16[128,896]{1,0:T(8,128)(2,1)S(1)} %get-tuple-element.71), channel_id=1, source_target_pairs={{0,32},{1,33},{2,34},{3,35},{4,36},{5,37},{6,38},{7,39},{8,40},{9,... | collective-permute-start | bytes 688136 | tf_op jit(solution)/shard_map/ppermute | solution.py:29
  157.7 9.6 %collective-permute-start.31 = (bf16[768,256]{1,0:T(8,128)(2,1)S(1)}, bf16[768,256]{1,0:T(8,128)(2,1)S(1)}, u32[]{:S(2)}, u32[]{:S(2)}) collective-permute-start(bf16[768,256]{1,0:T(8,128)(2,1)S(1)} %pad_maximum_fusion.7), channel_id=1, source_target_pairs={{0,6},{1,7},{2,0},{3,1},{4,2},{5,3},{6,4},{7,5},{8,14},{9,15},{10,... | collective-permute-start | bytes 1179656 | tf_op jit(solution)/shard_map/ppermute | solution.py:29
  160.4 7.9 %collective-permute-start.29 = (bf16[768,256]{1,0:T(8,128)(2,1)S(1)}, bf16[768,256]{1,0:T(8,128)(2,1)S(1)}, u32[]{:S(2)}, u32[]{:S(2)}) collective-permute-start(bf16[768,256]{1,0:T(8,128)(2,1)S(1)} %pad_maximum_fusion.6), channel_id=1, source_target_pairs={{0,2},{1,3},{2,4},{3,5},{4,6},{5,7},{6,0},{7,1},{8,10},{9,11},{10,... | collective-permute-start | bytes 1179656 | tf_op jit(solution)/shard_map/ppermute | solution.py:29
  163.3 12.5 %collective-permute-start.39 = (bf16[256,896]{1,0:T(8,128)(2,1)S(1)}, bf16[256,896]{1,0:T(8,128)(2,1)S(1)}, u32[]{:S(2)}, u32[]{:S(2)}) collective-permute-start(bf16[256,896]{1,0:T(8,128)(2,1)S(1)} %pad_maximum_fusion.1), channel_id=1, source_target_pairs={{0,96},{1,97},{2,98},{3,99},{4,100},{5,101},{6,102},{7,103},{8,104... | collective-permute-start | bytes 1376264 | tf_op jit(solution)/shard_map/ppermute | solution.py:29
  163.5 16.7 %collective-permute-start.37 = (bf16[256,896]{1,0:T(8,128)(2,1)S(1)}, bf16[256,896]{1,0:T(8,128)(2,1)S(1)}, u32[]{:S(2)}, u32[]{:S(2)}) collective-permute-start(bf16[256,896]{1,0:T(8,128)(2,1)S(1)} %pad_maximum_fusion), channel_id=1, source_target_pairs={{0,32},{1,33},{2,34},{3,35},{4,36},{5,37},{6,38},{7,39},{8,40},{9,... | collective-permute-start | bytes 1376264 | tf_op jit(solution)/shard_map/ppermute | solution.py:29
  165.0 16.9 %collective-permute-start.43 = (bf16[256,896]{1,0:T(8,128)(2,1)S(1)}, bf16[256,896]{1,0:T(8,128)(2,1)S(1)}, u32[]{:S(2)}, u32[]{:S(2)}) collective-permute-start(bf16[256,896]{1,0:T(8,128)(2,1)S(1)} %pad_maximum_fusion.3), channel_id=1, source_target_pairs={{0,96},{1,97},{2,98},{3,99},{4,100},{5,101},{6,102},{7,103},{8,104... | collective-permute-start | bytes 1376264 | tf_op jit(solution)/shard_map/ppermute | solution.py:29
  167.3 18.5 %collective-permute-start.41 = (bf16[256,896]{1,0:T(8,128)(2,1)S(1)}, bf16[256,896]{1,0:T(8,128)(2,1)S(1)}, u32[]{:S(2)}, u32[]{:S(2)}) collective-permute-start(bf16[256,896]{1,0:T(8,128)(2,1)S(1)} %pad_maximum_fusion.2), channel_id=1, source_target_pairs={{0,32},{1,33},{2,34},{3,35},{4,36},{5,37},{6,38},{7,39},{8,40},{9,... | collective-permute-start | bytes 1376264 | tf_op jit(solution)/shard_map/ppermute | solution.py:29
  168.5 18.3 %collective-permute-start.34 = (f32[192,256]{1,0:T(8,128)S(1)}, f32[192,256]{1,0:T(8,128)S(1)}, u32[]{:S(2)}, u32[]{:S(2)}) collective-permute-start(f32[192,256]{1,0:T(8,128)S(1)} %get-tuple-element.102), channel_id=1, source_target_pairs={{0,8},{1,24},{2,10},{3,26},{4,12},{5,28},{6,14},{7,30},{8,0},{9,16... | collective-permute-start | bytes 589832 | tf_op jit(solution)/shard_map/ppermute | solution.py:29
  175.9 10.9 %collective-permute-start.35 = (f32[192,256]{1,0:T(8,128)S(1)}, f32[192,256]{1,0:T(8,128)S(1)}, u32[]{:S(2)}, u32[]{:S(2)}) collective-permute-start(f32[192,256]{1,0:T(8,128)S(1)} %get-tuple-element.101), channel_id=1, source_target_pairs={{0,24},{1,8},{2,26},{3,10},{4,28},{5,12},{6,30},{7,14},{8,16},{9,0... | collective-permute-start | bytes 589832 | tf_op jit(solution)/shard_map/ppermute | solution.py:29
  180.1 6.7 %collective-permute-start.32 = (f32[192,256]{1,0:T(8,128)S(1)}, f32[192,256]{1,0:T(8,128)S(1)}, u32[]{:S(2)}, u32[]{:S(2)}) collective-permute-start(f32[192,256]{1,0:T(8,128)S(1)} %get-tuple-element.100), channel_id=1, source_target_pairs={{0,0},{1,16},{2,2},{3,18},{4,4},{5,20},{6,6},{7,22},{8,8},{9,24},{... | collective-permute-start | bytes 589832 | tf_op jit(solution)/shard_map/ppermute | solution.py:29
  181.9 7.8 %collective-permute-start.33 = (f32[192,256]{1,0:T(8,128)S(1)}, f32[192,256]{1,0:T(8,128)S(1)}, u32[]{:S(2)}, u32[]{:S(2)}) collective-permute-start(f32[192,256]{1,0:T(8,128)S(1)} %get-tuple-element.99), channel_id=1, source_target_pairs={{0,16},{1,0},{2,18},{3,2},{4,20},{5,4},{6,22},{7,6},{8,24},{9,8},{... | collective-permute-start | bytes 589832 | tf_op jit(solution)/shard_map/ppermute | solution.py:29
  (16 other events, 50.4 us)

commit v2 on v0

v2 whole, which is shorter than its diff:
```python
import functools

import jax
import jax.numpy as jnp
from jax import lax
from jax.experimental import pallas as pl
from jax.experimental.pallas import tpu as pltpu
from jax.sharding import PartitionSpec as P

FF = 14336
F32 = jnp.float32
BF16 = jnp.bfloat16
CHUNKS = (384, 512)
SCALE = 1.0
VMEM = pl.BlockSpec(memory_space=pltpu.VMEM)
SMEM = pl.BlockSpec(memory_space=pltpu.SMEM)
PARAMS = pltpu.CompilerParams(vmem_limit_bytes=32 * 1024 * 1024)


def _split(device):
    dp, tensor = divmod(device, 8)
    return dp // 4, (dp // 2) % 2, dp % 2, tensor // 2, tensor % 2


def _join(z, yl, c, x, yh):
    return ((z % 4) * 4 + yl * 2 + c) * 8 + (x % 4) * 2 + yh


def _move(value, where):
    pairs = [(d, _join(*where(*_split(d)))) for d in range(128)]
    return lax.ppermute(value, ("dp", "tensor"), pairs)


def z_shift(value, by):
    return _move(value, lambda z, yl, c, x, yh: (z + by, yl, c, x, yh))


def x_shift(value, by):
    return _move(value, lambda z, yl, c, x, yh: (z, yl, c, x + by, yh))


def core_swap(value):
    return _move(value, lambda z, yl, c, x, yh: (z, yl, 1 - c, x, yh))


def y_swap(value):
    return _move(value, lambda z, yl, c, x, yh: (z, 1 - yl, c, x, yh))


def far_swap(value):
    return _move(value, lambda z, yl, c, x, yh: (z, 1 - yl, 1 - c, x, 1 - yh))


def after(value, *others):
    return lax.optimization_barrier((value, *others))[0]


def shape(*dims, dtype=F32):
    return jax.ShapeDtypeStruct(dims, dtype)


def local_kernel(kernel, outs, microseconds, *args, scalars=0, scratch=()):
    return pl.pallas_call(
        kernel,
        in_specs=[SMEM] * scalars + [VMEM] * (len(args) - scalars),
        out_specs=[VMEM] * len(outs),
        out_shape=outs,
        scratch_shapes=scratch,
        compiler_params=PARAMS,
        cost_estimate=cost(microseconds),
    )(*args)


def cost(microseconds):
    return pl.CostEstimate(
        flops=int(microseconds * SCALE * 1.1e9), bytes_accessed=1000, transcendentals=0
    )


def arrange_kernel(source, included, x, cotangents, *outs):
    for block in range(16):
        columns = pl.ds(pl.multiple_of(source[block] * 256, 256), 256)
        out, k = outs[block // 4], block % 4
        out[0, k] = x[:, columns]
        total = jnp.zeros((x.shape[0], 256), F32)
        for later in range(4):
            total = total + included[later].astype(F32) * cotangents[later, :, columns].astype(F32)
        out[1, k] = total.astype(BF16)


def arrange(source, included, activations, cotangents):
    rows = 48
    return pl.pallas_call(
        arrange_kernel,
        grid_spec=pltpu.PrefetchScalarGridSpec(
            num_scalar_prefetch=2,
            grid=(192 // rows,),
            in_specs=[
                pl.BlockSpec((rows, 4096), lambda i, *_: (i, 0)),
                pl.BlockSpec((4, rows, 4096), lambda i, *_: (0, i, 0)),
            ],
            out_specs=[pl.BlockSpec((2, 4, rows, 256), lambda i, *_: (0, 0, i, 0))] * 4,
        ),
        out_shape=[shape(2, 4, 192, 256, dtype=BF16)] * 4,
        compiler_params=PARAMS,
        cost_estimate=cost(3.0),
    )(source, included, activations, cotangents)


def spread(kept, far, sibling, sibling_far):
    return (kept, y_swap(far), core_swap(sibling), far_swap(sibling_far))


def turn_kernel(t0, t1, t2, t3, *outs):
    for which, out in enumerate(outs):
        for k in range(4):
            whole = jnp.concatenate([t[which, k] for t in (t0, t1, t2, t3)], axis=0)
            out[k * 256 : (k + 1) * 256, :] = whole.T


def fill(rows, far, low, high, own, nxt, prev):
    far[0:384] = low[...]
    far[384:768] = high[...]
    for m in range(rows.shape[0]):
        for k, part in enumerate((own, nxt, far, prev)):
            rows[m, k * 256 : (k + 1) * 256] = part[m * 256 : (m + 1) * 256]


def pre_kernel(t0, t1, t2, t3, own, nxt, low, high, prev, keep, s0, s1, s2, left, rows, far):
    fill(rows, far, low, high, own, nxt, prev)
    for outs, first, second in (((s0, s1, s2), t2, t3), (keep, t0, t1)):
        for which in range(2):
            for k in range(4):
                left[0:192, k * 256 : (k + 1) * 256] = first[which, k]
                left[192:384, k * 256 : (k + 1) * 256] = second[which, k]
            for m in ((0, 1), (2,))[which]:
                block = jnp.dot(left[...], rows[m], preferred_element_type=F32)
                if outs is keep:
                    keep[m] = block
                else:
                    outs[m][...] = block


def delta_kernel(half, other, other_grad, out):
    def part(first, swapped):
        @pl.loop(0, 192 // 16)
        def _(i):
            mine = pl.ds(pl.multiple_of(first + i * 16, 16), 16)
            theirs = pl.ds(pl.multiple_of(swapped + i * 16, 16), 16)
            gate, up = (half[m, mine] + other[m, theirs].astype(F32) for m in range(2))
            grad = half[2, mine] + other_grad[theirs].astype(F32)
            sigmoid = jax.nn.sigmoid(gate)
            silu = gate * sigmoid
            out[0, mine] = (grad * up * sigmoid * (1.0 + gate * (1.0 - sigmoid))).astype(BF16)
            out[1, mine] = (grad * silu).astype(BF16)
            out[2, mine] = (silu * up).astype(BF16)

    part(0, 192)
    part(192, 0)


def grad_kernel(tokens, cotangents, mine, theirs, b0, b1, low, high, b3, right):
    for m in range(3):
        right[0:384] = mine[m]
        right[384:768] = theirs[m]
        left = tokens if m < 2 else cotangents
        for k in (2, 1, 3, 0):
            block = jnp.dot(
                left[k * 256 : (k + 1) * 256, :], right[...], preferred_element_type=F32
            )
            if k != 2:
                (b0, b1, None, b3)[k][m * 256 : (m + 1) * 256] = block
                continue
            block = block.astype(BF16)
            if m == 0:
                low[0:256] = block
            elif m == 1:
                low[256:384] = block[:128]
                high[0:128] = block[128:]
            else:
                high[128:384] = block


def middle_kernel(b1, b3, low, high, ahead, behind):
    ahead[0:384] = (b1[0:384] + low[...].astype(F32)).astype(BF16)
    ahead[384:768] = b1[384:768].astype(BF16)
    behind[0:384] = b3[0:384].astype(BF16)
    behind[384:768] = (b3[384:768] + high[...].astype(F32)).astype(BF16)


def finish_kernel(*refs):
    parts, outs = refs[:-3], refs[-3:]
    for m, out in enumerate(outs):
        rows = slice(m * 256, (m + 1) * 256)
        first = 0
        for i in range(len(parts) // 3):
            b0, r1, r3 = parts[3 * i : 3 * i + 3]
            last = first + b0.shape[1]
            out[:, first:last] = b0[rows] + r1[rows].astype(F32) + r3[rows].astype(F32)
            first = last


def input_kernel(last, has_total, order, mine, theirs, own, nxt, low, high, prev, *refs):
    if has_total:
        total, *refs = refs
    *outs, rows, far = refs
    fill(rows, far, low, high, own, nxt, prev)
    over_units = (((1,), (1,)), ((), ()))
    for j in range(4):
        here = pl.ds(pl.multiple_of(order[j] * 256, 256), 256)
        for part, delta in enumerate((mine, theirs)):
            tokens = slice(part * 384, (part + 1) * 384)
            block = lax.dot_general(
                delta[0], rows[0, here, :], over_units, preferred_element_type=F32
            ) + lax.dot_general(delta[1], rows[1, here, :], over_units, preferred_element_type=F32)
            if has_total:
                block = block + total[j, tokens]
            if last:
                outs[j][tokens] = block.astype(outs[j].dtype)
            else:
                outs[0][j, tokens] = block


def local(activations, cotangents, gate_weight, up_weight, down_weight):
    dp, tensor = lax.axis_index("dp"), lax.axis_index("tensor")
    z, yl, c = dp // 4, (dp // 2) % 2, dp % 2
    x, yh = tensor // 2, tensor % 2
    source = jnp.stack(
        [
            ((z + k) % 4) * 4 + (yl ^ far) * 2 + (c ^ sibling)
            for sibling in range(2)
            for far in range(2)
            for k in range(4)
        ]
    ).astype(jnp.int32)
    first_unit = tensor * gate_weight.shape[1]
    band_index = (
        1
        + (first_unit >= FF // 8).astype(jnp.int32)
        + (first_unit >= FF // 4).astype(jnp.int32)
        + (first_unit >= FF // 2).astype(jnp.int32)
    )
    included = jnp.stack([(k + 1 >= band_index).astype(jnp.int32) for k in range(4)])
    order = jnp.stack([(x + j - z) % 4 for j in range(4)]).astype(jnp.int32)

    rows, first = [], 0
    for width in CHUNKS:
        own = jnp.concatenate(
            [w[:, first : first + width] for w in (gate_weight, up_weight, down_weight)], axis=0
        )
        if rows:
            own = after(own, rows[-1][1])
        nxt, prev = z_shift(own, -1), z_shift(own, 1)
        rows.append((own, nxt, z_shift(nxt[:384], -1), z_shift(prev[384:], 1), prev))
        first += width

    pieces = spread(*arrange(source, included, activations, cotangents))
    turned = local_kernel(turn_kernel, [shape(1024, 768, dtype=BF16)] * 2, 3.0, *pieces)

    halves = []
    for i, width in enumerate(CHUNKS):
        own, nxt, low, high, prev = rows[i]
        late = pieces[0]
        if i == 1:
            late = after(late, halves[0][1], *turned)
        keep, *send = local_kernel(
            pre_kernel,
            [shape(3, 384, width)] + [shape(384, width)] * 3,
            width / 128,
            late,
            *pieces[1:],
            own,
            nxt,
            low,
            high,
            prev,
            scratch=(
                pltpu.VMEM((384, 1024), BF16),
                pltpu.VMEM((3, 1024, width), BF16),
                pltpu.VMEM((768, width), BF16),
            ),
        )
        received = [core_swap(part) for part in send]
        if halves:
            received[0] = after(received[0], halves[-1][2])
        half = keep + jnp.stack(received)
        pair, single = half[:2].astype(BF16), half[2].astype(BF16)
        sent = (pair, single)
        halves.append((half, y_swap(pair), y_swap(single)))
        if i == 0:
            own, nxt, low, high, prev = rows[1]
            nxt_late, prev_late = after(nxt, *sent), after(prev, *sent)
            rows[1] = (own, nxt, z_shift(nxt_late[:384], -1), z_shift(prev_late[384:], 1), prev)

    total, ready, finished = None, None, []
    for i, width in enumerate(CHUNKS):
        half, other, other_grad = halves[i]
        if ready is not None:
            other = after(other, *ready)

        (mine,) = local_kernel(
            delta_kernel, [shape(3, 384, width, dtype=BF16)], width / 256, half, other, other_grad
        )
        theirs = core_swap(mine)
        last = i == len(CHUNKS) - 1
        outs = [shape(4, 768, 256)]
        if last:
            outs = [shape(768, 256)] + [shape(768, 256, dtype=BF16)] * 3
        partial = local_kernel(
            functools.partial(input_kernel, last, total is not None),
            outs,
            width / 128,
            order,
            mine,
            theirs,
            *rows[i],
            *(() if total is None else (total,)),
            scalars=1,
            scratch=(pltpu.VMEM((2, 1024, width), BF16), pltpu.VMEM((768, width), BF16)),
        )
        total = partial[0]
        b0, b1, low, high, b3 = local_kernel(
            grad_kernel,
            [shape(768, width)] * 2
            + [shape(384, width, dtype=BF16)] * 2
            + [shape(768, width)],
            width / 128,
            *turned,
            mine,
            theirs,
            scratch=(pltpu.VMEM((768, width), BF16),),
        )
        ahead, behind = local_kernel(
            middle_kernel,
            [shape(768, width, dtype=BF16)] * 2,
            width / 400,
            b1,
            b3,
            z_shift(low, 1),
            z_shift(high, -1),
        )
        finished += [b0, z_shift(ahead, 1), z_shift(behind, -1)]
        ready = (*finished[-2:], total)
    gate_grad, up_grad, down_grad = local_kernel(
        finish_kernel, [shape(256, sum(CHUNKS))] * 3, 2.0, *finished
    )

    columns = (
        partial[0]
        + x_shift(partial[1], 1).astype(F32)
        + x_shift(partial[2], 2).astype(F32)
        + x_shift(partial[3], -1).astype(F32)
    ).reshape(2, 2, 192, 256)
    sides = []
    for j in range(2):
        moved = []
        for i in range(2):
            block = lax.dynamic_index_in_dim(columns[j], (i + yh + yl) % 2, 0, keepdims=False)
            moved.append(
                _move(block, lambda z, yl, c, x, yh, i=i, j=j: (z, yh ^ i, c ^ j, x, yl))
            )
        sides.append(moved[0] + moved[1])
    input_grad = jnp.where(
        c == 0,
        jnp.concatenate([sides[0], sides[1]], axis=1),
        jnp.concatenate([sides[1], sides[0]], axis=1),
    )
    return (input_grad, gate_grad, up_grad, down_grad)


def solution(mesh):
    return jax.shard_map(
        local,
        mesh=mesh,
        in_specs=(
            P("dp", None),
            P(None, "dp", None),
            P("dp", "tensor"),
            P("dp", "tensor"),
            P("dp", "tensor"),
        ),
        out_specs=(P("dp", "tensor"), P("dp", "tensor"), P("dp", "tensor"), P("dp", "tensor")),
        check_vma=False,
    )
```

time: 404 us -> 177 us (0.44)
  waiting for transfers between devices: 327 us -> 67.5 us
  matrix products: 42 us -> 0 us
  starting transfers between devices: 10.6 us -> 48.4 us
  Pallas kernels: 0 us -> 28.3 us
  local copies, waits for them, and re-layouts: 6 us -> 24 us
  between operations: 14.2 us -> 1.24 us
    all_gather x6 -> x0, waiting for transfers between devices: 215 us -> none  [the longest x1 47.1 us: local(): lax.all_gather(down_weight, 'dp', axis=0, tiled=True)]
    reduce_scatter x1 -> x0, waiting for transfers between devices: 76.5 us -> none  [local(): lax.psum_scatter(partial_input, 'tensor', scatter_dimension=1, tiled=True)]
    ppermute x0 -> x38, waiting for transfers between devices: none -> 67.5 us  [_move(): return lax.ppermute(value, ('dp', 'tensor'), pairs)]
    ppermute x0 -> x38, starting transfers between devices: none -> 48.4 us  [_move(): return lax.ppermute(value, ('dp', 'tensor'), pairs)]
    dot_general x8 -> x0, matrix products: 42 us -> none  [the longest x1 6.27 us: local(): up_pre = jnp.dot(activations, full_up, preferred_element_type=jnp.float32)]
    all_to_all x2 -> x0, waiting for transfers between devices: 31.7 us -> none  [the longest x1 31.7 us: local(): lax.all_to_all(activations, 'dp', split_axis=1, concat_axis=0, tiled=True)]
    pallas_call x0 -> x13, Pallas kernels: none -> 28.3 us  [the longest x12 25.8 us: local_kernel(): pl.pallas_call(kernel, in_specs=[SMEM] * scalars + [VMEM] * (len(args) -...]
    unnamed x9 -> x88, local copies, waits for them, and re-layouts: 2.9 us -> 17.5 us
  transfers between devices with their start and end apart: 9 -> 38, of which waited for: 8 -> 15; matrix products, arithmetic and copies ran while one was open for 11% -> 5% of each run, Pallas kernels for 0% -> 11%
where the time goes in v2:
time: 177 us; the launch traced here: 175 us
  waiting for transfers between devices  67.5 us (38%)
  starting transfers between devices  48.4 us (27%)
  Pallas kernels  28.3 us (16%)
  local copies, waits for them, and re-layouts  24 us (14%)
  other arithmetic  5.38 us (3%)
    ppermute x38, waiting for transfers between devices, _move(): return lax.ppermute(value, ('dp', 'tensor'), pairs)  67.5 us
    ppermute x38, starting transfers between devices, _move(): return lax.ppermute(value, ('dp', 'tensor'), pairs)  48.4 us
    pallas_call x12, Pallas kernels, local_kernel(): pl.pallas_call(kernel, in_specs=[SMEM] * scalars + [VMEM] * (len(args) -...  25.8 us
    unnamed x88, local copies, waits for them, and re-layouts  17.5 us
  transfers between devices with their start and end apart: 38, of which 15 were waited for; matrix products, arithmetic and copies ran while one was open for 5% of the time, Pallas kernels for 11%

profile of v2, /device:TPU:1, one launch (start us, length us, event | category | flops | bytes accessed | tf_op | source)
XLA Modules:
  0.0 174.8 jit_solution(7765785294438547749)
XLA Ops:
  0.6 1.1 slice.56
  1.7 0.9 slice.57
  3.7 2.5 %collective-permute-start.5 = (bf16[768,384]{1,0:T(8,128)(2,1)S(1)}, bf16[768,384]{1,0:T(8,128)(2,1)S(1)}, u32[]{:S(2)}, u32[]{:S(2)}) collective-permute-start(bf16[768,384]{1,0:T(8,128)(2,1)S(1)} %pad_maximum_fusion.1.own), channel_id=1, source_target_pairs={{0,32},{1,33},{2,34},{3,35},{4,36},{5,37},{6,38},{7,39},{8,40},{9,... | collective-permute-start | bytes 1769480 | tf_op jit(solution)/shard_map/ppermute | solution.py:31
  6.2 2.2 %collective-permute-start.3 = (bf16[768,384]{1,0:T(8,128)(2,1)S(1)}, bf16[768,384]{1,0:T(8,128)(2,1)S(1)}, u32[]{:S(2)}, u32[]{:S(2)}) collective-permute-start(bf16[768,384]{1,0:T(8,128)(2,1)S(1)} %pad_maximum_fusion.1.own), channel_id=1, source_target_pairs={{0,96},{1,97},{2,98},{3,99},{4,100},{5,101},{6,102},{7,103},{8,104... | collective-permute-start | bytes 1769480 | tf_op jit(solution)/shard_map/ppermute | solution.py:31
  8.6 2.8 %copy-done.10 = bf16[4,192,4096]{2,1,0:T(8,128)(2,1)S(1)} copy-done((bf16[4,192,4096]{2,1,0:T(8,128)(2,1)S(1)}, bf16[4,192,4096]{2,1,0:T(8,128)(2,1)}, u32[]{:S(2)}) %copy-start.10) | copy-done | bytes 6291480
  11.4 2.5 %shard_map.84 = (bf16[2,4,192,256]{3,2,1,0:T(8,128)(2,1)S(1)}, bf16[2,4,192,256]{3,2,1,0:T(8,128)(2,1)S(1)}, bf16[2,4,192,256]{3,2,1,0:T(8,128)(2,1)S(1)}, bf16[2,4,192,256]{3,2,1,0:T(8,128)(2,1)S(1)}) custom-call(s32[16]{0:T(128)S(1)} %stack.132.source, s32[4]{0:T(128)S(1)} %add_convert_fusion.included, bf16[192,4096]{1,0:T(8,128)(2,1)S(1)} %copy-done.11, ...), custom_call_target="tpu_custom_call" | custom-call | flops 3300000000 | bytes 1000 | tf_op jit(solution)/shard_map/pallas_call | solution.py:93
  13.9 1.4 collective-permute-start
  15.3 1.2 collective-permute-start.1
  16.5 1.8 %collective-permute-start.2 = (bf16[2,4,192,256]{3,2,1,0:T(8,128)(2,1)S(1)}, bf16[2,4,192,256]{3,2,1,0:T(8,128)(2,1)S(1)}, u32[]{:S(2)}, u32[]{:S(2)}) collective-permute-start(bf16[2,4,192,256]{3,2,1,0:T(8,128)(2,1)S(1)} %get-tuple-element.48), channel_id=1, source_target_pairs={{0,25},{1,24},{2,27},{3,26},{4,29},{5,28},{6,31},{7,30},{8,17},{9,... | collective-permute-start | bytes 2359304 | tf_op jit(solution)/shard_map/ppermute | solution.py:31
  18.3 3.1 %collective-permute-done.5.prev = bf16[768,384]{1,0:T(8,128)(2,1)S(1)} collective-permute-done((bf16[768,384]{1,0:T(8,128)(2,1)S(1)}, bf16[768,384]{1,0:T(8,128)(2,1)S(1)}, u32[]{:S(2)}, u32[]{:S(2)}) %collective-permute-start.5) | collective-permute-done | bytes 589856 | tf_op jit(solution)/shard_map/ppermute | solution.py:31
  21.6 2.7 %collective-permute-start.4 = (bf16[384,384]{1,0:T(8,128)(2,1)S(1)}, bf16[384,384]{1,0:T(8,128)(2,1)S(1)}, u32[]{:S(2)}, u32[]{:S(2)}) collective-permute-start(bf16[384,384]{1,0:T(8,128)(2,1)S(1)} %slice.72), channel_id=1, source_target_pairs={{0,96},{1,97},{2,98},{3,99},{4,100},{5,101},{6,102},{7,103},{8,104... | collective-permute-start | bytes 884744 | tf_op jit(solution)/shard_map/ppermute | solution.py:31
  24.3 7.8 %collective-permute-done.t1 = bf16[2,4,192,256]{3,2,1,0:T(8,128)(2,1)S(1)} collective-permute-done((bf16[2,4,192,256]{3,2,1,0:T(8,128)(2,1)S(1)}, bf16[2,4,192,256]{3,2,1,0:T(8,128)(2,1)S(1)}, u32[]{:S(2)}, u32[]{:S(2)}) %collective-permute-start) | collective-permute-done | bytes 786464 | tf_op jit(solution)/shard_map/ppermute | solution.py:31
  32.1 4.8 %collective-permute-done.2.t3 = bf16[2,4,192,256]{3,2,1,0:T(8,128)(2,1)S(1)} collective-permute-done((bf16[2,4,192,256]{3,2,1,0:T(8,128)(2,1)S(1)}, bf16[2,4,192,256]{3,2,1,0:T(8,128)(2,1)S(1)}, u32[]{:S(2)}, u32[]{:S(2)}) %collective-permute-start.2) | collective-permute-done | bytes 786464 | tf_op jit(solution)/shard_map/ppermute | solution.py:31
  36.9 2.7 %shard_map.85 = (f32[3,384,384]{2,1,0:T(8,128)S(1)}, f32[384,384]{1,0:T(8,128)S(1)}, f32[384,384]{1,0:T(8,128)S(1)}, f32[384,384]{1,0:T(8,128)S(1)}) custom-call(bf16[2,4,192,256]{3,2,1,0:T(8,128)(2,1)S(1)} %get-tuple-element.55.t0, bf16[2,4,192,256]{3,2,1,0:T(8,128)(2,1)S(1)} %collective-permute-done.t1, ...), custom_call_target="tpu_custom_call" | custom-call | flops 3300000000 | bytes 1000 | tf_op jit(solution)/shard_map/pallas_call | solution.py:63
  40.9 2.7 %collective-permute-start.11 = (bf16[768,512]{1,0:T(8,128)(2,1)S(1)}, bf16[768,512]{1,0:T(8,128)(2,1)S(1)}, u32[]{:S(2)}, u32[]{:S(2)}) collective-permute-start(bf16[768,512]{1,0:T(8,128)(2,1)S(1)} %pad_maximum_fusion.own), channel_id=1, source_target_pairs={{0,96},{1,97},{2,98},{3,99},{4,100},{5,101},{6,102},{7,103},{8,104... | collective-permute-start | bytes 2359304 | tf_op jit(solution)/shard_map/ppermute | solution.py:31
  44.0 1.5 collective-permute-start.16
  45.6 15.7 %collective-permute-done.13.prev = bf16[768,512]{1,0:T(8,128)(2,1)S(1)} collective-permute-done((bf16[768,512]{1,0:T(8,128)(2,1)S(1)}, bf16[768,512]{1,0:T(8,128)(2,1)S(1)}, u32[]{:S(2)}, u32[]{:S(2)}) %collective-permute-start.13) | collective-permute-done | bytes 786464 | tf_op jit(solution)/shard_map/ppermute | solution.py:31
  61.4 2.7 %collective-permute-start.12 = (bf16[384,512]{1,0:T(8,128)(2,1)S(1)}, bf16[384,512]{1,0:T(8,128)(2,1)S(1)}, u32[]{:S(2)}, u32[]{:S(2)}) collective-permute-start(bf16[384,512]{1,0:T(8,128)(2,1)S(1)} %slice.66), channel_id=1, source_target_pairs={{0,96},{1,97},{2,98},{3,99},{4,100},{5,101},{6,102},{7,103},{8,104... | collective-permute-start | bytes 1179656 | tf_op jit(solution)/shard_map/ppermute | solution.py:31
  65.5 1.5 collective-permute-start.20
  67.0 5.4 %collective-permute-done.14.high = bf16[384,512]{1,0:T(8,128)(2,1)S(1)} collective-permute-done((bf16[384,512]{1,0:T(8,128)(2,1)S(1)}, bf16[384,512]{1,0:T(8,128)(2,1)S(1)}, u32[]{:S(2)}, u32[]{:S(2)}) %collective-permute-start.14) | collective-permute-done | bytes 393248 | tf_op jit(solution)/shard_map/ppermute | solution.py:31
  72.4 2.6 %shard_map.87 = (f32[3,384,512]{2,1,0:T(8,128)S(1)}, f32[384,512]{1,0:T(8,128)S(1)}, f32[384,512]{1,0:T(8,128)S(1)}, f32[384,512]{1,0:T(8,128)S(1)}) custom-call(bf16[2,4,192,256]{3,2,1,0:T(8,128)(2,1)S(1)} %get-tuple-element.55.t0, bf16[2,4,192,256]{3,2,1,0:T(8,128)(2,1)S(1)} %collective-permute-done.t1, ...), custom_call_target="tpu_custom_call" | custom-call | flops 4400000000 | bytes 1000 | tf_op jit(solution)/shard_map/pallas_call | solution.py:63
  75.0 1.8 %collective-permute-start.15 = (f32[384,512]{1,0:T(8,128)S(1)}, f32[384,512]{1,0:T(8,128)S(1)}, u32[]{:S(2)}, u32[]{:S(2)}) collective-permute-start(f32[384,512]{1,0:T(8,128)S(1)} %get-tuple-element.60), channel_id=1, source_target_pairs={{0,8},{1,9},{2,10},{3,11},{4,12},{5,13},{6,14},{7,15},{8,0},{9,1},... | collective-permute-start | bytes 2359304 | tf_op jit(solution)/shard_map/ppermute | solution.py:31
  77.4 1.4 collective-permute-done.15
  78.8 2.7 %shard_map.89 = (f32[768,384]{1,0:T(8,128)S(1)}, f32[768,384]{1,0:T(8,128)S(1)}, bf16[384,384]{1,0:T(8,128)(2,1)}, bf16[384,384]{1,0:T(8,128)(2,1)}, f32[768,384]{1,0:T(8,128)S(1)}) custom-call(bf16[1024,768]{1,0:T(8,128)(2,1)S(1)} %get-tuple-element.53.tokens, bf16[1024,768]{1,0:T(8,128)(2,1)S(1)} %get-tuple-element.54.cotangents, ...), custom_call_target="tpu_custom_call" | custom-call | flops 3300000000 | bytes 1000 | tf_op jit(solution)/shard_map/pallas_call | solution.py:63
  82.1 2.2 %collective-permute-start.22 = (bf16[384,384]{1,0:T(8,128)(2,1)}, bf16[384,384]{1,0:T(8,128)(2,1)}, u32[]{:S(2)}, u32[]{:S(2)}) collective-permute-start(bf16[384,384]{1,0:T(8,128)(2,1)} %get-tuple-element.67), channel_id=1, source_target_pairs={{0,96},{1,97},{2,98},{3,99},{4,100},{5,101},{6,102},{7,103},{8,104... | collective-permute-start | bytes 884744 | tf_op jit(solution)/shard_map/ppermute | solution.py:31
  85.0 1.0 copy-done.42
  87.0 4.4 %collective-permute-done.21.low = bf16[384,384]{1,0:T(8,128)(2,1)} collective-permute-done((bf16[384,384]{1,0:T(8,128)(2,1)}, bf16[384,384]{1,0:T(8,128)(2,1)}, u32[]{:S(2)}, u32[]{:S(2)}) %collective-permute-start.21) | collective-permute-done | bytes 294944 | tf_op jit(solution)/shard_map/ppermute | solution.py:31
  91.3 1.3 copy-done.27
  92.6 1.3 copy-done.29
  93.9 1.4 shard_map.90
  96.0 2.1 %collective-permute-start.24 = (bf16[768,384]{1,0:T(8,128)(2,1)S(1)}, bf16[768,384]{1,0:T(8,128)(2,1)S(1)}, u32[]{:S(2)}, u32[]{:S(2)}) collective-permute-start(bf16[768,384]{1,0:T(8,128)(2,1)S(1)} %get-tuple-element.69), channel_id=1, source_target_pairs={{0,96},{1,97},{2,98},{3,99},{4,100},{5,101},{6,102},{7,103},{8,104... | collective-permute-start | bytes 1769480 | tf_op jit(solution)/shard_map/ppermute | solution.py:31
  98.0 1.0 slice_bitcast_fusion
  99.3 2.5 %shard_map.91.refs_0_ = f32[4,768,256]{2,1,0:T(8,128)S(1)} custom-call(s32[4]{0:T(128)S(1)} %pad_add_fusion.order, bf16[3,384,384]{2,1,0:T(8,128)(2,1)S(1)} %copy-done.13, bf16[3,384,384]{2,1,0:T(8,128)(2,1)S(1)} %copy-done.15, bf16[768,384]{1,0:T(8,128)(2,1)S(1)} %copy-done.1, bf16[768,384]{1,0:T(8,128)(2,1)S(1)} %copy-done.9, ...), custom_call_target="tpu_custom_call" | custom-call | flops 3300000000 | bytes 1000 | tf_op jit(solution)/shard_map/pallas_call | solution.py:63
  101.8 3.6 %collective-permute-done.19.other = bf16[2,384,512]{2,1,0:T(8,128)(2,1)} collective-permute-done((bf16[2,384,512]{2,1,0:T(8,128)(2,1)}, bf16[2,384,512]{2,1,0:T(8,128)(2,1)}, u32[]{:S(2)}, u32[]{:S(2)}) %collective-permute-start.19) | collective-permute-done | bytes 786464 | tf_op jit(solution)/shard_map/ppermute | solution.py:31
  105.4 4.7 %collective-permute-done.23.refs_1_ = bf16[768,384]{1,0:T(8,128)(2,1)S(1)} collective-permute-done((bf16[768,384]{1,0:T(8,128)(2,1)S(1)}, bf16[768,384]{1,0:T(8,128)(2,1)S(1)}, u32[]{:S(2)}, u32[]{:S(2)}) %collective-permute-start.23) | collective-permute-done | bytes 589856 | tf_op jit(solution)/shard_map/ppermute | solution.py:31
  111.8 2.0 %collective-permute-done.25.other_grad = bf16[384,512]{1,0:T(8,128)(2,1)S(1)} collective-permute-done((bf16[384,512]{1,0:T(8,128)(2,1)S(1)}, bf16[384,512]{1,0:T(8,128)(2,1)S(1)}, u32[]{:S(2)}, u32[]{:S(2)}) %collective-permute-start.25) | collective-permute-done | bytes 393248 | tf_op jit(solution)/shard_map/ppermute | solution.py:31
  113.8 1.9 %shard_map.92.mine = bf16[3,384,512]{2,1,0:T(8,128)(2,1)S(1)} custom-call(f32[3,384,512]{2,1,0:T(8,128)S(1)} %get-tuple-element.87.half, bf16[2,384,512]{2,1,0:T(8,128)(2,1)} %collective-permute-done.19.other, bf16[384,512]{1,0:T(8,128)(2,1)S(1)} %collective-permute-done.25.other_grad), custom_call_target="tpu_custom_call" | custom-call | flops 2200000000 | bytes 1000 | tf_op jit(solution)/shard_map/pallas_call | solution.py:63
  115.7 1.9 %collective-permute-start.26 = (bf16[3,384,512]{2,1,0:T(8,128)(2,1)S(1)}, bf16[3,384,512]{2,1,0:T(8,128)(2,1)S(1)}, u32[]{:S(2)}, u32[]{:S(2)}) collective-permute-start(bf16[3,384,512]{2,1,0:T(8,128)(2,1)S(1)} %shard_map.92.mine), channel_id=1, source_target_pairs={{0,8},{1,9},{2,10},{3,11},{4,12},{5,13},{6,14},{7,15},{8,0},{9,1},... | collective-permute-start | bytes 3538952 | tf_op jit(solution)/shard_map/ppermute | solution.py:31
  117.6 2.5 %collective-permute-done.26.theirs = bf16[3,384,512]{2,1,0:T(8,128)(2,1)S(1)} collective-permute-done((bf16[3,384,512]{2,1,0:T(8,128)(2,1)S(1)}, bf16[3,384,512]{2,1,0:T(8,128)(2,1)S(1)}, u32[]{:S(2)}, u32[]{:S(2)}) %collective-permute-start.26) | collective-permute-done | bytes 1179680 | tf_op jit(solution)/shard_map/ppermute | solution.py:31
  120.0 3.3 %shard_map.94 = (f32[768,512]{1,0:T(8,128)S(1)}, f32[768,512]{1,0:T(8,128)S(1)}, bf16[384,512]{1,0:T(8,128)(2,1)}, bf16[384,512]{1,0:T(8,128)(2,1)}, f32[768,512]{1,0:T(8,128)S(1)}) custom-call(bf16[1024,768]{1,0:T(8,128)(2,1)S(1)} %copy-done.39, bf16[1024,768]{1,0:T(8,128)(2,1)S(1)} %copy-done.41, bf16[3,384,512]{2,1,0:T(8,128)(2,1)S(1)} %shard_map.92.mine, ...), custom_call_target="tpu_custom_call" | custom-call | flops 4400000000 | bytes 1000 | tf_op jit(solution)/shard_map/pallas_call | solution.py:63
  123.3 1.2 copy-done.30
  124.5 1.2 copy-done.32
  125.7 1.2 copy-done.34
  126.9 2.7 %collective-permute-start.35 = (bf16[384,512]{1,0:T(8,128)(2,1)}, bf16[384,512]{1,0:T(8,128)(2,1)}, u32[]{:S(2)}, u32[]{:S(2)}) collective-permute-start(bf16[384,512]{1,0:T(8,128)(2,1)} %get-tuple-element.80), channel_id=1, source_target_pairs={{0,96},{1,97},{2,98},{3,99},{4,100},{5,101},{6,102},{7,103},{8,104... | collective-permute-start | bytes 1179656 | tf_op jit(solution)/shard_map/ppermute | solution.py:31
  129.6 3.3 %shard_map.93 = (f32[768,256]{1,0:T(8,128)S(1)}, bf16[768,256]{1,0:T(8,128)(2,1)}, bf16[768,256]{1,0:T(8,128)(2,1)}, bf16[768,256]{1,0:T(8,128)(2,1)}) custom-call(s32[4]{0:T(128)S(1)} %pad_add_fusion.order, bf16[3,384,512]{2,1,0:T(8,128)(2,1)S(1)} %shard_map.92.mine, bf16[3,384,512]{2,1,0:T(8,128)(2,1)S(1)} %collective-permute-done.26.theirs, ...), custom_call_target="tpu_custom_call" | custom-call | flops 4400000000 | bytes 1000 | tf_op jit(solution)/shard_map/pallas_call | solution.py:63
  132.9 1.2 collective-permute-start.27
  134.1 2.4 %collective-permute-start.28 = (bf16[768,256]{1,0:T(8,128)(2,1)}, bf16[768,256]{1,0:T(8,128)(2,1)}, u32[]{:S(2)}, u32[]{:S(2)}) collective-permute-start(bf16[768,256]{1,0:T(8,128)(2,1)} %get-tuple-element.73), channel_id=1, source_target_pairs={{0,4},{1,5},{2,6},{3,7},{4,0},{5,1},{6,2},{7,3},{8,12},{9,13},{10,... | collective-permute-start | bytes 1179656 | tf_op jit(solution)/shard_map/ppermute | solution.py:31
  136.6 1.2 collective-permute-start.29
  137.7 1.0 collective-permute-done.34.low
  138.8 1.4 copy-done.31
  140.2 1.4 copy-done.33
  141.6 2.2 %shard_map.95 = (bf16[768,512]{1,0:T(8,128)(2,1)}, bf16[768,512]{1,0:T(8,128)(2,1)S(1)}) custom-call(f32[768,512]{1,0:T(8,128)S(1)} %copy-done.31, f32[768,512]{1,0:T(8,128)S(1)} %copy-done.33, bf16[384,512]{1,0:T(8,128)(2,1)} %collective-permute-done.34.low, bf16[384,512]{1,0:T(8,128)(2,1)} %collective-permute-done.35.high), custom_call_target="tpu_custom_call" | custom-call | flops 1408000000 | bytes 1000 | tf_op jit(solution)/shard_map/pallas_call | solution.py:63
  143.8 2.7 %collective-permute-start.37 = (bf16[768,512]{1,0:T(8,128)(2,1)S(1)}, bf16[768,512]{1,0:T(8,128)(2,1)S(1)}, u32[]{:S(2)}, u32[]{:S(2)}) collective-permute-start(bf16[768,512]{1,0:T(8,128)(2,1)S(1)} %get-tuple-element.82), channel_id=1, source_target_pairs={{0,96},{1,97},{2,98},{3,99},{4,100},{5,101},{6,102},{7,103},{8,104... | collective-permute-start | bytes 2359304 | tf_op jit(solution)/shard_map/ppermute | solution.py:31
  146.5 7.1 %collective-permute-done.28 = bf16[768,256]{1,0:T(8,128)(2,1)} collective-permute-done((bf16[768,256]{1,0:T(8,128)(2,1)}, bf16[768,256]{1,0:T(8,128)(2,1)}, u32[]{:S(2)}, u32[]{:S(2)}) %collective-permute-start.28) | collective-permute-done | bytes 393248 | tf_op jit(solution)/shard_map/ppermute | solution.py:31
  153.6 1.3 convert_add_fusion
  155.0 1.8 %collective-permute-start.33 = (f32[192,256]{1,0:T(8,128)S(1)}, f32[192,256]{1,0:T(8,128)}, u32[]{:S(2)}, u32[]{:S(2)}) collective-permute-start(f32[192,256]{1,0:T(8,128)S(1)} %get-tuple-element.94), channel_id=1, source_target_pairs={{0,24},{1,8},{2,26},{3,10},{4,28},{5,12},{6,30},{7,14},{8,16},{9,0... | collective-permute-start | bytes 589832 | tf_op jit(solution)/shard_map/ppermute | solution.py:31
  157.7 2.3 %collective-permute-start.31 = (f32[192,256]{1,0:T(8,128)}, f32[192,256]{1,0:T(8,128)S(1)}, u32[]{:S(2)}, u32[]{:S(2)}) collective-permute-start(f32[192,256]{1,0:T(8,128)} %get-tuple-element.92), channel_id=1, source_target_pairs={{0,16},{1,0},{2,18},{3,2},{4,20},{5,4},{6,22},{7,6},{8,24},{9,8},{... | collective-permute-start | bytes 589832 | tf_op jit(solution)/shard_map/ppermute | solution.py:31
  160.0 3.1 %collective-permute-done.33 = f32[192,256]{1,0:T(8,128)} collective-permute-done((f32[192,256]{1,0:T(8,128)S(1)}, f32[192,256]{1,0:T(8,128)}, u32[]{:S(2)}, u32[]{:S(2)}) %collective-permute-start.33) | collective-permute-done | bytes 196640 | tf_op jit(solution)/shard_map/ppermute | solution.py:31
  163.2 3.0 %collective-permute-start.30 = (f32[192,256]{1,0:T(8,128)}, f32[192,256]{1,0:T(8,128)}, u32[]{:S(2)}, u32[]{:S(2)}) collective-permute-start(f32[192,256]{1,0:T(8,128)} %get-tuple-element.93), channel_id=1, source_target_pairs={{0,0},{1,16},{2,2},{3,18},{4,4},{5,20},{6,6},{7,22},{8,8},{9,24},{... | collective-permute-start | bytes 589832 | tf_op jit(solution)/shard_map/ppermute | solution.py:31
  166.1 1.2 add.272
  168.8 1.0 add.271
  170.6 1.1 copy-done.19
  171.7 1.3 copy-done.37
  173.0 1.8 %shard_map.96 = (f32[256,896]{1,0:T(8,128)}, f32[256,896]{1,0:T(8,128)}, f32[256,896]{1,0:T(8,128)}) custom-call(f32[768,384]{1,0:T(8,128)S(1)} %copy-done.37, bf16[768,384]{1,0:T(8,128)(2,1)S(1)} %copy-done.17, bf16[768,384]{1,0:T(8,128)(2,1)S(1)} %copy-done.19, f32[768,512]{1,0:T(8,128)S(1)} %copy-done.35, ...), custom_call_target="tpu_custom_call" | custom-call | flops 2200000000 | bytes 1000 | tf_op jit(solution)/shard_map/pallas_call | solution.py:63
  (144 shorter events, 13.1 us)
Async XLA Ops:
  0.6 8.0 %copy-start.11 = (bf16[192,4096]{1,0:T(8,128)(2,1)S(1)}, bf16[192,4096]{1,0:T(8,128)(2,1)}, u32[]{:S(2)}) copy-start(bf16[192,4096]{1,0:T(8,128)(2,1)} %x.1) | copy-start | bytes 4718596
  3.7 33.2 %copy-start = (bf16[768,384]{1,0:T(8,128)(2,1)}, bf16[768,384]{1,0:T(8,128)(2,1)S(1)}, u32[]{:S(2)}) copy-start(bf16[768,384]{1,0:T(8,128)(2,1)S(1)} %pad_maximum_fusion.1.own) | copy-start | bytes 1769476
  3.7 17.7 %collective-permute-start.5 = (bf16[768,384]{1,0:T(8,128)(2,1)S(1)}, bf16[768,384]{1,0:T(8,128)(2,1)S(1)}, u32[]{:S(2)}, u32[]{:S(2)}) collective-permute-start(bf16[768,384]{1,0:T(8,128)(2,1)S(1)} %pad_maximum_fusion.1.own), channel_id=1, source_target_pairs={{0,32},{1,33},{2,34},{3,35},{4,36},{5,37},{6,38},{7,39},{8,40},{9,... | collective-permute-start | bytes 1769480 | tf_op jit(solution)/shard_map/ppermute | solution.py:31
  6.2 15.3 %collective-permute-start.3 = (bf16[768,384]{1,0:T(8,128)(2,1)S(1)}, bf16[768,384]{1,0:T(8,128)(2,1)S(1)}, u32[]{:S(2)}, u32[]{:S(2)}) collective-permute-start(bf16[768,384]{1,0:T(8,128)(2,1)S(1)} %pad_maximum_fusion.1.own), channel_id=1, source_target_pairs={{0,96},{1,97},{2,98},{3,99},{4,100},{5,101},{6,102},{7,103},{8,104... | collective-permute-start | bytes 1769480 | tf_op jit(solution)/shard_map/ppermute | solution.py:31
  13.9 18.2 %collective-permute-start = (bf16[2,4,192,256]{3,2,1,0:T(8,128)(2,1)S(1)}, bf16[2,4,192,256]{3,2,1,0:T(8,128)(2,1)S(1)}, u32[]{:S(2)}, u32[]{:S(2)}) collective-permute-start(bf16[2,4,192,256]{3,2,1,0:T(8,128)(2,1)S(1)} %get-tuple-element.46), channel_id=1, source_target_pairs={{0,16},{1,17},{2,18},{3,19},{4,20},{5,21},{6,22},{7,23},{8,24},{9,... | collective-permute-start | bytes 2359304 | tf_op jit(solution)/shard_map/ppermute | solution.py:31
  15.3 16.8 %collective-permute-start.1 = (bf16[2,4,192,256]{3,2,1,0:T(8,128)(2,1)S(1)}, bf16[2,4,192,256]{3,2,1,0:T(8,128)(2,1)S(1)}, u32[]{:S(2)}, u32[]{:S(2)}) collective-permute-start(bf16[2,4,192,256]{3,2,1,0:T(8,128)(2,1)S(1)} %get-tuple-element.47), channel_id=1, source_target_pairs={{0,8},{1,9},{2,10},{3,11},{4,12},{5,13},{6,14},{7,15},{8,0},{9,1},... | collective-permute-start | bytes 2359304 | tf_op jit(solution)/shard_map/ppermute | solution.py:31
  16.5 20.4 %collective-permute-start.2 = (bf16[2,4,192,256]{3,2,1,0:T(8,128)(2,1)S(1)}, bf16[2,4,192,256]{3,2,1,0:T(8,128)(2,1)S(1)}, u32[]{:S(2)}, u32[]{:S(2)}) collective-permute-start(bf16[2,4,192,256]{3,2,1,0:T(8,128)(2,1)S(1)} %get-tuple-element.48), channel_id=1, source_target_pairs={{0,25},{1,24},{2,27},{3,26},{4,29},{5,28},{6,31},{7,30},{8,17},{9,... | collective-permute-start | bytes 2359304 | tf_op jit(solution)/shard_map/ppermute | solution.py:31
  21.4 18.2 %copy-start.6 = (bf16[768,384]{1,0:T(8,128)(2,1)}, bf16[768,384]{1,0:T(8,128)(2,1)S(1)}, u32[]{:S(2)}) copy-start(bf16[768,384]{1,0:T(8,128)(2,1)S(1)} %collective-permute-done.5.prev) | copy-start | bytes 1769476
  21.4 15.4 %collective-permute-start.6 = (bf16[384,384]{1,0:T(8,128)(2,1)S(1)}, bf16[384,384]{1,0:T(8,128)(2,1)S(1)}, u32[]{:S(2)}, u32[]{:S(2)}) collective-permute-start(bf16[384,384]{1,0:T(8,128)(2,1)S(1)} %slice.73), channel_id=1, source_target_pairs={{0,32},{1,33},{2,34},{3,35},{4,36},{5,37},{6,38},{7,39},{8,40},{9,... | collective-permute-start | bytes 884744 | tf_op jit(solution)/shard_map/ppermute | solution.py:31
  21.5 18.1 %copy-start.8 = (bf16[768,384]{1,0:T(8,128)(2,1)}, bf16[768,384]{1,0:T(8,128)(2,1)S(1)}, u32[]{:S(2)}) copy-start(bf16[768,384]{1,0:T(8,128)(2,1)S(1)} %collective-permute-done.3.nxt) | copy-start | bytes 1769476
  21.6 15.3 %collective-permute-start.4 = (bf16[384,384]{1,0:T(8,128)(2,1)S(1)}, bf16[384,384]{1,0:T(8,128)(2,1)S(1)}, u32[]{:S(2)}, u32[]{:S(2)}) collective-permute-start(bf16[384,384]{1,0:T(8,128)(2,1)S(1)} %slice.72), channel_id=1, source_target_pairs={{0,96},{1,97},{2,98},{3,99},{4,100},{5,101},{6,102},{7,103},{8,104... | collective-permute-start | bytes 884744 | tf_op jit(solution)/shard_map/ppermute | solution.py:31
  39.7 3.9 %collective-permute-start.7 = (f32[384,384]{1,0:T(8,128)S(1)}, f32[384,384]{1,0:T(8,128)S(1)}, u32[]{:S(2)}, u32[]{:S(2)}) collective-permute-start(f32[384,384]{1,0:T(8,128)S(1)} %get-tuple-element.50), channel_id=1, source_target_pairs={{0,8},{1,9},{2,10},{3,11},{4,12},{5,13},{6,14},{7,15},{8,0},{9,1},... | collective-permute-start | bytes 1769480 | tf_op jit(solution)/shard_map/ppermute | solution.py:31
  39.8 3.8 %collective-permute-start.8 = (f32[384,384]{1,0:T(8,128)S(1)}, f32[384,384]{1,0:T(8,128)S(1)}, u32[]{:S(2)}, u32[]{:S(2)}) collective-permute-start(f32[384,384]{1,0:T(8,128)S(1)} %get-tuple-element.51), channel_id=1, source_target_pairs={{0,8},{1,9},{2,10},{3,11},{4,12},{5,13},{6,14},{7,15},{8,0},{9,1},... | collective-permute-start | bytes 1769480 | tf_op jit(solution)/shard_map/ppermute | solution.py:31
  40.3 3.3 %collective-permute-start.9 = (f32[384,384]{1,0:T(8,128)S(1)}, f32[384,384]{1,0:T(8,128)S(1)}, u32[]{:S(2)}, u32[]{:S(2)}) collective-permute-start(f32[384,384]{1,0:T(8,128)S(1)} %get-tuple-element.52), channel_id=1, source_target_pairs={{0,8},{1,9},{2,10},{3,11},{4,12},{5,13},{6,14},{7,15},{8,0},{9,1},... | collective-permute-start | bytes 1769480 | tf_op jit(solution)/shard_map/ppermute | solution.py:31
  40.8 20.4 %collective-permute-start.13 = (bf16[768,512]{1,0:T(8,128)(2,1)S(1)}, bf16[768,512]{1,0:T(8,128)(2,1)S(1)}, u32[]{:S(2)}, u32[]{:S(2)}) collective-permute-start(bf16[768,512]{1,0:T(8,128)(2,1)S(1)} %pad_maximum_fusion.own), channel_id=1, source_target_pairs={{0,32},{1,33},{2,34},{3,35},{4,36},{5,37},{6,38},{7,39},{8,40},{9,... | collective-permute-start | bytes 2359304 | tf_op jit(solution)/shard_map/ppermute | solution.py:31
  40.9 20.3 %collective-permute-start.11 = (bf16[768,512]{1,0:T(8,128)(2,1)S(1)}, bf16[768,512]{1,0:T(8,128)(2,1)S(1)}, u32[]{:S(2)}, u32[]{:S(2)}) collective-permute-start(bf16[768,512]{1,0:T(8,128)(2,1)S(1)} %pad_maximum_fusion.own), channel_id=1, source_target_pairs={{0,96},{1,97},{2,98},{3,99},{4,100},{5,101},{6,102},{7,103},{8,104... | collective-permute-start | bytes 2359304 | tf_op jit(solution)/shard_map/ppermute | solution.py:31
  43.9 21.0 %collective-permute-start.10 = (bf16[2,384,384]{2,1,0:T(8,128)(2,1)S(1)}, bf16[2,384,384]{2,1,0:T(8,128)(2,1)S(1)}, u32[]{:S(2)}, u32[]{:S(2)}) collective-permute-start(bf16[2,384,384]{2,1,0:T(8,128)(2,1)S(1)} %slice.74), channel_id=1, source_target_pairs={{0,16},{1,17},{2,18},{3,19},{4,20},{5,21},{6,22},{7,23},{8,24},{9,... | collective-permute-start | bytes 1769480 | tf_op jit(solution)/shard_map/ppermute | solution.py:31
  44.0 20.9 %collective-permute-start.16 = (bf16[384,384]{1,0:T(8,128)(2,1)S(1)}, bf16[384,384]{1,0:T(8,128)(2,1)S(1)}, u32[]{:S(2)}, u32[]{:S(2)}) collective-permute-start(bf16[384,384]{1,0:T(8,128)(2,1)S(1)} %slice_bitcast_fusion.1), channel_id=1, source_target_pairs={{0,16},{1,17},{2,18},{3,19},{4,20},{5,21},{6,22},{7,23},{8,24},{9,... | collective-permute-start | bytes 884744 | tf_op jit(solution)/shard_map/ppermute | solution.py:31
  61.2 11.2 %copy-start.2 = (bf16[768,512]{1,0:T(8,128)(2,1)}, bf16[768,512]{1,0:T(8,128)(2,1)S(1)}, u32[]{:S(2)}) copy-start(bf16[768,512]{1,0:T(8,128)(2,1)S(1)} %collective-permute-done.13.prev) | copy-start | bytes 2359300
  61.2 11.2 %copy-start.4 = (bf16[768,512]{1,0:T(8,128)(2,1)}, bf16[768,512]{1,0:T(8,128)(2,1)S(1)}, u32[]{:S(2)}) copy-start(bf16[768,512]{1,0:T(8,128)(2,1)S(1)} %collective-permute-done.11.nxt) | copy-start | bytes 2359300
  61.3 11.1 %collective-permute-start.14 = (bf16[384,512]{1,0:T(8,128)(2,1)S(1)}, bf16[384,512]{1,0:T(8,128)(2,1)S(1)}, u32[]{:S(2)}, u32[]{:S(2)}) collective-permute-start(bf16[384,512]{1,0:T(8,128)(2,1)S(1)} %slice.67), channel_id=1, source_target_pairs={{0,32},{1,33},{2,34},{3,35},{4,36},{5,37},{6,38},{7,39},{8,40},{9,... | collective-permute-start | bytes 1179656 | tf_op jit(solution)/shard_map/ppermute | solution.py:31
  61.4 11.0 %collective-permute-start.12 = (bf16[384,512]{1,0:T(8,128)(2,1)S(1)}, bf16[384,512]{1,0:T(8,128)(2,1)S(1)}, u32[]{:S(2)}, u32[]{:S(2)}) collective-permute-start(bf16[384,512]{1,0:T(8,128)(2,1)S(1)} %slice.66), channel_id=1, source_target_pairs={{0,96},{1,97},{2,98},{3,99},{4,100},{5,101},{6,102},{7,103},{8,104... | collective-permute-start | bytes 1179656 | tf_op jit(solution)/shard_map/ppermute | solution.py:31
  64.9 13.8 %copy-start.38 = (bf16[1024,768]{1,0:T(8,128)(2,1)}, bf16[1024,768]{1,0:T(8,128)(2,1)S(1)}, u32[]{:S(2)}) copy-start(bf16[1024,768]{1,0:T(8,128)(2,1)S(1)} %get-tuple-element.53.tokens) | copy-start | bytes 4718596
  64.9 13.8 %copy-start.40 = (bf16[1024,768]{1,0:T(8,128)(2,1)}, bf16[1024,768]{1,0:T(8,128)(2,1)S(1)}, u32[]{:S(2)}) copy-start(bf16[1024,768]{1,0:T(8,128)(2,1)S(1)} %get-tuple-element.54.cotangents) | copy-start | bytes 4718596
  65.5 13.3 %copy-start.12 = (bf16[3,384,384]{2,1,0:T(8,128)(2,1)}, bf16[3,384,384]{2,1,0:T(8,128)(2,1)S(1)}, u32[]{:S(2)}) copy-start(bf16[3,384,384]{2,1,0:T(8,128)(2,1)S(1)} %shard_map.88.mine) | copy-start | bytes 2654212
  65.5 13.2 %collective-permute-start.20 = (bf16[3,384,384]{2,1,0:T(8,128)(2,1)S(1)}, bf16[3,384,384]{2,1,0:T(8,128)(2,1)S(1)}, u32[]{:S(2)}, u32[]{:S(2)}) collective-permute-start(bf16[3,384,384]{2,1,0:T(8,128)(2,1)S(1)} %shard_map.88.mine), channel_id=1, source_target_pairs={{0,8},{1,9},{2,10},{3,11},{4,12},{5,13},{6,14},{7,15},{8,0},{9,1},... | collective-permute-start | bytes 2654216 | tf_op jit(solution)/shard_map/ppermute | solution.py:31
  75.0 3.7 %collective-permute-start.15 = (f32[384,512]{1,0:T(8,128)S(1)}, f32[384,512]{1,0:T(8,128)S(1)}, u32[]{:S(2)}, u32[]{:S(2)}) collective-permute-start(f32[384,512]{1,0:T(8,128)S(1)} %get-tuple-element.60), channel_id=1, source_target_pairs={{0,8},{1,9},{2,10},{3,11},{4,12},{5,13},{6,14},{7,15},{8,0},{9,1},... | collective-permute-start | bytes 2359304 | tf_op jit(solution)/shard_map/ppermute | solution.py:31
  76.8 7.5 %collective-permute-start.17 = (f32[384,512]{1,0:T(8,128)S(1)}, f32[384,512]{1,0:T(8,128)S(1)}, u32[]{:S(2)}, u32[]{:S(2)}) collective-permute-start(f32[384,512]{1,0:T(8,128)S(1)} %get-tuple-element.62), channel_id=1, source_target_pairs={{0,8},{1,9},{2,10},{3,11},{4,12},{5,13},{6,14},{7,15},{8,0},{9,1},... | collective-permute-start | bytes 2359304 | tf_op jit(solution)/shard_map/ppermute | solution.py:31
  76.9 7.4 %collective-permute-start.18 = (f32[384,512]{1,0:T(8,128)S(1)}, f32[384,512]{1,0:T(8,128)S(1)}, u32[]{:S(2)}, u32[]{:S(2)}) collective-permute-start(f32[384,512]{1,0:T(8,128)S(1)} %get-tuple-element.63), channel_id=1, source_target_pairs={{0,8},{1,9},{2,10},{3,11},{4,12},{5,13},{6,14},{7,15},{8,0},{9,1},... | collective-permute-start | bytes 2359304 | tf_op jit(solution)/shard_map/ppermute | solution.py:31
  81.5 3.4 %copy-start.26 = (f32[768,384]{1,0:T(8,128)}, f32[768,384]{1,0:T(8,128)S(1)}, u32[]{:S(2)}) copy-start(f32[768,384]{1,0:T(8,128)S(1)} %get-tuple-element.64.b1) | copy-start | bytes 3538948
  81.5 3.5 %copy-start.28 = (f32[768,384]{1,0:T(8,128)}, f32[768,384]{1,0:T(8,128)S(1)}, u32[]{:S(2)}) copy-start(f32[768,384]{1,0:T(8,128)S(1)} %get-tuple-element.65.b3) | copy-start | bytes 3538948
  81.5 3.5 %copy-start.36 = (f32[768,384]{1,0:T(8,128)}, f32[768,384]{1,0:T(8,128)S(1)}, u32[]{:S(2)}) copy-start(f32[768,384]{1,0:T(8,128)S(1)} %get-tuple-element.75.refs_0_) | copy-start | bytes 3538948
  81.5 9.8 %collective-permute-start.21 = (bf16[384,384]{1,0:T(8,128)(2,1)}, bf16[384,384]{1,0:T(8,128)(2,1)}, u32[]{:S(2)}, u32[]{:S(2)}) collective-permute-start(bf16[384,384]{1,0:T(8,128)(2,1)} %get-tuple-element.66), channel_id=1, source_target_pairs={{0,32},{1,33},{2,34},{3,35},{4,36},{5,37},{6,38},{7,39},{8,40},{9,... | collective-permute-start | bytes 884744 | tf_op jit(solution)/shard_map/ppermute | solution.py:31
  82.1 9.2 %collective-permute-start.22 = (bf16[384,384]{1,0:T(8,128)(2,1)}, bf16[384,384]{1,0:T(8,128)(2,1)}, u32[]{:S(2)}, u32[]{:S(2)}) collective-permute-start(bf16[384,384]{1,0:T(8,128)(2,1)} %get-tuple-element.67), channel_id=1, source_target_pairs={{0,96},{1,97},{2,98},{3,99},{4,100},{5,101},{6,102},{7,103},{8,104... | collective-permute-start | bytes 884744 | tf_op jit(solution)/shard_map/ppermute | solution.py:31
  87.0 18.5 %collective-permute-start.19 = (bf16[2,384,512]{2,1,0:T(8,128)(2,1)}, bf16[2,384,512]{2,1,0:T(8,128)(2,1)}, u32[]{:S(2)}, u32[]{:S(2)}) collective-permute-start(bf16[2,384,512]{2,1,0:T(8,128)(2,1)} %slice.76), channel_id=1, source_target_pairs={{0,16},{1,17},{2,18},{3,19},{4,20},{5,21},{6,22},{7,23},{8,24},{9,... | collective-permute-start | bytes 2359304 | tf_op jit(solution)/shard_map/ppermute | solution.py:31
  93.9 5.4 %copy-start.1 = (bf16[768,384]{1,0:T(8,128)(2,1)S(1)}, bf16[768,384]{1,0:T(8,128)(2,1)}, u32[]{:S(2)}) copy-start(bf16[768,384]{1,0:T(8,128)(2,1)} %copy-done) | copy-start | bytes 1769476
  93.9 5.4 %copy-start.7 = (bf16[768,384]{1,0:T(8,128)(2,1)S(1)}, bf16[768,384]{1,0:T(8,128)(2,1)}, u32[]{:S(2)}) copy-start(bf16[768,384]{1,0:T(8,128)(2,1)} %copy-done.6) | copy-start | bytes 1769476
  93.9 5.4 %copy-start.9 = (bf16[768,384]{1,0:T(8,128)(2,1)S(1)}, bf16[768,384]{1,0:T(8,128)(2,1)}, u32[]{:S(2)}) copy-start(bf16[768,384]{1,0:T(8,128)(2,1)} %copy-done.8) | copy-start | bytes 1769476
  93.9 5.4 %copy-start.13 = (bf16[3,384,384]{2,1,0:T(8,128)(2,1)S(1)}, bf16[3,384,384]{2,1,0:T(8,128)(2,1)}, u32[]{:S(2)}) copy-start(bf16[3,384,384]{2,1,0:T(8,128)(2,1)} %copy-done.12) | copy-start | bytes 2654212
  93.9 5.4 %copy-start.15 = (bf16[3,384,384]{2,1,0:T(8,128)(2,1)S(1)}, bf16[3,384,384]{2,1,0:T(8,128)(2,1)}, u32[]{:S(2)}) copy-start(bf16[3,384,384]{2,1,0:T(8,128)(2,1)} %copy-done.14) | copy-start | bytes 2654212
  93.9 5.4 %copy-start.23 = (bf16[384,384]{1,0:T(8,128)(2,1)S(1)}, bf16[384,384]{1,0:T(8,128)(2,1)}, u32[]{:S(2)}) copy-start(bf16[384,384]{1,0:T(8,128)(2,1)} %copy-done.22) | copy-start | bytes 884740
  93.9 5.4 %copy-start.25 = (bf16[384,384]{1,0:T(8,128)(2,1)S(1)}, bf16[384,384]{1,0:T(8,128)(2,1)}, u32[]{:S(2)}) copy-start(bf16[384,384]{1,0:T(8,128)(2,1)} %copy-done.24) | copy-start | bytes 884740
  95.3 14.9 %collective-permute-start.23 = (bf16[768,384]{1,0:T(8,128)(2,1)S(1)}, bf16[768,384]{1,0:T(8,128)(2,1)S(1)}, u32[]{:S(2)}, u32[]{:S(2)}) collective-permute-start(bf16[768,384]{1,0:T(8,128)(2,1)S(1)} %get-tuple-element.68), channel_id=1, source_target_pairs={{0,32},{1,33},{2,34},{3,35},{4,36},{5,37},{6,38},{7,39},{8,40},{9,... | collective-permute-start | bytes 1769480 | tf_op jit(solution)/shard_map/ppermute | solution.py:31
  96.0 15.0 %collective-permute-start.24 = (bf16[768,384]{1,0:T(8,128)(2,1)S(1)}, bf16[768,384]{1,0:T(8,128)(2,1)S(1)}, u32[]{:S(2)}, u32[]{:S(2)}) collective-permute-start(bf16[768,384]{1,0:T(8,128)(2,1)S(1)} %get-tuple-element.69), channel_id=1, source_target_pairs={{0,96},{1,97},{2,98},{3,99},{4,100},{5,101},{6,102},{7,103},{8,104... | collective-permute-start | bytes 1769480 | tf_op jit(solution)/shard_map/ppermute | solution.py:31
  99.1 14.7 %collective-permute-start.25 = (bf16[384,512]{1,0:T(8,128)(2,1)S(1)}, bf16[384,512]{1,0:T(8,128)(2,1)S(1)}, u32[]{:S(2)}, u32[]{:S(2)}) collective-permute-start(bf16[384,512]{1,0:T(8,128)(2,1)S(1)} %slice_bitcast_fusion), channel_id=1, source_target_pairs={{0,16},{1,17},{2,18},{3,19},{4,20},{5,21},{6,22},{7,23},{8,24},{9,... | collective-permute-start | bytes 1179656 | tf_op jit(solution)/shard_map/ppermute | solution.py:31
  113.8 6.3 %copy-start.39 = (bf16[1024,768]{1,0:T(8,128)(2,1)S(1)}, bf16[1024,768]{1,0:T(8,128)(2,1)}, u32[]{:S(2)}) copy-start(bf16[1024,768]{1,0:T(8,128)(2,1)} %copy-done.38) | copy-start | bytes 4718596
  113.8 6.3 %copy-start.41 = (bf16[1024,768]{1,0:T(8,128)(2,1)S(1)}, bf16[1024,768]{1,0:T(8,128)(2,1)}, u32[]{:S(2)}) copy-start(bf16[1024,768]{1,0:T(8,128)(2,1)} %copy-done.40) | copy-start | bytes 4718596
  115.7 13.9 %copy-start.3 = (bf16[768,512]{1,0:T(8,128)(2,1)S(1)}, bf16[768,512]{1,0:T(8,128)(2,1)}, u32[]{:S(2)}) copy-start(bf16[768,512]{1,0:T(8,128)(2,1)} %copy-done.2) | copy-start | bytes 2359300
  115.7 13.9 %copy-start.5 = (bf16[768,512]{1,0:T(8,128)(2,1)S(1)}, bf16[768,512]{1,0:T(8,128)(2,1)}, u32[]{:S(2)}) copy-start(bf16[768,512]{1,0:T(8,128)(2,1)} %copy-done.4) | copy-start | bytes 2359300
  115.7 13.9 %copy-start.21 = (bf16[384,512]{1,0:T(8,128)(2,1)S(1)}, bf16[384,512]{1,0:T(8,128)(2,1)}, u32[]{:S(2)}) copy-start(bf16[384,512]{1,0:T(8,128)(2,1)} %copy-done.20) | copy-start | bytes 1179652
  115.7 4.3 %collective-permute-start.26 = (bf16[3,384,512]{2,1,0:T(8,128)(2,1)S(1)}, bf16[3,384,512]{2,1,0:T(8,128)(2,1)S(1)}, u32[]{:S(2)}, u32[]{:S(2)}) collective-permute-start(bf16[3,384,512]{2,1,0:T(8,128)(2,1)S(1)} %shard_map.92.mine), channel_id=1, source_target_pairs={{0,8},{1,9},{2,10},{3,11},{4,12},{5,13},{6,14},{7,15},{8,0},{9,1},... | collective-permute-start | bytes 3538952 | tf_op jit(solution)/shard_map/ppermute | solution.py:31
  126.9 11.9 %collective-permute-start.34 = (bf16[384,512]{1,0:T(8,128)(2,1)}, bf16[384,512]{1,0:T(8,128)(2,1)}, u32[]{:S(2)}, u32[]{:S(2)}) collective-permute-start(bf16[384,512]{1,0:T(8,128)(2,1)} %get-tuple-element.79), channel_id=1, source_target_pairs={{0,32},{1,33},{2,34},{3,35},{4,36},{5,37},{6,38},{7,39},{8,40},{9,... | collective-permute-start | bytes 1179656 | tf_op jit(solution)/shard_map/ppermute | solution.py:31
  126.9 11.9 %collective-permute-start.35 = (bf16[384,512]{1,0:T(8,128)(2,1)}, bf16[384,512]{1,0:T(8,128)(2,1)}, u32[]{:S(2)}, u32[]{:S(2)}) collective-permute-start(bf16[384,512]{1,0:T(8,128)(2,1)} %get-tuple-element.80), channel_id=1, source_target_pairs={{0,96},{1,97},{2,98},{3,99},{4,100},{5,101},{6,102},{7,103},{8,104... | collective-permute-start | bytes 1179656 | tf_op jit(solution)/shard_map/ppermute | solution.py:31
  132.9 13.5 %collective-permute-start.27 = (bf16[768,256]{1,0:T(8,128)(2,1)}, bf16[768,256]{1,0:T(8,128)(2,1)S(1)}, u32[]{:S(2)}, u32[]{:S(2)}) collective-permute-start(bf16[768,256]{1,0:T(8,128)(2,1)} %get-tuple-element.72), channel_id=1, source_target_pairs={{0,2},{1,3},{2,4},{3,5},{4,6},{5,7},{6,0},{7,1},{8,10},{9,11},{10,... | collective-permute-start | bytes 1179656 | tf_op jit(solution)/shard_map/ppermute | solution.py:31
  134.1 19.4 %collective-permute-start.28 = (bf16[768,256]{1,0:T(8,128)(2,1)}, bf16[768,256]{1,0:T(8,128)(2,1)}, u32[]{:S(2)}, u32[]{:S(2)}) collective-permute-start(bf16[768,256]{1,0:T(8,128)(2,1)} %get-tuple-element.73), channel_id=1, source_target_pairs={{0,4},{1,5},{2,6},{3,7},{4,0},{5,1},{6,2},{7,3},{8,12},{9,13},{10,... | collective-permute-start | bytes 1179656 | tf_op jit(solution)/shard_map/ppermute | solution.py:31
  136.6 17.0 %collective-permute-start.29 = (bf16[768,256]{1,0:T(8,128)(2,1)}, bf16[768,256]{1,0:T(8,128)(2,1)}, u32[]{:S(2)}, u32[]{:S(2)}) collective-permute-start(bf16[768,256]{1,0:T(8,128)(2,1)} %get-tuple-element.74), channel_id=1, source_target_pairs={{0,6},{1,7},{2,0},{3,1},{4,2},{5,3},{6,4},{7,5},{8,14},{9,15},{10,... | collective-permute-start | bytes 1179656 | tf_op jit(solution)/shard_map/ppermute | solution.py:31
  143.8 26.8 %collective-permute-start.36 = (bf16[768,512]{1,0:T(8,128)(2,1)}, bf16[768,512]{1,0:T(8,128)(2,1)S(1)}, u32[]{:S(2)}, u32[]{:S(2)}) collective-permute-start(bf16[768,512]{1,0:T(8,128)(2,1)} %get-tuple-element.81), channel_id=1, source_target_pairs={{0,32},{1,33},{2,34},{3,35},{4,36},{5,37},{6,38},{7,39},{8,40},{9,... | collective-permute-start | bytes 2359304 | tf_op jit(solution)/shard_map/ppermute | solution.py:31
  143.8 26.8 %collective-permute-start.37 = (bf16[768,512]{1,0:T(8,128)(2,1)S(1)}, bf16[768,512]{1,0:T(8,128)(2,1)S(1)}, u32[]{:S(2)}, u32[]{:S(2)}) collective-permute-start(bf16[768,512]{1,0:T(8,128)(2,1)S(1)} %get-tuple-element.82), channel_id=1, source_target_pairs={{0,96},{1,97},{2,98},{3,99},{4,100},{5,101},{6,102},{7,103},{8,104... | collective-permute-start | bytes 2359304 | tf_op jit(solution)/shard_map/ppermute | solution.py:31
  154.9 15.7 %copy-start.17 = (bf16[768,384]{1,0:T(8,128)(2,1)S(1)}, bf16[768,384]{1,0:T(8,128)(2,1)}, u32[]{:S(2)}) copy-start(bf16[768,384]{1,0:T(8,128)(2,1)} %copy-done.16) | copy-start | bytes 1769476
  155.0 8.2 %collective-permute-start.33 = (f32[192,256]{1,0:T(8,128)S(1)}, f32[192,256]{1,0:T(8,128)}, u32[]{:S(2)}, u32[]{:S(2)}) collective-permute-start(f32[192,256]{1,0:T(8,128)S(1)} %get-tuple-element.94), channel_id=1, source_target_pairs={{0,24},{1,8},{2,26},{3,10},{4,28},{5,12},{6,30},{7,14},{8,16},{9,0... | collective-permute-start | bytes 589832 | tf_op jit(solution)/shard_map/ppermute | solution.py:31
  156.8 9.4 %collective-permute-start.32 = (f32[192,256]{1,0:T(8,128)S(1)}, f32[192,256]{1,0:T(8,128)}, u32[]{:S(2)}, u32[]{:S(2)}) collective-permute-start(f32[192,256]{1,0:T(8,128)S(1)} %get-tuple-element.95), channel_id=1, source_target_pairs={{0,8},{1,24},{2,10},{3,26},{4,12},{5,28},{6,14},{7,30},{8,0},{9,16... | collective-permute-start | bytes 589832 | tf_op jit(solution)/shard_map/ppermute | solution.py:31
  157.7 10.4 %collective-permute-start.31 = (f32[192,256]{1,0:T(8,128)}, f32[192,256]{1,0:T(8,128)S(1)}, u32[]{:S(2)}, u32[]{:S(2)}) collective-permute-start(f32[192,256]{1,0:T(8,128)} %get-tuple-element.92), channel_id=1, source_target_pairs={{0,16},{1,0},{2,18},{3,2},{4,20},{5,4},{6,22},{7,6},{8,24},{9,8},{... | collective-permute-start | bytes 589832 | tf_op jit(solution)/shard_map/ppermute | solution.py:31
  163.2 5.6 %collective-permute-start.30 = (f32[192,256]{1,0:T(8,128)}, f32[192,256]{1,0:T(8,128)}, u32[]{:S(2)}, u32[]{:S(2)}) collective-permute-start(f32[192,256]{1,0:T(8,128)} %get-tuple-element.93), channel_id=1, source_target_pairs={{0,0},{1,16},{2,2},{3,18},{4,4},{5,20},{6,6},{7,22},{8,8},{9,24},{... | collective-permute-start | bytes 589832 | tf_op jit(solution)/shard_map/ppermute | solution.py:31
  166.1 4.5 %copy-start.35 = (f32[768,512]{1,0:T(8,128)S(1)}, f32[768,512]{1,0:T(8,128)}, u32[]{:S(2)}) copy-start(f32[768,512]{1,0:T(8,128)} %copy-done.34) | copy-start | bytes 4718596
  (21 other events, 31.4 us)

commit v3 on v2

v3 whole, which is shorter than its diff:
```python
import functools

import jax
import jax.numpy as jnp
from jax import lax
from jax.experimental import pallas as pl
from jax.experimental.pallas import tpu as pltpu
from jax.sharding import PartitionSpec as P

FF = 14336
F32 = jnp.float32
BF16 = jnp.bfloat16
CHUNKS = (384, 512)
SCALE = 1.0
CSPLIT = (3,)
YSPLIT = (3,)
W_AFTER = True
MERGE = False
BB_AFTER = True
KB_AFTER = 1
HB_AFTER = 2
GA_AFTER = True
INPUT_FIRST = True
VMEM = pl.BlockSpec(memory_space=pltpu.VMEM)
SMEM = pl.BlockSpec(memory_space=pltpu.SMEM)
PARAMS = pltpu.CompilerParams(vmem_limit_bytes=10 * 1024 * 1024)


def _split(device):
    dp, tensor = divmod(device, 8)
    return dp // 4, (dp // 2) % 2, dp % 2, tensor // 2, tensor % 2


def _join(z, yl, c, x, yh):
    return ((z % 4) * 4 + yl * 2 + c) * 8 + (x % 4) * 2 + yh


def _move(value, where):
    pairs = [(d, _join(*where(*_split(d)))) for d in range(128)]
    return lax.ppermute(value, ("dp", "tensor"), pairs)


def z_shift(value, by):
    return _move(value, lambda z, yl, c, x, yh: (z + by, yl, c, x, yh))


def x_shift(value, by):
    return _move(value, lambda z, yl, c, x, yh: (z, yl, c, x + by, yh))


def core_swap(value):
    return _move(value, lambda z, yl, c, x, yh: (z, yl, 1 - c, x, yh))


def y_swap(value):
    return _move(value, lambda z, yl, c, x, yh: (z, 1 - yl, c, x, yh))


def far_swap(value):
    return _move(value, lambda z, yl, c, x, yh: (z, 1 - yl, 1 - c, x, 1 - yh))


def after(value, *others):
    return lax.optimization_barrier((value, *others))[0]


def shape(*dims, dtype=F32):
    return jax.ShapeDtypeStruct(dims, dtype)


def local_kernel(kernel, outs, microseconds, *args, scalars=0, scratch=()):
    return pl.pallas_call(
        kernel,
        in_specs=[SMEM] * scalars + [VMEM] * (len(args) - scalars),
        out_specs=[VMEM] * len(outs),
        out_shape=outs,
        scratch_shapes=scratch,
        compiler_params=PARAMS,
        cost_estimate=cost(microseconds),
    )(*args)


def cost(microseconds):
    return pl.CostEstimate(
        flops=int(microseconds * SCALE * 1.1e9), bytes_accessed=1000, transcendentals=0
    )


def arrange_kernel(numbers, x, cotangents, *outs):
    for block in range(16):
        columns = pl.ds(pl.multiple_of(numbers[block] * 256, 256), 256)
        out, k = outs[block // 4], block % 4
        out[0, k] = x[:, columns]
        total = jnp.zeros((x.shape[0], 256), F32)
        for later in range(4):
            total = total + numbers[16 + later].astype(F32) * cotangents[later, :, columns].astype(F32)
        out[1, k] = total.astype(BF16)


def arrange(numbers, activations, cotangents):
    rows = 48
    return pl.pallas_call(
        arrange_kernel,
        grid_spec=pltpu.PrefetchScalarGridSpec(
            num_scalar_prefetch=1,
            grid=(192 // rows,),
            in_specs=[
                pl.BlockSpec((rows, 4096), lambda i, *_: (i, 0)),
                pl.BlockSpec((4, rows, 4096), lambda i, *_: (0, i, 0)),
            ],
            out_specs=[pl.BlockSpec((2, 4, rows, 256), lambda i, *_: (0, 0, i, 0))] * 4,
        ),
        out_shape=[shape(2, 4, 192, 256, dtype=BF16)] * 4,
        compiler_params=PARAMS,
        cost_estimate=cost(3.0),
    )(numbers, activations, cotangents)


def spread(kept, far, sibling, sibling_far):
    return (kept, y_swap(far), core_swap(sibling), far_swap(sibling_far))


def turn_kernel(t0, t1, t2, t3, *outs):
    for which, out in enumerate(outs):
        for k in range(4):
            whole = jnp.concatenate([t[which, k] for t in (t0, t1, t2, t3)], axis=0)
            out[k * 256 : (k + 1) * 256, :] = whole.T


def stack_kernel(*refs):
    weights, outs = refs[:3], refs[3:]
    first = 0
    for out in outs:
        last = first + out.shape[1]
        for m, weight in enumerate(weights):
            out[m * 256 : (m + 1) * 256] = weight[:, first:last]
        first = last


def fill(first, rows, far, low, high, own, nxt, prev):
    far[0:384] = low[...]
    far[384:768] = high[...]
    width = rows.shape[2]
    for m in range(rows.shape[0]):
        for k, part in enumerate((own, nxt, far, prev)):
            start = 0 if part is far else first
            rows[m, k * 256 : (k + 1) * 256] = part[
                m * 256 : (m + 1) * 256, start : start + width
            ]


def part_of(parts, m):
    for part in parts:
        if m < part.shape[0]:
            return part.at[m]
        m -= part.shape[0]


def pre_kernel(first, t0, t1, t2, t3, own, nxt, low, high, prev, keep, *refs):
    *sends, left, rows, far = refs
    fill(first, rows, far, low, high, own, nxt, prev)
    for outs, upper, lower in ((sends, t2, t3), ((keep,), t0, t1)):
        for which in range(2):
            for k in range(4):
                left[0:192, k * 256 : (k + 1) * 256] = upper[which, k]
                left[192:384, k * 256 : (k + 1) * 256] = lower[which, k]
            for m in ((0, 1), (2,))[which]:
                part_of(outs, m)[...] = jnp.dot(
                    left[...], rows[m], preferred_element_type=F32
                )


def half_kernel(keep, *refs):
    received, outs = refs[: len(CSPLIT)], refs[len(CSPLIT) :]
    for m in range(3):
        part_of(outs, m)[...] = (keep[m] + part_of(received, m)[...]).astype(BF16)


def cut_kernel(first, nxt, prev, low, high):
    columns = slice(first, first + low.shape[1])
    low[...] = nxt[0:384, columns]
    high[...] = prev[384:768, columns]


def column_kernel(numbers, own, r1, r2, r3, *outs):
    for j in range(2):
        for i in range(2):
            block = (i + numbers[24]) % 2
            rows = pl.ds(pl.multiple_of(j * 384 + block * 192, 192), 192)
            outs[2 * j + i][...] = (
                own[rows]
                + r1[rows].astype(F32)
                + r2[rows].astype(F32)
                + r3[rows].astype(F32)
            )


def place_kernel(numbers, a0, a1, b0, b1, out):
    for j, (first, second) in enumerate(((a0, a1), (b0, b1))):
        side = (j + numbers[25]) % 2
        out[:, pl.ds(pl.multiple_of(side * 256, 256), 256)] = first[...] + second[...]


def delta_kernel(keep, *refs):
    *refs, out = refs
    received, others = refs[: len(CSPLIT)], refs[len(CSPLIT) :]

    def part(first, swapped):
        @pl.loop(0, 192 // 16)
        def _(i):
            mine = pl.ds(pl.multiple_of(first + i * 16, 16), 16)
            theirs = pl.ds(pl.multiple_of(swapped + i * 16, 16), 16)
            gate, up, grad = (
                (keep[m, mine] + part_of(received, m)[mine])
                + part_of(others, m)[theirs].astype(F32)
                for m in range(3)
            )
            sigmoid = jax.nn.sigmoid(gate)
            silu = gate * sigmoid
            out[0, mine] = (grad * up * sigmoid * (1.0 + gate * (1.0 - sigmoid))).astype(BF16)
            out[1, mine] = (grad * silu).astype(BF16)
            out[2, mine] = (silu * up).astype(BF16)

    part(0, 192)
    part(192, 0)


def grad_kernel(tokens, cotangents, mine, theirs, b0, b1, low, high, b3, right):
    for m in range(3):
        right[0:384] = mine[m]
        right[384:768] = theirs[m]
        left = tokens if m < 2 else cotangents
        for k in (2, 1, 3, 0):
            block = jnp.dot(
                left[k * 256 : (k + 1) * 256, :], right[...], preferred_element_type=F32
            )
            if k != 2:
                (b0, b1, None, b3)[k][m * 256 : (m + 1) * 256] = block
                continue
            block = block.astype(BF16)
            if m == 0:
                low[0:256] = block
            elif m == 1:
                low[256:384] = block[:128]
                high[0:128] = block[128:]
            else:
                high[128:384] = block


def middle_kernel(b1, b3, low, high, ahead, behind):
    ahead[0:384] = (b1[0:384] + low[...].astype(F32)).astype(BF16)
    ahead[384:768] = b1[384:768].astype(BF16)
    behind[0:384] = b3[0:384].astype(BF16)
    behind[384:768] = (b3[384:768] + high[...].astype(F32)).astype(BF16)


def finish_kernel(*refs):
    parts, outs = refs[:-3], refs[-3:]
    for m, out in enumerate(outs):
        rows = slice(m * 256, (m + 1) * 256)
        first = 0
        for i in range(len(parts) // 3):
            b0, r1, r3 = parts[3 * i : 3 * i + 3]
            last = first + b0.shape[1]
            out[:, first:last] = b0[rows] + r1[rows].astype(F32) + r3[rows].astype(F32)
            first = last


def input_kernel(first, last, has_total, numbers, mine, theirs, own, nxt, low, high, prev, *refs):
    if has_total:
        total, *refs = refs
    *outs, rows, far = refs
    fill(first, rows, far, low, high, own, nxt, prev)
    over_units = (((1,), (1,)), ((), ()))
    for j in range(4):
        here = pl.ds(pl.multiple_of(numbers[20 + j] * 256, 256), 256)
        for part, delta in enumerate((mine, theirs)):
            tokens = slice(part * 384, (part + 1) * 384)
            block = lax.dot_general(
                delta[0], rows[0, here, :], over_units, preferred_element_type=F32
            ) + lax.dot_general(delta[1], rows[1, here, :], over_units, preferred_element_type=F32)
            if has_total:
                block = block + total[j, tokens]
            if last:
                outs[j][tokens] = block.astype(outs[j].dtype)
            else:
                outs[0][j, tokens] = block


def local(activations, cotangents, gate_weight, up_weight, down_weight):
    dp, tensor = lax.axis_index("dp"), lax.axis_index("tensor")
    z, yl, c = dp // 4, (dp // 2) % 2, dp % 2
    x, yh = tensor // 2, tensor % 2
    first_unit = tensor * gate_weight.shape[1]
    band_index = (
        1
        + (first_unit >= FF // 8).astype(jnp.int32)
        + (first_unit >= FF // 4).astype(jnp.int32)
        + (first_unit >= FF // 2).astype(jnp.int32)
    )
    source = [
        ((z + k) % 4) * 4 + (yl ^ far) * 2 + (c ^ sibling)
        for sibling in range(2)
        for far in range(2)
        for k in range(4)
    ]
    included = [(k + 1 >= band_index).astype(jnp.int32) for k in range(4)]
    order = [(x + j - z) % 4 for j in range(4)]
    numbers = jnp.stack(source + included + order + [(yh + yl) % 2, c]).astype(jnp.int32)

    stacks = local_kernel(
        stack_kernel,
        [shape(768, width, dtype=BF16) for width in ((896,) if MERGE else CHUNKS)],
        1.0,
        gate_weight,
        up_weight,
        down_weight,
    )

    def first_step(own):
        return own, z_shift(own, -1), z_shift(own, 1)

    columns = [0] * len(CHUNKS)
    if MERGE:
        columns = [sum(CHUNKS[:i]) for i in range(len(CHUNKS))]

    def second_step(own, nxt, prev, first, width):
        low, high = local_kernel(
            functools.partial(cut_kernel, first),
            [shape(384, width, dtype=BF16)] * 2,
            0.5,
            nxt,
            prev,
        )
        return own, nxt, z_shift(low, -1), z_shift(high, 1), prev

    pieces = spread(*arrange(numbers, activations, cotangents))
    turned = local_kernel(turn_kernel, [shape(1024, 768, dtype=BF16)] * 2, 1.0, *pieces)

    rows, halves = [], []
    near = first_step(stacks[0])
    for i, width in enumerate(CHUNKS):
        own, nxt, prev = near
        if i and BB_AFTER:
            nxt = after(nxt, *halves[-1][2])
        column = columns[i]
        rows.append(second_step(own, nxt, prev, column, width))
        if i + 1 < len(CHUNKS) and not MERGE:
            near = first_step(after(stacks[i + 1], near[1]) if W_AFTER else stacks[i + 1])
        late = pieces[0]
        if i:
            late = after(late, *turned, *halves[-1][3][:KB_AFTER])
        keep, *send = local_kernel(
            functools.partial(pre_kernel, column),
            [shape(3, 384, width)] + [shape(count, 384, width) for count in CSPLIT],
            2.6,
            late,
            *pieces[1:],
            *rows[i],
            scratch=(
                pltpu.VMEM((384, 1024), BF16),
                pltpu.VMEM((3, 1024, width), BF16),
                pltpu.VMEM((768, width), BF16),
            ),
        )
        received = [core_swap(part) for part in send]
        if i and HB_AFTER:
            received[0] = after(received[0], *halves[-1][3][:HB_AFTER])
        sent = local_kernel(
            half_kernel,
            [shape(count, 384, width, dtype=BF16) for count in YSPLIT],
            1.0,
            keep,
            *received,
        )
        halves.append((keep, received, sent, [y_swap(part) for part in sent]))

    total, ready, finished = None, None, []
    for i, width in enumerate(CHUNKS):
        keep, received, sent, others = halves[i]
        last = i == len(CHUNKS) - 1
        if ready is not None:
            others = [after(others[0], *ready), *others[1:]]
        (mine,) = local_kernel(
            delta_kernel,
            [shape(3, 384, width, dtype=BF16)],
            width / 300,
            keep,
            *received,
            *others,
        )
        theirs = core_swap(mine)
        if GA_AFTER and not last:
            theirs = after(theirs, *halves[i + 1][2])
        outs = [shape(4, 768, 256)]
        if last:
            outs = [shape(768, 256)] + [shape(768, 256, dtype=BF16)] * 3

        def run_input(theirs):
            return local_kernel(
                functools.partial(input_kernel, columns[i], last, total is not None),
                outs,
                3.0,
                numbers,
                mine,
                theirs,
                *rows[i],
                *(() if total is None else (total,)),
                scalars=1,
                scratch=(pltpu.VMEM((2, 1024, width), BF16), pltpu.VMEM((768, width), BF16)),
            )

        def run_grad(theirs):
            return local_kernel(
                grad_kernel,
                [shape(768, width)] * 2
                + [shape(384, width, dtype=BF16)] * 2
                + [shape(768, width)],
                3.0,
                *turned,
                mine,
                theirs,
                scratch=(pltpu.VMEM((768, width), BF16),),
            )

        if last and INPUT_FIRST:
            partial = run_input(theirs)
            b0, b1, low, high, b3 = run_grad(after(theirs, partial[1]))
        else:
            b0, b1, low, high, b3 = run_grad(theirs)
            partial = run_input(after(theirs, low))
        total = partial[0]
        ahead, behind = local_kernel(
            middle_kernel,
            [shape(768, width, dtype=BF16)] * 2,
            1.0,
            b1,
            b3,
            z_shift(low, 1),
            z_shift(high, -1),
        )
        finished += [b0, z_shift(ahead, 1), z_shift(behind, -1)]
        ready = (*finished[-2:], total)

    blocks = local_kernel(
        column_kernel,
        [shape(192, 256)] * 4,
        1.0,
        numbers,
        partial[0],
        x_shift(partial[1], 1),
        x_shift(partial[2], 2),
        x_shift(partial[3], -1),
        scalars=1,
    )
    moved = [
        _move(
            blocks[2 * j + i],
            lambda z, yl, c, x, yh, i=i, j=j: (z, yh ^ i, c ^ j, x, yl),
        )
        for j in range(2)
        for i in range(2)
    ]
    (input_grad,) = local_kernel(
        place_kernel, [shape(192, 512)], 1.0, numbers, *moved, scalars=1
    )
    gate_grad, up_grad, down_grad = local_kernel(
        finish_kernel, [shape(256, sum(CHUNKS))] * 3, 2.0, *finished
    )
    return (input_grad, gate_grad, up_grad, down_grad)


def solution(mesh):
    return jax.shard_map(
        local,
        mesh=mesh,
        in_specs=(
            P("dp", None),
            P(None, "dp", None),
            P("dp", "tensor"),
            P("dp", "tensor"),
            P("dp", "tensor"),
        ),
        out_specs=(P("dp", "tensor"), P("dp", "tensor"), P("dp", "tensor"), P("dp", "tensor")),
        check_vma=False,
    )
```

time: 177 us -> 167 us (0.944)
  local copies, waits for them, and re-layouts: 24 us -> 6.05 us
  waiting for transfers between devices: 67.5 us -> 83.7 us
  other arithmetic: 5.38 us -> 0 us
    ppermute x38 -> x32, waiting for transfers between devices: 67.5 us -> 83.7 us  [_move(): return lax.ppermute(value, ('dp', 'tensor'), pairs)]
    unnamed x88 -> x10, local copies, waits for them, and re-layouts: 17.5 us -> 5.95 us
    slice x16 -> x0, local copies, waits for them, and re-layouts: 4.54 us -> none  [the longest x9 3.38 us: local(): w[:, first:first + width]]
    add x3 -> x0, other arithmetic: 3.48 us -> none  [the longest x2 2.21 us: local(): sides.append(moved[0] + moved[1])]
    pallas_call x12 -> x19, Pallas kernels: 25.8 us -> 25.2 us  [local_kernel(): pl.pallas_call(kernel, in_specs=[SMEM] * scalars + [VMEM] * (len(args) -...]
    ppermute x38 -> x32, starting transfers between devices: 48.4 us -> 47.9 us  [_move(): return lax.ppermute(value, ('dp', 'tensor'), pairs)]
  transfers between devices with their start and end apart: 38 -> 32, of which waited for: 15 -> 17; matrix products, arithmetic and copies ran while one was open for 5% -> 0% of each run, Pallas kernels for 11% -> 8%
where the time goes in v3:
time: 167 us; the launch traced here: 166 us
  waiting for transfers between devices  83.7 us (50%)
  starting transfers between devices  47.9 us (29%)
  Pallas kernels  27.7 us (17%)
  local copies, waits for them, and re-layouts  6.05 us (4%)
    ppermute x32, waiting for transfers between devices, _move(): return lax.ppermute(value, ('dp', 'tensor'), pairs)  83.7 us
    ppermute x32, starting transfers between devices, _move(): return lax.ppermute(value, ('dp', 'tensor'), pairs)  47.9 us
    pallas_call x19, Pallas kernels, local_kernel(): pl.pallas_call(kernel, in_specs=[SMEM] * scalars + [VMEM] * (len(args) -...  25.2 us
    unnamed x10, local copies, waits for them, and re-layouts  5.95 us
  transfers between devices with their start and end apart: 32, of which 17 were waited for; matrix products, arithmetic and copies ran while one was open for 0% of the time, Pallas kernels for 8%

profile of v3, /device:TPU:1, one launch (start us, length us, event | category | flops | bytes accessed | tf_op | source)
XLA Modules:
  0.0 166.1 jit_solution(9459893674544937052)
XLA Ops:
  0.7 1.1 copy-done.2
  1.8 1.0 copy-done.3
  2.8 1.0 copy-done.4
  3.9 4.7 %collective-permute-start.3 = (bf16[768,384]{1,0:T(8,128)(2,1)S(1)}, bf16[768,384]{1,0:T(8,128)(2,1)S(1)}, u32[]{:S(2)}, u32[]{:S(2)}) collective-permute-start(bf16[768,384]{1,0:T(8,128)(2,1)S(1)} %get-tuple-element.59.own), channel_id=1, source_target_pairs={{0,96},{1,97},{2,98},{3,99},{4,100},{5,101},{6,102},{7,103},{8,104... | collective-permute-start | bytes 1769480 | tf_op jit(solution)/shard_map/ppermute | solution.py:40
  8.7 2.8 %copy-done = bf16[4,192,4096]{2,1,0:T(8,128)(2,1)S(1)} copy-done((bf16[4,192,4096]{2,1,0:T(8,128)(2,1)S(1)}, bf16[4,192,4096]{2,1,0:T(8,128)(2,1)}, u32[]{:S(2)}) %copy-start) | copy-done | bytes 6291480
  11.5 2.5 %shard_map.84 = (bf16[2,4,192,256]{3,2,1,0:T(8,128)(2,1)S(1)}, bf16[2,4,192,256]{3,2,1,0:T(8,128)(2,1)S(1)}, bf16[2,4,192,256]{3,2,1,0:T(8,128)(2,1)S(1)}, bf16[2,4,192,256]{3,2,1,0:T(8,128)(2,1)S(1)}) custom-call(s32[26]{0:T(128)S(1)} %stack.123.numbers, bf16[192,4096]{1,0:T(8,128)(2,1)S(1)} %copy-done.1, bf16[4,192,4096]{2,1,0:T(8,128)(2,1)S(1)} %copy-done), custom_call_target="tpu_custom_call" | custom-call | flops 3300000000 | bytes 1000 | tf_op jit(solution)/shard_map/pallas_call | solution.py:102
  14.0 1.4 collective-permute-start
  15.4 1.2 collective-permute-start.1
  16.6 1.8 %collective-permute-start.2 = (bf16[2,4,192,256]{3,2,1,0:T(8,128)(2,1)S(1)}, bf16[2,4,192,256]{3,2,1,0:T(8,128)(2,1)S(1)}, u32[]{:S(2)}, u32[]{:S(2)}) collective-permute-start(bf16[2,4,192,256]{3,2,1,0:T(8,128)(2,1)S(1)} %get-tuple-element.56), channel_id=1, source_target_pairs={{0,25},{1,24},{2,27},{3,26},{4,29},{5,28},{6,31},{7,30},{8,17},{9,... | collective-permute-start | bytes 2359304 | tf_op jit(solution)/shard_map/ppermute | solution.py:40
  18.4 2.2 %collective-permute-done.3.nxt = bf16[768,384]{1,0:T(8,128)(2,1)S(1)} collective-permute-done((bf16[768,384]{1,0:T(8,128)(2,1)S(1)}, bf16[768,384]{1,0:T(8,128)(2,1)S(1)}, u32[]{:S(2)}, u32[]{:S(2)}) %collective-permute-start.3) | collective-permute-done | bytes 589856 | tf_op jit(solution)/shard_map/ppermute | solution.py:40
  20.6 3.2 %collective-permute-done.4.prev = bf16[768,384]{1,0:T(8,128)(2,1)} collective-permute-done((bf16[768,384]{1,0:T(8,128)(2,1)S(1)}, bf16[768,384]{1,0:T(8,128)(2,1)}, u32[]{:S(2)}, u32[]{:S(2)}) %collective-permute-start.4) | collective-permute-done | bytes 589856 | tf_op jit(solution)/shard_map/ppermute | solution.py:40
  23.8 1.1 shard_map.87
  24.9 0.3 collective-permute-start.5
  25.2 1.3 collective-permute-start.6
  26.4 5.7 %collective-permute-done.t1 = bf16[2,4,192,256]{3,2,1,0:T(8,128)(2,1)S(1)} collective-permute-done((bf16[2,4,192,256]{3,2,1,0:T(8,128)(2,1)S(1)}, bf16[2,4,192,256]{3,2,1,0:T(8,128)(2,1)S(1)}, u32[]{:S(2)}, u32[]{:S(2)}) %collective-permute-start) | collective-permute-done | bytes 786464 | tf_op jit(solution)/shard_map/ppermute | solution.py:40
  32.2 4.8 %collective-permute-done.2.t3 = bf16[2,4,192,256]{3,2,1,0:T(8,128)(2,1)S(1)} collective-permute-done((bf16[2,4,192,256]{3,2,1,0:T(8,128)(2,1)S(1)}, bf16[2,4,192,256]{3,2,1,0:T(8,128)(2,1)S(1)}, u32[]{:S(2)}, u32[]{:S(2)}) %collective-permute-start.2) | collective-permute-done | bytes 786464 | tf_op jit(solution)/shard_map/ppermute | solution.py:40
  37.0 3.8 %shard_map.88 = (f32[3,384,384]{2,1,0:T(8,128)S(1)}, f32[3,384,384]{2,1,0:T(8,128)S(1)}) custom-call(bf16[2,4,192,256]{3,2,1,0:T(8,128)(2,1)S(1)} %get-tuple-element.64.t0, bf16[2,4,192,256]{3,2,1,0:T(8,128)(2,1)S(1)} %collective-permute-done.t1, bf16[2,4,192,256]{3,2,1,0:T(8,128)(2,1)S(1)} %collective-permute-done.1.t2, ...), custom_call_target="tpu_custom_call" | custom-call | flops 2860000000 | bytes 1000 | tf_op jit(solution)/shard_map/pallas_call | solution.py:72
  40.9 3.0 %collective-permute-start.9 = (bf16[768,512]{1,0:T(8,128)(2,1)S(1)}, bf16[768,512]{1,0:T(8,128)(2,1)S(1)}, u32[]{:S(2)}, u32[]{:S(2)}) collective-permute-start(bf16[768,512]{1,0:T(8,128)(2,1)S(1)} %get-tuple-element.66.own), channel_id=1, source_target_pairs={{0,96},{1,97},{2,98},{3,99},{4,100},{5,101},{6,102},{7,103},{8,104... | collective-permute-start | bytes 2359304 | tf_op jit(solution)/shard_map/ppermute | solution.py:40
  43.9 0.7 collective-permute-done.7.refs_0_
  44.5 0.2 shard_map.89
  44.8 15.6 %collective-permute-done.9.nxt = bf16[768,512]{1,0:T(8,128)(2,1)S(1)} collective-permute-done((bf16[768,512]{1,0:T(8,128)(2,1)S(1)}, bf16[768,512]{1,0:T(8,128)(2,1)S(1)}, u32[]{:S(2)}, u32[]{:S(2)}) %collective-permute-start.9) | collective-permute-done | bytes 786464 | tf_op jit(solution)/shard_map/ppermute | solution.py:40
  60.4 3.1 %collective-permute-done.10.prev = bf16[768,512]{1,0:T(8,128)(2,1)S(1)} collective-permute-done((bf16[768,512]{1,0:T(8,128)(2,1)S(1)}, bf16[768,512]{1,0:T(8,128)(2,1)S(1)}, u32[]{:S(2)}, u32[]{:S(2)}) %collective-permute-start.10) | collective-permute-done | bytes 786464 | tf_op jit(solution)/shard_map/ppermute | solution.py:40
  63.5 0.4 collective-permute-start.11
  63.9 1.1 collective-permute-start.12
  65.0 0.9 shard_map.85
  65.9 6.7 %collective-permute-done.11.low = bf16[384,512]{1,0:T(8,128)(2,1)S(1)} collective-permute-done((bf16[384,512]{1,0:T(8,128)(2,1)S(1)}, bf16[384,512]{1,0:T(8,128)(2,1)S(1)}, u32[]{:S(2)}, u32[]{:S(2)}) %collective-permute-start.11) | collective-permute-done | bytes 393248 | tf_op jit(solution)/shard_map/ppermute | solution.py:40
  72.6 1.6 collective-permute-done.12.high
  74.2 2.6 %shard_map.91 = (f32[3,384,512]{2,1,0:T(8,128)S(1)}, f32[3,384,512]{2,1,0:T(8,128)S(1)}) custom-call(bf16[2,4,192,256]{3,2,1,0:T(8,128)(2,1)S(1)} %get-tuple-element.64.t0, bf16[2,4,192,256]{3,2,1,0:T(8,128)(2,1)S(1)} %collective-permute-done.t1, bf16[2,4,192,256]{3,2,1,0:T(8,128)(2,1)S(1)} %collective-permute-done.1.t2, ...), custom_call_target="tpu_custom_call" | custom-call | flops 2860000000 | bytes 1000 | tf_op jit(solution)/shard_map/pallas_call | solution.py:72
  76.8 2.5 %collective-permute-start.13 = (f32[3,384,512]{2,1,0:T(8,128)S(1)}, f32[3,384,512]{2,1,0:T(8,128)S(1)}, u32[]{:S(2)}, u32[]{:S(2)}) collective-permute-start(f32[3,384,512]{2,1,0:T(8,128)S(1)} %get-tuple-element.71), channel_id=1, source_target_pairs={{0,8},{1,9},{2,10},{3,11},{4,12},{5,13},{6,14},{7,15},{8,0},{9,1},... | collective-permute-start | bytes 7077896 | tf_op jit(solution)/shard_map/ppermute | solution.py:40
  79.3 0.6 shard_map.93.mine
  80.0 3.4 %collective-permute-done.13.refs_0_ = f32[3,384,512]{2,1,0:T(8,128)S(1)} collective-permute-done((f32[3,384,512]{2,1,0:T(8,128)S(1)}, f32[3,384,512]{2,1,0:T(8,128)S(1)}, u32[]{:S(2)}, u32[]{:S(2)}) %collective-permute-start.13) | collective-permute-done | bytes 2359328 | tf_op jit(solution)/shard_map/ppermute | solution.py:40
  83.5 0.2 shard_map.92
  83.7 0.8 collective-permute-start.14
  84.5 0.2 collective-permute-done.15.theirs
  84.7 2.6 %shard_map.94 = (f32[768,384]{1,0:T(8,128)S(1)}, f32[768,384]{1,0:T(8,128)S(1)}, bf16[384,384]{1,0:T(8,128)(2,1)S(1)}, bf16[384,384]{1,0:T(8,128)(2,1)S(1)}, f32[768,384]{1,0:T(8,128)S(1)}) custom-call(bf16[1024,768]{1,0:T(8,128)(2,1)S(1)} %get-tuple-element.57.tokens, bf16[1024,768]{1,0:T(8,128)(2,1)S(1)} %get-tuple-element.58.cotangents, ...), custom_call_target="tpu_custom_call" | custom-call | flops 3300000000 | bytes 1000 | tf_op jit(solution)/shard_map/pallas_call | solution.py:72
  87.5 2.7 %collective-permute-start.17 = (bf16[384,384]{1,0:T(8,128)(2,1)S(1)}, bf16[384,384]{1,0:T(8,128)(2,1)S(1)}, u32[]{:S(2)}, u32[]{:S(2)}) collective-permute-start(bf16[384,384]{1,0:T(8,128)(2,1)S(1)} %get-tuple-element.77), channel_id=1, source_target_pairs={{0,96},{1,97},{2,98},{3,99},{4,100},{5,101},{6,102},{7,103},{8,104... | collective-permute-start | bytes 884744 | tf_op jit(solution)/shard_map/ppermute | solution.py:40
  90.1 6.7 %collective-permute-done.16.low = bf16[384,384]{1,0:T(8,128)(2,1)S(1)} collective-permute-done((bf16[384,384]{1,0:T(8,128)(2,1)S(1)}, bf16[384,384]{1,0:T(8,128)(2,1)S(1)}, u32[]{:S(2)}, u32[]{:S(2)}) %collective-permute-start.16) | collective-permute-done | bytes 294944 | tf_op jit(solution)/shard_map/ppermute | solution.py:40
  96.8 0.2 shard_map.95
  97.0 2.7 %collective-permute-start.19 = (bf16[768,384]{1,0:T(8,128)(2,1)S(1)}, bf16[768,384]{1,0:T(8,128)(2,1)S(1)}, u32[]{:S(2)}, u32[]{:S(2)}) collective-permute-start(bf16[768,384]{1,0:T(8,128)(2,1)S(1)} %get-tuple-element.79), channel_id=1, source_target_pairs={{0,96},{1,97},{2,98},{3,99},{4,100},{5,101},{6,102},{7,103},{8,104... | collective-permute-start | bytes 1769480 | tf_op jit(solution)/shard_map/ppermute | solution.py:40
  99.7 3.1 %shard_map.96.refs_0_ = f32[4,768,256]{2,1,0:T(8,128)S(1)} custom-call(s32[26]{0:T(128)S(1)} %stack.123.numbers, bf16[3,384,384]{2,1,0:T(8,128)(2,1)S(1)} %shard_map.93.mine, bf16[3,384,384]{2,1,0:T(8,128)(2,1)S(1)} %collective-permute-done.15.theirs, bf16[768,384]{1,0:T(8,128)(2,1)S(1)} %get-tuple-element.59.own, ...), custom_call_target="tpu_custom_call" | custom-call | flops 3300000000 | bytes 1000 | tf_op jit(solution)/shard_map/pallas_call | solution.py:72
  102.8 9.0 %collective-permute-done.18.refs_1_ = bf16[768,384]{1,0:T(8,128)(2,1)S(1)} collective-permute-done((bf16[768,384]{1,0:T(8,128)(2,1)S(1)}, bf16[768,384]{1,0:T(8,128)(2,1)S(1)}, u32[]{:S(2)}, u32[]{:S(2)}) %collective-permute-start.18) | collective-permute-done | bytes 589856 | tf_op jit(solution)/shard_map/ppermute | solution.py:40
  111.8 0.7 shard_map.97.mine
  112.5 2.3 %collective-permute-start.20 = (bf16[3,384,512]{2,1,0:T(8,128)(2,1)S(1)}, bf16[3,384,512]{2,1,0:T(8,128)(2,1)S(1)}, u32[]{:S(2)}, u32[]{:S(2)}) collective-permute-start(bf16[3,384,512]{2,1,0:T(8,128)(2,1)S(1)} %shard_map.97.mine), channel_id=1, source_target_pairs={{0,8},{1,9},{2,10},{3,11},{4,12},{5,13},{6,14},{7,15},{8,0},{9,1},... | collective-permute-start | bytes 3538952 | tf_op jit(solution)/shard_map/ppermute | solution.py:40
  114.8 2.5 %collective-permute-done.20.theirs = bf16[3,384,512]{2,1,0:T(8,128)(2,1)S(1)} collective-permute-done((bf16[3,384,512]{2,1,0:T(8,128)(2,1)S(1)}, bf16[3,384,512]{2,1,0:T(8,128)(2,1)S(1)}, u32[]{:S(2)}, u32[]{:S(2)}) %collective-permute-start.20) | collective-permute-done | bytes 1179680 | tf_op jit(solution)/shard_map/ppermute | solution.py:40
  117.3 2.5 %shard_map.98 = (f32[768,256]{1,0:T(8,128)S(1)}, bf16[768,256]{1,0:T(8,128)(2,1)S(1)}, bf16[768,256]{1,0:T(8,128)(2,1)S(1)}, bf16[768,256]{1,0:T(8,128)(2,1)S(1)}) custom-call(s32[26]{0:T(128)S(1)} %stack.123.numbers, bf16[3,384,512]{2,1,0:T(8,128)(2,1)S(1)} %shard_map.97.mine, bf16[3,384,512]{2,1,0:T(8,128)(2,1)S(1)} %collective-permute-done.20.theirs, ...), custom_call_target="tpu_custom_call" | custom-call | flops 3300000000 | bytes 1000 | tf_op jit(solution)/shard_map/pallas_call | solution.py:72
  119.8 2.6 %shard_map.101 = (f32[768,512]{1,0:T(8,128)S(1)}, f32[768,512]{1,0:T(8,128)S(1)}, bf16[384,512]{1,0:T(8,128)(2,1)S(1)}, bf16[384,512]{1,0:T(8,128)(2,1)S(1)}, f32[768,512]{1,0:T(8,128)S(1)}) custom-call(bf16[1024,768]{1,0:T(8,128)(2,1)S(1)} %get-tuple-element.57.tokens, bf16[1024,768]{1,0:T(8,128)(2,1)S(1)} %get-tuple-element.58.cotangents, ...), custom_call_target="tpu_custom_call" | custom-call | flops 3300000000 | bytes 1000 | tf_op jit(solution)/shard_map/pallas_call | solution.py:72
  122.4 0.6 collective-permute-start.28
  123.0 2.2 %collective-permute-start.29 = (bf16[384,512]{1,0:T(8,128)(2,1)S(1)}, bf16[384,512]{1,0:T(8,128)(2,1)S(1)}, u32[]{:S(2)}, u32[]{:S(2)}) collective-permute-start(bf16[384,512]{1,0:T(8,128)(2,1)S(1)} %get-tuple-element.96), channel_id=1, source_target_pairs={{0,96},{1,97},{2,98},{3,99},{4,100},{5,101},{6,102},{7,103},{8,104... | collective-permute-start | bytes 1179656 | tf_op jit(solution)/shard_map/ppermute | solution.py:40
  125.2 1.2 collective-permute-start.21
  126.4 2.4 %collective-permute-start.22 = (bf16[768,256]{1,0:T(8,128)(2,1)S(1)}, bf16[768,256]{1,0:T(8,128)(2,1)S(1)}, u32[]{:S(2)}, u32[]{:S(2)}) collective-permute-start(bf16[768,256]{1,0:T(8,128)(2,1)S(1)} %get-tuple-element.84), channel_id=1, source_target_pairs={{0,4},{1,5},{2,6},{3,7},{4,0},{5,1},{6,2},{7,3},{8,12},{9,13},{10,... | collective-permute-start | bytes 1179656 | tf_op jit(solution)/shard_map/ppermute | solution.py:40
  128.9 1.3 collective-permute-start.23
  130.1 3.9 %collective-permute-done.28.low = bf16[384,512]{1,0:T(8,128)(2,1)S(1)} collective-permute-done((bf16[384,512]{1,0:T(8,128)(2,1)S(1)}, bf16[384,512]{1,0:T(8,128)(2,1)S(1)}, u32[]{:S(2)}, u32[]{:S(2)}) %collective-permute-start.28) | collective-permute-done | bytes 393248 | tf_op jit(solution)/shard_map/ppermute | solution.py:40
  134.0 0.2 shard_map.102
  134.2 0.7 collective-permute-start.30
  134.9 2.1 %collective-permute-start.31 = (bf16[768,512]{1,0:T(8,128)(2,1)S(1)}, bf16[768,512]{1,0:T(8,128)(2,1)S(1)}, u32[]{:S(2)}, u32[]{:S(2)}) collective-permute-start(bf16[768,512]{1,0:T(8,128)(2,1)S(1)} %get-tuple-element.98), channel_id=1, source_target_pairs={{0,96},{1,97},{2,98},{3,99},{4,100},{5,101},{6,102},{7,103},{8,104... | collective-permute-start | bytes 2359304 | tf_op jit(solution)/shard_map/ppermute | solution.py:40
  137.0 8.6 %collective-permute-done.22.r2 = bf16[768,256]{1,0:T(8,128)(2,1)S(1)} collective-permute-done((bf16[768,256]{1,0:T(8,128)(2,1)S(1)}, bf16[768,256]{1,0:T(8,128)(2,1)S(1)}, u32[]{:S(2)}, u32[]{:S(2)}) %collective-permute-start.22) | collective-permute-done | bytes 393248 | tf_op jit(solution)/shard_map/ppermute | solution.py:40
  145.6 0.7 shard_map.99
  146.3 0.7 collective-permute-start.24
  147.0 3.0 %collective-permute-start.25 = (f32[192,256]{1,0:T(8,128)S(1)}, f32[192,256]{1,0:T(8,128)S(1)}, u32[]{:S(2)}, u32[]{:S(2)}) collective-permute-start(f32[192,256]{1,0:T(8,128)S(1)} %get-tuple-element.87), channel_id=1, source_target_pairs={{0,16},{1,0},{2,18},{3,2},{4,20},{5,4},{6,22},{7,6},{8,24},{9,8},{... | collective-permute-start | bytes 589832 | tf_op jit(solution)/shard_map/ppermute | solution.py:40
  150.0 2.3 %collective-permute-start.26 = (f32[192,256]{1,0:T(8,128)S(1)}, f32[192,256]{1,0:T(8,128)S(1)}, u32[]{:S(2)}, u32[]{:S(2)}) collective-permute-start(f32[192,256]{1,0:T(8,128)S(1)} %get-tuple-element.88), channel_id=1, source_target_pairs={{0,8},{1,24},{2,10},{3,26},{4,12},{5,28},{6,14},{7,30},{8,0},{9,16... | collective-permute-start | bytes 589832 | tf_op jit(solution)/shard_map/ppermute | solution.py:40
  152.4 4.7 %collective-permute-start.27 = (f32[192,256]{1,0:T(8,128)S(1)}, f32[192,256]{1,0:T(8,128)S(1)}, u32[]{:S(2)}, u32[]{:S(2)}) collective-permute-start(f32[192,256]{1,0:T(8,128)S(1)} %get-tuple-element.89), channel_id=1, source_target_pairs={{0,24},{1,8},{2,26},{3,10},{4,28},{5,12},{6,30},{7,14},{8,16},{9,0... | collective-permute-start | bytes 589832 | tf_op jit(solution)/shard_map/ppermute | solution.py:40
  157.1 5.9 %collective-permute-done.27.b1 = f32[192,256]{1,0:T(8,128)S(1)} collective-permute-done((f32[192,256]{1,0:T(8,128)S(1)}, f32[192,256]{1,0:T(8,128)S(1)}, u32[]{:S(2)}, u32[]{:S(2)}) %collective-permute-start.27) | collective-permute-done | bytes 196640 | tf_op jit(solution)/shard_map/ppermute | solution.py:40
  163.0 1.3 shard_map.100
  164.3 1.8 %shard_map.103 = (f32[256,896]{1,0:T(8,128)}, f32[256,896]{1,0:T(8,128)}, f32[256,896]{1,0:T(8,128)}) custom-call(f32[768,384]{1,0:T(8,128)S(1)} %get-tuple-element.90.refs_0_, bf16[768,384]{1,0:T(8,128)(2,1)S(1)} %collective-permute-done.18.refs_1_, bf16[768,384]{1,0:T(8,128)(2,1)S(1)} %collective-permute-done.19.refs_2_, ...), custom_call_target="tpu_custom_call" | custom-call | flops 2200000000 | bytes 1000 | tf_op jit(solution)/shard_map/pallas_call | solution.py:72
  (31 shorter events, 0.8 us)
Async XLA Ops:
  0.6 8.1 %copy-start.1 = (bf16[192,4096]{1,0:T(8,128)(2,1)S(1)}, bf16[192,4096]{1,0:T(8,128)(2,1)}, u32[]{:S(2)}) copy-start(bf16[192,4096]{1,0:T(8,128)(2,1)} %x.1) | copy-start | bytes 4718596
  0.6 1.1 copy-start.2
  1.8 1.0 copy-start.3
  2.8 1.0 copy-start.4
  3.9 16.7 %collective-permute-start.3 = (bf16[768,384]{1,0:T(8,128)(2,1)S(1)}, bf16[768,384]{1,0:T(8,128)(2,1)S(1)}, u32[]{:S(2)}, u32[]{:S(2)}) collective-permute-start(bf16[768,384]{1,0:T(8,128)(2,1)S(1)} %get-tuple-element.59.own), channel_id=1, source_target_pairs={{0,96},{1,97},{2,98},{3,99},{4,100},{5,101},{6,102},{7,103},{8,104... | collective-permute-start | bytes 1769480 | tf_op jit(solution)/shard_map/ppermute | solution.py:40
  8.6 15.2 %collective-permute-start.4 = (bf16[768,384]{1,0:T(8,128)(2,1)S(1)}, bf16[768,384]{1,0:T(8,128)(2,1)}, u32[]{:S(2)}, u32[]{:S(2)}) collective-permute-start(bf16[768,384]{1,0:T(8,128)(2,1)S(1)} %get-tuple-element.59.own), channel_id=1, source_target_pairs={{0,32},{1,33},{2,34},{3,35},{4,36},{5,37},{6,38},{7,39},{8,40},{9,... | collective-permute-start | bytes 1769480 | tf_op jit(solution)/shard_map/ppermute | solution.py:40
  8.7 2.8 %copy-start = (bf16[4,192,4096]{2,1,0:T(8,128)(2,1)S(1)}, bf16[4,192,4096]{2,1,0:T(8,128)(2,1)}, u32[]{:S(2)}) copy-start(bf16[4,192,4096]{2,1,0:T(8,128)(2,1)} %cotangents.1) | copy-start | bytes 18874372
  14.0 18.2 %collective-permute-start = (bf16[2,4,192,256]{3,2,1,0:T(8,128)(2,1)S(1)}, bf16[2,4,192,256]{3,2,1,0:T(8,128)(2,1)S(1)}, u32[]{:S(2)}, u32[]{:S(2)}) collective-permute-start(bf16[2,4,192,256]{3,2,1,0:T(8,128)(2,1)S(1)} %get-tuple-element.54), channel_id=1, source_target_pairs={{0,16},{1,17},{2,18},{3,19},{4,20},{5,21},{6,22},{7,23},{8,24},{9,... | collective-permute-start | bytes 2359304 | tf_op jit(solution)/shard_map/ppermute | solution.py:40
  15.4 16.8 %collective-permute-start.1 = (bf16[2,4,192,256]{3,2,1,0:T(8,128)(2,1)S(1)}, bf16[2,4,192,256]{3,2,1,0:T(8,128)(2,1)S(1)}, u32[]{:S(2)}, u32[]{:S(2)}) collective-permute-start(bf16[2,4,192,256]{3,2,1,0:T(8,128)(2,1)S(1)} %get-tuple-element.55), channel_id=1, source_target_pairs={{0,8},{1,9},{2,10},{3,11},{4,12},{5,13},{6,14},{7,15},{8,0},{9,1},... | collective-permute-start | bytes 2359304 | tf_op jit(solution)/shard_map/ppermute | solution.py:40
  16.6 20.4 %collective-permute-start.2 = (bf16[2,4,192,256]{3,2,1,0:T(8,128)(2,1)S(1)}, bf16[2,4,192,256]{3,2,1,0:T(8,128)(2,1)S(1)}, u32[]{:S(2)}, u32[]{:S(2)}) collective-permute-start(bf16[2,4,192,256]{3,2,1,0:T(8,128)(2,1)S(1)} %get-tuple-element.56), channel_id=1, source_target_pairs={{0,25},{1,24},{2,27},{3,26},{4,29},{5,28},{6,31},{7,30},{8,17},{9,... | collective-permute-start | bytes 2359304 | tf_op jit(solution)/shard_map/ppermute | solution.py:40
  24.9 12.1 %collective-permute-start.5 = (bf16[384,384]{1,0:T(8,128)(2,1)S(1)}, bf16[384,384]{1,0:T(8,128)(2,1)S(1)}, u32[]{:S(2)}, u32[]{:S(2)}) collective-permute-start(bf16[384,384]{1,0:T(8,128)(2,1)S(1)} %get-tuple-element.60), channel_id=1, source_target_pairs={{0,96},{1,97},{2,98},{3,99},{4,100},{5,101},{6,102},{7,103},{8,104... | collective-permute-start | bytes 884744 | tf_op jit(solution)/shard_map/ppermute | solution.py:40
  25.2 11.8 %collective-permute-start.6 = (bf16[384,384]{1,0:T(8,128)(2,1)S(1)}, bf16[384,384]{1,0:T(8,128)(2,1)S(1)}, u32[]{:S(2)}, u32[]{:S(2)}) collective-permute-start(bf16[384,384]{1,0:T(8,128)(2,1)S(1)} %get-tuple-element.61), channel_id=1, source_target_pairs={{0,32},{1,33},{2,34},{3,35},{4,36},{5,37},{6,38},{7,39},{8,40},{9,... | collective-permute-start | bytes 884744 | tf_op jit(solution)/shard_map/ppermute | solution.py:40
  40.8 3.8 %collective-permute-start.7 = (f32[3,384,384]{2,1,0:T(8,128)S(1)}, f32[3,384,384]{2,1,0:T(8,128)S(1)}, u32[]{:S(2)}, u32[]{:S(2)}) collective-permute-start(f32[3,384,384]{2,1,0:T(8,128)S(1)} %get-tuple-element.63), channel_id=1, source_target_pairs={{0,8},{1,9},{2,10},{3,11},{4,12},{5,13},{6,14},{7,15},{8,0},{9,1},... | collective-permute-start | bytes 5308424 | tf_op jit(solution)/shard_map/ppermute | solution.py:40
  40.9 19.5 %collective-permute-start.9 = (bf16[768,512]{1,0:T(8,128)(2,1)S(1)}, bf16[768,512]{1,0:T(8,128)(2,1)S(1)}, u32[]{:S(2)}, u32[]{:S(2)}) collective-permute-start(bf16[768,512]{1,0:T(8,128)(2,1)S(1)} %get-tuple-element.66.own), channel_id=1, source_target_pairs={{0,96},{1,97},{2,98},{3,99},{4,100},{5,101},{6,102},{7,103},{8,104... | collective-permute-start | bytes 2359304 | tf_op jit(solution)/shard_map/ppermute | solution.py:40
  43.9 19.6 %collective-permute-start.10 = (bf16[768,512]{1,0:T(8,128)(2,1)S(1)}, bf16[768,512]{1,0:T(8,128)(2,1)S(1)}, u32[]{:S(2)}, u32[]{:S(2)}) collective-permute-start(bf16[768,512]{1,0:T(8,128)(2,1)S(1)} %get-tuple-element.66.own), channel_id=1, source_target_pairs={{0,32},{1,33},{2,34},{3,35},{4,36},{5,37},{6,38},{7,39},{8,40},{9,... | collective-permute-start | bytes 2359304 | tf_op jit(solution)/shard_map/ppermute | solution.py:40
  44.7 21.2 %collective-permute-start.8 = (bf16[3,384,384]{2,1,0:T(8,128)(2,1)S(1)}, bf16[3,384,384]{2,1,0:T(8,128)(2,1)S(1)}, u32[]{:S(2)}, u32[]{:S(2)}) collective-permute-start(bf16[3,384,384]{2,1,0:T(8,128)(2,1)S(1)} %shard_map.89), channel_id=1, source_target_pairs={{0,16},{1,17},{2,18},{3,19},{4,20},{5,21},{6,22},{7,23},{8,24},{9,... | collective-permute-start | bytes 2654216 | tf_op jit(solution)/shard_map/ppermute | solution.py:40
  63.5 9.1 %collective-permute-start.11 = (bf16[384,512]{1,0:T(8,128)(2,1)S(1)}, bf16[384,512]{1,0:T(8,128)(2,1)S(1)}, u32[]{:S(2)}, u32[]{:S(2)}) collective-permute-start(bf16[384,512]{1,0:T(8,128)(2,1)S(1)} %get-tuple-element.68), channel_id=1, source_target_pairs={{0,96},{1,97},{2,98},{3,99},{4,100},{5,101},{6,102},{7,103},{8,104... | collective-permute-start | bytes 1179656 | tf_op jit(solution)/shard_map/ppermute | solution.py:40
  63.9 10.3 %collective-permute-start.12 = (bf16[384,512]{1,0:T(8,128)(2,1)S(1)}, bf16[384,512]{1,0:T(8,128)(2,1)S(1)}, u32[]{:S(2)}, u32[]{:S(2)}) collective-permute-start(bf16[384,512]{1,0:T(8,128)(2,1)S(1)} %get-tuple-element.69), channel_id=1, source_target_pairs={{0,32},{1,33},{2,34},{3,35},{4,36},{5,37},{6,38},{7,39},{8,40},{9,... | collective-permute-start | bytes 1179656 | tf_op jit(solution)/shard_map/ppermute | solution.py:40
  76.8 6.7 %collective-permute-start.13 = (f32[3,384,512]{2,1,0:T(8,128)S(1)}, f32[3,384,512]{2,1,0:T(8,128)S(1)}, u32[]{:S(2)}, u32[]{:S(2)}) collective-permute-start(f32[3,384,512]{2,1,0:T(8,128)S(1)} %get-tuple-element.71), channel_id=1, source_target_pairs={{0,8},{1,9},{2,10},{3,11},{4,12},{5,13},{6,14},{7,15},{8,0},{9,1},... | collective-permute-start | bytes 7077896 | tf_op jit(solution)/shard_map/ppermute | solution.py:40
  79.9 4.8 %collective-permute-start.15 = (bf16[3,384,384]{2,1,0:T(8,128)(2,1)S(1)}, bf16[3,384,384]{2,1,0:T(8,128)(2,1)S(1)}, u32[]{:S(2)}, u32[]{:S(2)}) collective-permute-start(bf16[3,384,384]{2,1,0:T(8,128)(2,1)S(1)} %shard_map.93.mine), channel_id=1, source_target_pairs={{0,8},{1,9},{2,10},{3,11},{4,12},{5,13},{6,14},{7,15},{8,0},{9,1},... | collective-permute-start | bytes 2654216 | tf_op jit(solution)/shard_map/ppermute | solution.py:40
  83.7 28.1 %collective-permute-start.14 = (bf16[3,384,512]{2,1,0:T(8,128)(2,1)S(1)}, bf16[3,384,512]{2,1,0:T(8,128)(2,1)S(1)}, u32[]{:S(2)}, u32[]{:S(2)}) collective-permute-start(bf16[3,384,512]{2,1,0:T(8,128)(2,1)S(1)} %shard_map.92), channel_id=1, source_target_pairs={{0,16},{1,17},{2,18},{3,19},{4,20},{5,21},{6,22},{7,23},{8,24},{9,... | collective-permute-start | bytes 3538952 | tf_op jit(solution)/shard_map/ppermute | solution.py:40
  87.4 9.4 %collective-permute-start.16 = (bf16[384,384]{1,0:T(8,128)(2,1)S(1)}, bf16[384,384]{1,0:T(8,128)(2,1)S(1)}, u32[]{:S(2)}, u32[]{:S(2)}) collective-permute-start(bf16[384,384]{1,0:T(8,128)(2,1)S(1)} %get-tuple-element.76), channel_id=1, source_target_pairs={{0,32},{1,33},{2,34},{3,35},{4,36},{5,37},{6,38},{7,39},{8,40},{9,... | collective-permute-start | bytes 884744 | tf_op jit(solution)/shard_map/ppermute | solution.py:40
  87.5 9.3 %collective-permute-start.17 = (bf16[384,384]{1,0:T(8,128)(2,1)S(1)}, bf16[384,384]{1,0:T(8,128)(2,1)S(1)}, u32[]{:S(2)}, u32[]{:S(2)}) collective-permute-start(bf16[384,384]{1,0:T(8,128)(2,1)S(1)} %get-tuple-element.77), channel_id=1, source_target_pairs={{0,96},{1,97},{2,98},{3,99},{4,100},{5,101},{6,102},{7,103},{8,104... | collective-permute-start | bytes 884744 | tf_op jit(solution)/shard_map/ppermute | solution.py:40
  97.0 14.8 %collective-permute-start.18 = (bf16[768,384]{1,0:T(8,128)(2,1)S(1)}, bf16[768,384]{1,0:T(8,128)(2,1)S(1)}, u32[]{:S(2)}, u32[]{:S(2)}) collective-permute-start(bf16[768,384]{1,0:T(8,128)(2,1)S(1)} %get-tuple-element.78), channel_id=1, source_target_pairs={{0,32},{1,33},{2,34},{3,35},{4,36},{5,37},{6,38},{7,39},{8,40},{9,... | collective-permute-start | bytes 1769480 | tf_op jit(solution)/shard_map/ppermute | solution.py:40
  97.0 14.7 %collective-permute-start.19 = (bf16[768,384]{1,0:T(8,128)(2,1)S(1)}, bf16[768,384]{1,0:T(8,128)(2,1)S(1)}, u32[]{:S(2)}, u32[]{:S(2)}) collective-permute-start(bf16[768,384]{1,0:T(8,128)(2,1)S(1)} %get-tuple-element.79), channel_id=1, source_target_pairs={{0,96},{1,97},{2,98},{3,99},{4,100},{5,101},{6,102},{7,103},{8,104... | collective-permute-start | bytes 1769480 | tf_op jit(solution)/shard_map/ppermute | solution.py:40
  112.5 4.8 %collective-permute-start.20 = (bf16[3,384,512]{2,1,0:T(8,128)(2,1)S(1)}, bf16[3,384,512]{2,1,0:T(8,128)(2,1)S(1)}, u32[]{:S(2)}, u32[]{:S(2)}) collective-permute-start(bf16[3,384,512]{2,1,0:T(8,128)(2,1)S(1)} %shard_map.97.mine), channel_id=1, source_target_pairs={{0,8},{1,9},{2,10},{3,11},{4,12},{5,13},{6,14},{7,15},{8,0},{9,1},... | collective-permute-start | bytes 3538952 | tf_op jit(solution)/shard_map/ppermute | solution.py:40
  122.4 11.6 %collective-permute-start.28 = (bf16[384,512]{1,0:T(8,128)(2,1)S(1)}, bf16[384,512]{1,0:T(8,128)(2,1)S(1)}, u32[]{:S(2)}, u32[]{:S(2)}) collective-permute-start(bf16[384,512]{1,0:T(8,128)(2,1)S(1)} %get-tuple-element.95), channel_id=1, source_target_pairs={{0,32},{1,33},{2,34},{3,35},{4,36},{5,37},{6,38},{7,39},{8,40},{9,... | collective-permute-start | bytes 1179656 | tf_op jit(solution)/shard_map/ppermute | solution.py:40
  123.0 11.0 %collective-permute-start.29 = (bf16[384,512]{1,0:T(8,128)(2,1)S(1)}, bf16[384,512]{1,0:T(8,128)(2,1)S(1)}, u32[]{:S(2)}, u32[]{:S(2)}) collective-permute-start(bf16[384,512]{1,0:T(8,128)(2,1)S(1)} %get-tuple-element.96), channel_id=1, source_target_pairs={{0,96},{1,97},{2,98},{3,99},{4,100},{5,101},{6,102},{7,103},{8,104... | collective-permute-start | bytes 1179656 | tf_op jit(solution)/shard_map/ppermute | solution.py:40
  125.2 11.8 %collective-permute-start.21 = (bf16[768,256]{1,0:T(8,128)(2,1)S(1)}, bf16[768,256]{1,0:T(8,128)(2,1)S(1)}, u32[]{:S(2)}, u32[]{:S(2)}) collective-permute-start(bf16[768,256]{1,0:T(8,128)(2,1)S(1)} %get-tuple-element.83), channel_id=1, source_target_pairs={{0,2},{1,3},{2,4},{3,5},{4,6},{5,7},{6,0},{7,1},{8,10},{9,11},{10,... | collective-permute-start | bytes 1179656 | tf_op jit(solution)/shard_map/ppermute | solution.py:40
  126.4 19.2 %collective-permute-start.22 = (bf16[768,256]{1,0:T(8,128)(2,1)S(1)}, bf16[768,256]{1,0:T(8,128)(2,1)S(1)}, u32[]{:S(2)}, u32[]{:S(2)}) collective-permute-start(bf16[768,256]{1,0:T(8,128)(2,1)S(1)} %get-tuple-element.84), channel_id=1, source_target_pairs={{0,4},{1,5},{2,6},{3,7},{4,0},{5,1},{6,2},{7,3},{8,12},{9,13},{10,... | collective-permute-start | bytes 1179656 | tf_op jit(solution)/shard_map/ppermute | solution.py:40
  128.9 16.7 %collective-permute-start.23 = (bf16[768,256]{1,0:T(8,128)(2,1)S(1)}, bf16[768,256]{1,0:T(8,128)(2,1)S(1)}, u32[]{:S(2)}, u32[]{:S(2)}) collective-permute-start(bf16[768,256]{1,0:T(8,128)(2,1)S(1)} %get-tuple-element.85), channel_id=1, source_target_pairs={{0,6},{1,7},{2,0},{3,1},{4,2},{5,3},{6,4},{7,5},{8,14},{9,15},{10,... | collective-permute-start | bytes 1179656 | tf_op jit(solution)/shard_map/ppermute | solution.py:40
  134.2 30.1 %collective-permute-start.30 = (bf16[768,512]{1,0:T(8,128)(2,1)S(1)}, bf16[768,512]{1,0:T(8,128)(2,1)S(1)}, u32[]{:S(2)}, u32[]{:S(2)}) collective-permute-start(bf16[768,512]{1,0:T(8,128)(2,1)S(1)} %get-tuple-element.97), channel_id=1, source_target_pairs={{0,32},{1,33},{2,34},{3,35},{4,36},{5,37},{6,38},{7,39},{8,40},{9,... | collective-permute-start | bytes 2359304 | tf_op jit(solution)/shard_map/ppermute | solution.py:40
  134.9 29.4 %collective-permute-start.31 = (bf16[768,512]{1,0:T(8,128)(2,1)S(1)}, bf16[768,512]{1,0:T(8,128)(2,1)S(1)}, u32[]{:S(2)}, u32[]{:S(2)}) collective-permute-start(bf16[768,512]{1,0:T(8,128)(2,1)S(1)} %get-tuple-element.98), channel_id=1, source_target_pairs={{0,96},{1,97},{2,98},{3,99},{4,100},{5,101},{6,102},{7,103},{8,104... | collective-permute-start | bytes 2359304 | tf_op jit(solution)/shard_map/ppermute | solution.py:40
  146.3 6.0 %collective-permute-start.24 = (f32[192,256]{1,0:T(8,128)S(1)}, f32[192,256]{1,0:T(8,128)S(1)}, u32[]{:S(2)}, u32[]{:S(2)}) collective-permute-start(f32[192,256]{1,0:T(8,128)S(1)} %get-tuple-element.86), channel_id=1, source_target_pairs={{0,0},{1,16},{2,2},{3,18},{4,4},{5,20},{6,6},{7,22},{8,8},{9,24},{... | collective-permute-start | bytes 589832 | tf_op jit(solution)/shard_map/ppermute | solution.py:40
  147.0 10.1 %collective-permute-start.25 = (f32[192,256]{1,0:T(8,128)S(1)}, f32[192,256]{1,0:T(8,128)S(1)}, u32[]{:S(2)}, u32[]{:S(2)}) collective-permute-start(f32[192,256]{1,0:T(8,128)S(1)} %get-tuple-element.87), channel_id=1, source_target_pairs={{0,16},{1,0},{2,18},{3,2},{4,20},{5,4},{6,22},{7,6},{8,24},{9,8},{... | collective-permute-start | bytes 589832 | tf_op jit(solution)/shard_map/ppermute | solution.py:40
  150.0 7.1 %collective-permute-start.26 = (f32[192,256]{1,0:T(8,128)S(1)}, f32[192,256]{1,0:T(8,128)S(1)}, u32[]{:S(2)}, u32[]{:S(2)}) collective-permute-start(f32[192,256]{1,0:T(8,128)S(1)} %get-tuple-element.88), channel_id=1, source_target_pairs={{0,8},{1,24},{2,10},{3,26},{4,12},{5,28},{6,14},{7,30},{8,0},{9,16... | collective-permute-start | bytes 589832 | tf_op jit(solution)/shard_map/ppermute | solution.py:40
  152.4 10.6 %collective-permute-start.27 = (f32[192,256]{1,0:T(8,128)S(1)}, f32[192,256]{1,0:T(8,128)S(1)}, u32[]{:S(2)}, u32[]{:S(2)}) collective-permute-start(f32[192,256]{1,0:T(8,128)S(1)} %get-tuple-element.89), channel_id=1, source_target_pairs={{0,24},{1,8},{2,26},{3,10},{4,28},{5,12},{6,30},{7,14},{8,16},{9,0... | collective-permute-start | bytes 589832 | tf_op jit(solution)/shard_map/ppermute | solution.py:40

commit v4 on v3

--- a/solution.py
+++ b/solution.py
@@ -10,18 +10,15 @@
 FF = 14336
 F32 = jnp.float32
 BF16 = jnp.bfloat16
-CHUNKS = (384, 512)
-SCALE = 1.0
-CSPLIT = (3,)
+CHUNKS = (256, 384, 256)
+COSTS = {}
+ORDER = {"own1": ["nxt0"], "own2": ["nxt1"], "pre2": ["ahead0", "total0"], "half1": ["other0"], "half2": ["other1"], "grad0": ["sent1"], "grad1": ["sent2"], "delta2": ["ahead1", "total1"], "middle1": ["r10", "r30"], "middle2": ["r11", "r31"], "cut2": ["low0"]}
+PARTS = 4
+CSPLIT = (1, 1, 1)
 YSPLIT = (3,)
-W_AFTER = True
-MERGE = False
-BB_AFTER = True
-KB_AFTER = 1
-HB_AFTER = 2
-GA_AFTER = True
 INPUT_FIRST = True
 VMEM = pl.BlockSpec(memory_space=pltpu.VMEM)
+HBM = pl.BlockSpec(memory_space=pltpu.HBM)
 SMEM = pl.BlockSpec(memory_space=pltpu.SMEM)
 PARAMS = pltpu.CompilerParams(vmem_limit_bytes=10 * 1024 * 1024)
 
@@ -68,7 +65,7 @@
     return jax.ShapeDtypeStruct(dims, dtype)
 
 
-def local_kernel(kernel, outs, microseconds, *args, scalars=0, scratch=()):
+def local_kernel(kernel, outs, name, *args, scalars=0, scratch=()):
     return pl.pallas_call(
         kernel,
         in_specs=[SMEM] * scalars + [VMEM] * (len(args) - scalars),
@@ -76,44 +73,64 @@
         out_shape=outs,
         scratch_shapes=scratch,
         compiler_params=PARAMS,
-        cost_estimate=cost(microseconds),
+        cost_estimate=cost(name),
     )(*args)
 
 
-def cost(microseconds):
+def cost(name):
     return pl.CostEstimate(
-        flops=int(microseconds * SCALE * 1.1e9), bytes_accessed=1000, transcendentals=0
+        flops=int(COSTS.get(name, 1.0) * 1.1e9), bytes_accessed=1000, transcendentals=0
     )
 
 
-def arrange_kernel(numbers, x, cotangents, *outs):
-    for block in range(16):
-        columns = pl.ds(pl.multiple_of(numbers[block] * 256, 256), 256)
-        out, k = outs[block // 4], block % 4
-        out[0, k] = x[:, columns]
-        total = jnp.zeros((x.shape[0], 256), F32)
-        for later in range(4):
-            total = total + numbers[16 + later].astype(F32) * cotangents[later, :, columns].astype(F32)
-        out[1, k] = total.astype(BF16)
+def arrange_kernel(numbers, activations, cotangents, *refs):
+    outs, (x, later_x, x_sem, sem) = refs[:4], refs[4:]
+    rows = [pl.ds(part * (192 // PARTS), 192 // PARTS) for part in range(PARTS)]
+
+    def copy(part, later):
+        if later < 0:
+            return pltpu.make_async_copy(
+                activations.at[rows[part]], x.at[rows[part]], x_sem.at[part]
+            )
+        return pltpu.make_async_copy(
+            cotangents.at[later, rows[part]],
+            later_x.at[later, rows[part]],
+            sem.at[part, later],
+        )
+
+    for part in range(PARTS):
+        for later in range(-1, 4):
+            copy(part, later).start()
+    for part in range(PARTS):
+        for later in range(-1, 4):
+            copy(part, later).wait()
+        for block in range(16):
+            columns = pl.ds(pl.multiple_of(numbers[block] * 256, 256), 256)
+            out, k = outs[block // 4], block % 4
+            out[0, k, rows[part], :] = x[rows[part], columns]
+            total = jnp.zeros((192 // PARTS, 256), F32)
+            for later in range(4):
+                total = total + numbers[16 + later].astype(F32) * later_x[
+                    later, rows[part], columns
+                ].astype(F32)
+            out[1, k, rows[part], :] = total.astype(BF16)
 
 
 def arrange(numbers, activations, cotangents):
-    rows = 48
     return pl.pallas_call(
         arrange_kernel,
-        grid_spec=pltpu.PrefetchScalarGridSpec(
-            num_scalar_prefetch=1,
-            grid=(192 // rows,),
-            in_specs=[
-                pl.BlockSpec((rows, 4096), lambda i, *_: (i, 0)),
-                pl.BlockSpec((4, rows, 4096), lambda i, *_: (0, i, 0)),
-            ],
-            out_specs=[pl.BlockSpec((2, 4, rows, 256), lambda i, *_: (0, 0, i, 0))] * 4,
-        ),
+        in_specs=[SMEM, HBM, HBM],
+        out_specs=[VMEM] * 4,
         out_shape=[shape(2, 4, 192, 256, dtype=BF16)] * 4,
-        compiler_params=PARAMS,
-        cost_estimate=cost(3.0),
-    )(numbers, activations, cotangents)
+        scratch_shapes=[
+            pltpu.VMEM((192, 4096), BF16),
+            pltpu.VMEM((4, 192, 4096), BF16),
+            pltpu.SemaphoreType.DMA((PARTS,)),
+            pltpu.SemaphoreType.DMA((PARTS, 4)),
+        ],
+        compiler_params=pltpu.CompilerParams(vmem_limit_bytes=16 * 1024 * 1024),
+        cost_estimate=cost("arrange"),
+    )(numbers, *[pltpu.with_memory_space_constraint(v, pltpu.HBM) for v in (activations, cotangents)])
 
 
 def spread(kept, far, sibling, sibling_far):
@@ -128,25 +145,44 @@
 
 
 def stack_kernel(*refs):
-    weights, outs = refs[:3], refs[3:]
-    first = 0
-    for out in outs:
+    weights, outs, sem = refs[:3], refs[3:-1], refs[-1]
+    copies, first = [], 0
+    for i, out in enumerate(outs):
         last = first + out.shape[1]
         for m, weight in enumerate(weights):
-            out[m * 256 : (m + 1) * 256] = weight[:, first:last]
+            copies.append(
+                pltpu.make_async_copy(
+                    weight.at[:, pl.ds(first, last - first)],
+                    out.at[pl.ds(m * 256, 256)],
+                    sem.at[i, m],
+                )
+            )
         first = last
-
-
-def fill(first, rows, far, low, high, own, nxt, prev):
+    for copy in copies:
+        copy.start()
+    for copy in copies:
+        copy.wait()
+
+
+def stack(*weights):
+    outs = [shape(768, width, dtype=BF16) for width in CHUNKS]
+    return pl.pallas_call(
+        stack_kernel,
+        in_specs=[HBM] * 3,
+        out_specs=[VMEM] * len(outs),
+        out_shape=outs,
+        scratch_shapes=[pltpu.SemaphoreType.DMA((len(outs), 3))],
+        compiler_params=PARAMS,
+        cost_estimate=cost("stack"),
+    )(*[pltpu.with_memory_space_constraint(v, pltpu.HBM) for v in weights])
+
+
+def fill(rows, far, low, high, own, nxt, prev):
     far[0:384] = low[...]
     far[384:768] = high[...]
-    width = rows.shape[2]
     for m in range(rows.shape[0]):
         for k, part in enumerate((own, nxt, far, prev)):
-            start = 0 if part is far else first
-            rows[m, k * 256 : (k + 1) * 256] = part[
-                m * 256 : (m + 1) * 256, start : start + width
-            ]
+            rows[m, k * 256 : (k + 1) * 256] = part[m * 256 : (m + 1) * 256]
 
 
 def part_of(parts, m):
@@ -156,9 +192,9 @@
         m -= part.shape[0]
 
 
-def pre_kernel(first, t0, t1, t2, t3, own, nxt, low, high, prev, keep, *refs):
+def pre_kernel(t0, t1, t2, t3, own, nxt, low, high, prev, keep, *refs):
     *sends, left, rows, far = refs
-    fill(first, rows, far, low, high, own, nxt, prev)
+    fill(rows, far, low, high, own, nxt, prev)
     for outs, upper, lower in ((sends, t2, t3), ((keep,), t0, t1)):
         for which in range(2):
             for k in range(4):
@@ -176,10 +212,9 @@
         part_of(outs, m)[...] = (keep[m] + part_of(received, m)[...]).astype(BF16)
 
 
-def cut_kernel(first, nxt, prev, low, high):
-    columns = slice(first, first + low.shape[1])
-    low[...] = nxt[0:384, columns]
-    high[...] = prev[384:768, columns]
+def cut_kernel(nxt, prev, low, high):
+    low[...] = nxt[0:384]
+    high[...] = prev[384:768]
 
 
 def column_kernel(numbers, own, r1, r2, r3, *outs):
@@ -266,11 +301,11 @@
             first = last
 
 
-def input_kernel(first, last, has_total, numbers, mine, theirs, own, nxt, low, high, prev, *refs):
+def input_kernel(last, has_total, numbers, mine, theirs, own, nxt, low, high, prev, *refs):
     if has_total:
         total, *refs = refs
     *outs, rows, far = refs
-    fill(first, rows, far, low, high, own, nxt, prev)
+    fill(rows, far, low, high, own, nxt, prev)
     over_units = (((1,), (1,)), ((), ()))
     for j in range(4):
         here = pl.ds(pl.multiple_of(numbers[20 + j] * 256, 256), 256)
@@ -308,53 +343,40 @@
     order = [(x + j - z) % 4 for j in range(4)]
     numbers = jnp.stack(source + included + order + [(yh + yl) % 2, c]).astype(jnp.int32)
 
-    stacks = local_kernel(
-        stack_kernel,
-        [shape(768, width, dtype=BF16) for width in ((896,) if MERGE else CHUNKS)],
-        1.0,
-        gate_weight,
-        up_weight,
-        down_weight,
-    )
+    stacks = stack(gate_weight, up_weight, down_weight)
 
     def first_step(own):
         return own, z_shift(own, -1), z_shift(own, 1)
 
-    columns = [0] * len(CHUNKS)
-    if MERGE:
-        columns = [sum(CHUNKS[:i]) for i in range(len(CHUNKS))]
-
-    def second_step(own, nxt, prev, first, width):
+    def second_step(own, nxt, prev):
         low, high = local_kernel(
-            functools.partial(cut_kernel, first),
-            [shape(384, width, dtype=BF16)] * 2,
-            0.5,
-            nxt,
-            prev,
+            cut_kernel, [shape(384, own.shape[1], dtype=BF16)] * 2, "cut", nxt, prev
         )
         return own, nxt, z_shift(low, -1), z_shift(high, 1), prev
 
     pieces = spread(*arrange(numbers, activations, cotangents))
-    turned = local_kernel(turn_kernel, [shape(1024, 768, dtype=BF16)] * 2, 1.0, *pieces)
-
-    rows, halves = [], []
-    near = first_step(stacks[0])
-    for i, width in enumerate(CHUNKS):
-        own, nxt, prev = near
-        if i and BB_AFTER:
-            nxt = after(nxt, *halves[-1][2])
-        column = columns[i]
-        rows.append(second_step(own, nxt, prev, column, width))
-        if i + 1 < len(CHUNKS) and not MERGE:
-            near = first_step(after(stacks[i + 1], near[1]) if W_AFTER else stacks[i + 1])
-        late = pieces[0]
-        if i:
-            late = after(late, *turned, *halves[-1][3][:KB_AFTER])
+    turned = local_kernel(turn_kernel, [shape(1024, 768, dtype=BF16)] * 2, "turn", *pieces)
+
+    known, rows, halves = {}, [], []
+
+    def hold(stage, value):
+        names = ORDER.get(stage, ())
+        return after(value, *[known[name] for name in names]) if names else value
+
+    near = [first_step(stacks[0])]
+
+    def forward(i, width):
+        own, nxt, prev = near[0]
+        known[f"nxt{i}"], known[f"prev{i}"] = nxt, prev
+        rows.append(second_step(own, hold(f"cut{i}", nxt), prev))
+        if i + 1 < len(CHUNKS):
+            near[0] = first_step(hold(f"own{i + 1}", stacks[i + 1]))
+        late = pieces[0] if i == 0 else after(pieces[0], *turned)
         keep, *send = local_kernel(
-            functools.partial(pre_kernel, column),
+            pre_kernel,
             [shape(3, 384, width)] + [shape(count, 384, width) for count in CSPLIT],
-            2.6,
-            late,
+            f"pre{i}",
+            hold(f"pre{i}", late),
             *pieces[1:],
             *rows[i],
             scratch=(
@@ -364,46 +386,44 @@
             ),
         )
         received = [core_swap(part) for part in send]
-        if i and HB_AFTER:
-            received[0] = after(received[0], *halves[-1][3][:HB_AFTER])
         sent = local_kernel(
             half_kernel,
             [shape(count, 384, width, dtype=BF16) for count in YSPLIT],
-            1.0,
-            keep,
+            f"half{i}",
+            hold(f"half{i}", keep),
             *received,
         )
-        halves.append((keep, received, sent, [y_swap(part) for part in sent]))
-
-    total, ready, finished = None, None, []
-    for i, width in enumerate(CHUNKS):
-        keep, received, sent, others = halves[i]
+        others = [y_swap(part) for part in sent]
+        known[f"sent{i}"], known[f"other{i}"] = sent[0], others[0]
+        halves.append((keep, received, others))
+
+    finished, totals = [], [None]
+
+    def backward(i, width):
+        total = totals[0]
+        keep, received, others = halves[i]
         last = i == len(CHUNKS) - 1
-        if ready is not None:
-            others = [after(others[0], *ready), *others[1:]]
         (mine,) = local_kernel(
             delta_kernel,
             [shape(3, 384, width, dtype=BF16)],
-            width / 300,
-            keep,
+            f"delta{i}",
+            hold(f"delta{i}", keep),
             *received,
             *others,
         )
         theirs = core_swap(mine)
-        if GA_AFTER and not last:
-            theirs = after(theirs, *halves[i + 1][2])
         outs = [shape(4, 768, 256)]
         if last:
             outs = [shape(768, 256)] + [shape(768, 256, dtype=BF16)] * 3
 
         def run_input(theirs):
             return local_kernel(
-                functools.partial(input_kernel, columns[i], last, total is not None),
+                functools.partial(input_kernel, last, total is not None),
                 outs,
-                3.0,
+                f"input{i}",
                 numbers,
                 mine,
-                theirs,
+                hold(f"input{i}", theirs),
                 *rows[i],
                 *(() if total is None else (total,)),
                 scalars=1,
@@ -416,10 +436,10 @@
                 [shape(768, width)] * 2
                 + [shape(384, width, dtype=BF16)] * 2
                 + [shape(768, width)],
-                3.0,
+                f"grad{i}",
                 *turned,
                 mine,
-                theirs,
+                hold(f"grad{i}", theirs),
                 scratch=(pltpu.VMEM((768, width), BF16),),
             )
 
@@ -429,23 +449,33 @@
         else:
             b0, b1, low, high, b3 = run_grad(theirs)
             partial = run_input(after(theirs, low))
-        total = partial[0]
+        totals[0] = total = partial[0]
+        known[f"total{i}"] = total
         ahead, behind = local_kernel(
             middle_kernel,
             [shape(768, width, dtype=BF16)] * 2,
-            1.0,
-            b1,
+            f"middle{i}",
+            hold(f"middle{i}", b1),
             b3,
             z_shift(low, 1),
             z_shift(high, -1),
         )
-        finished += [b0, z_shift(ahead, 1), z_shift(behind, -1)]
-        ready = (*finished[-2:], total)
+        finished.extend([b0, z_shift(ahead, 1), z_shift(behind, -1)])
+        known[f"ahead{i}"] = ahead
+        known[f"r1{i}"], known[f"r3{i}"] = finished[-2:]
+        known[f"low{i}"] = low
+        return partial
+
+    for i, width in enumerate(CHUNKS):
+        forward(i, width)
+        if i:
+            backward(i - 1, CHUNKS[i - 1])
+    partial = backward(len(CHUNKS) - 1, CHUNKS[-1])
 
     blocks = local_kernel(
         column_kernel,
         [shape(192, 256)] * 4,
-        1.0,
+        "column",
         numbers,
         partial[0],
         x_shift(partial[1], 1),
@@ -462,10 +492,10 @@
         for i in range(2)
     ]
     (input_grad,) = local_kernel(
-        place_kernel, [shape(192, 512)], 1.0, numbers, *moved, scalars=1
+        place_kernel, [shape(192, 512)], "place", numbers, *moved, scalars=1
     )
     gate_grad, up_grad, down_grad = local_kernel(
-        finish_kernel, [shape(256, sum(CHUNKS))] * 3, 2.0, *finished
+        finish_kernel, [shape(256, sum(CHUNKS))] * 3, "finish", *finished
     )
     return (input_grad, gate_grad, up_grad, down_grad)
 

time: 167 us -> 151 us (0.904)
  waiting for transfers between devices: 83.7 us -> 61.2 us
  starting transfers between devices: 47.9 us -> 58.6 us
  local copies, waits for them, and re-layouts: 6.05 us -> 0.1 us
  Pallas kernels: 27.7 us -> 29.9 us
    ppermute x32 -> x49, waiting for transfers between devices: 83.7 us -> 61.2 us  [_move(): return lax.ppermute(value, ('dp', 'tensor'), pairs)]
    ppermute x32 -> x49, starting transfers between devices: 47.9 us -> 58.6 us  [_move(): return lax.ppermute(value, ('dp', 'tensor'), pairs)]
    unnamed x10 -> x0, local copies, waits for them, and re-layouts: 5.95 us -> none
    pallas_call x1 -> x2, Pallas kernels: 2.49 us -> 5.89 us  [the longest x1 4.4 us: arrange(): pl.pallas_call(arrange_kernel, in_specs=[SMEM, HBM, HBM], out_specs=[VMEM...]
    pallas_call x19 -> x25, Pallas kernels: 25.2 us -> 24 us  [local_kernel(): pl.pallas_call(kernel, in_specs=[SMEM] * scalars + [VMEM] * (len(args) -...]
  transfers between devices with their start and end apart: 32 -> 49, of which waited for: 17 -> 23; matrix products, arithmetic and copies ran while one was open for 0% -> 0% of each run, Pallas kernels for 8% -> 17%
where the time goes in v4:
time: 151 us
  waiting for transfers between devices  61.2 us (41%)
  starting transfers between devices  58.6 us (39%)
  Pallas kernels  29.9 us (20%)
    ppermute x49, waiting for transfers between devices, _move(): return lax.ppermute(value, ('dp', 'tensor'), pairs)  61.2 us
    ppermute x49, starting transfers between devices, _move(): return lax.ppermute(value, ('dp', 'tensor'), pairs)  58.6 us
    pallas_call x25, Pallas kernels, local_kernel(): pl.pallas_call(kernel, in_specs=[SMEM] * scalars + [VMEM] * (len(args) -...  24 us
    pallas_call x1, Pallas kernels, arrange(): pl.pallas_call(arrange_kernel, in_specs=[SMEM, HBM, HBM], out_specs=[VMEM...  4.4 us
  transfers between devices with their start and end apart: 49, of which 23 were waited for; matrix products, arithmetic and copies ran while one was open for 0% of the time, Pallas kernels for 17%

profile of v4, /device:TPU:1, one launch (start us, length us, event | category | flops | bytes accessed | tf_op | source)
XLA Modules:
  0.0 150.7 jit_solution(4989111312582667424)
XLA Ops:
  0.6 1.5 shard_map.86
  2.1 4.7 %collective-permute-start.3 = (bf16[768,256]{1,0:T(8,128)(2,1)S(1)}, bf16[768,256]{1,0:T(8,128)(2,1)S(1)}, u32[]{:S(2)}, u32[]{:S(2)}) collective-permute-start(bf16[768,256]{1,0:T(8,128)(2,1)S(1)} %get-tuple-element.85.own), channel_id=1, source_target_pairs={{0,96},{1,97},{2,98},{3,99},{4,100},{5,101},{6,102},{7,103},{8,104... | collective-permute-start | bytes 1179656 | tf_op jit(solution)/shard_map/ppermute | solution.py:37
  6.9 4.4 %shard_map.84 = (bf16[2,4,192,256]{3,2,1,0:T(8,128)(2,1)S(1)}, bf16[2,4,192,256]{3,2,1,0:T(8,128)(2,1)S(1)}, bf16[2,4,192,256]{3,2,1,0:T(8,128)(2,1)S(1)}, bf16[2,4,192,256]{3,2,1,0:T(8,128)(2,1)S(1)}) custom-call(s32[26]{0:T(128)S(1)} %stack.123.numbers, bf16[192,4096]{1,0:T(8,128)(2,1)} %activations.1, bf16[4,192,4096]{2,1,0:T(8,128)(2,1)} %cotangents.1), custom_call_target="tpu_custom_call" | custom-call | flops 1100000000 | bytes 1000 | tf_op jit(solution)/shard_map/pallas_call | solution.py:120
  11.3 1.4 collective-permute-start
  12.7 1.2 collective-permute-start.1
  13.9 1.8 %collective-permute-start.2 = (bf16[2,4,192,256]{3,2,1,0:T(8,128)(2,1)S(1)}, bf16[2,4,192,256]{3,2,1,0:T(8,128)(2,1)S(1)}, u32[]{:S(2)}, u32[]{:S(2)}) collective-permute-start(bf16[2,4,192,256]{3,2,1,0:T(8,128)(2,1)S(1)} %get-tuple-element.81), channel_id=1, source_target_pairs={{0,25},{1,24},{2,27},{3,26},{4,29},{5,28},{6,31},{7,30},{8,17},{9,... | collective-permute-start | bytes 2359304 | tf_op jit(solution)/shard_map/ppermute | solution.py:37
  15.7 1.9 %collective-permute-done.4.prev = bf16[768,256]{1,0:T(8,128)(2,1)S(1)} collective-permute-done((bf16[768,256]{1,0:T(8,128)(2,1)S(1)}, bf16[768,256]{1,0:T(8,128)(2,1)S(1)}, u32[]{:S(2)}, u32[]{:S(2)}) %collective-permute-start.4) | collective-permute-done | bytes 393248 | tf_op jit(solution)/shard_map/ppermute | solution.py:37
  17.7 1.1 collective-permute-start.5
  19.2 3.3 %collective-permute-done.5.low = bf16[384,256]{1,0:T(8,128)(2,1)S(1)} collective-permute-done((bf16[384,256]{1,0:T(8,128)(2,1)S(1)}, bf16[384,256]{1,0:T(8,128)(2,1)S(1)}, u32[]{:S(2)}, u32[]{:S(2)}) %collective-permute-start.5) | collective-permute-done | bytes 196640 | tf_op jit(solution)/shard_map/ppermute | solution.py:37
  22.6 3.0 %collective-permute-start.12 = (bf16[768,384]{1,0:T(8,128)(2,1)S(1)}, bf16[768,384]{1,0:T(8,128)(2,1)S(1)}, u32[]{:S(2)}, u32[]{:S(2)}) collective-permute-start(bf16[768,384]{1,0:T(8,128)(2,1)S(1)} %get-tuple-element.93.own), channel_id=1, source_target_pairs={{0,96},{1,97},{2,98},{3,99},{4,100},{5,101},{6,102},{7,103},{8,104... | collective-permute-start | bytes 1769480 | tf_op jit(solution)/shard_map/ppermute | solution.py:37
  25.5 3.9 %collective-permute-done.t1 = bf16[2,4,192,256]{3,2,1,0:T(8,128)(2,1)S(1)} collective-permute-done((bf16[2,4,192,256]{3,2,1,0:T(8,128)(2,1)S(1)}, bf16[2,4,192,256]{3,2,1,0:T(8,128)(2,1)S(1)}, u32[]{:S(2)}, u32[]{:S(2)}) %collective-permute-start) | collective-permute-done | bytes 786464 | tf_op jit(solution)/shard_map/ppermute | solution.py:37
  29.5 5.1 %collective-permute-done.2.t3 = bf16[2,4,192,256]{3,2,1,0:T(8,128)(2,1)S(1)} collective-permute-done((bf16[2,4,192,256]{3,2,1,0:T(8,128)(2,1)S(1)}, bf16[2,4,192,256]{3,2,1,0:T(8,128)(2,1)S(1)}, u32[]{:S(2)}, u32[]{:S(2)}) %collective-permute-start.2) | collective-permute-done | bytes 786464 | tf_op jit(solution)/shard_map/ppermute | solution.py:37
  34.6 1.4 shard_map.88
  36.1 0.5 collective-permute-start.8
  36.7 2.9 %collective-permute-done.13.prev = bf16[768,384]{1,0:T(8,128)(2,1)S(1)} collective-permute-done((bf16[768,384]{1,0:T(8,128)(2,1)S(1)}, bf16[768,384]{1,0:T(8,128)(2,1)S(1)}, u32[]{:S(2)}, u32[]{:S(2)}) %collective-permute-start.13) | collective-permute-done | bytes 589856 | tf_op jit(solution)/shard_map/ppermute | solution.py:37
  39.9 1.2 collective-permute-start.15
  41.1 0.9 shard_map.85
  42.2 3.0 %collective-permute-done.14.low = bf16[384,384]{1,0:T(8,128)(2,1)S(1)} collective-permute-done((bf16[384,384]{1,0:T(8,128)(2,1)S(1)}, bf16[384,384]{1,0:T(8,128)(2,1)S(1)}, u32[]{:S(2)}, u32[]{:S(2)}) %collective-permute-start.14) | collective-permute-done | bytes 294944 | tf_op jit(solution)/shard_map/ppermute | solution.py:37
  45.2 1.5 collective-permute-done.15.high
  46.7 2.7 %shard_map.92 = (f32[3,384,384]{2,1,0:T(8,128)S(1)}, f32[1,384,384]{2,1,0:T(8,128)S(1)}, f32[1,384,384]{2,1,0:T(8,128)S(1)}, f32[1,384,384]{2,1,0:T(8,128)S(1)}) custom-call(bf16[2,4,192,256]{3,2,1,0:T(8,128)(2,1)S(1)} %get-tuple-element.108.t0, bf16[2,4,192,256]{3,2,1,0:T(8,128)(2,1)S(1)} %collective-permute-done.t1, ...), custom_call_target="tpu_custom_call" | custom-call | flops 1100000000 | bytes 1000 | tf_op jit(solution)/shard_map/pallas_call | solution.py:69
  49.5 4.2 %collective-permute-start.16 = (f32[1,384,384]{2,1,0:T(8,128)S(1)}, f32[1,384,384]{2,1,0:T(8,128)S(1)}, u32[]{:S(2)}, u32[]{:S(2)}) collective-permute-start(f32[1,384,384]{2,1,0:T(8,128)S(1)} %get-tuple-element.98), channel_id=1, source_target_pairs={{0,8},{1,9},{2,10},{3,11},{4,12},{5,13},{6,14},{7,15},{8,0},{9,1},... | collective-permute-start | bytes 1769480 | tf_op jit(solution)/shard_map/ppermute | solution.py:37
  54.2 1.1 collective-permute-done.16.refs_0_
  55.3 0.8 collective-permute-done.17.refs_1_
  56.1 0.8 collective-permute-done.18.refs_2_
  57.7 1.5 %collective-permute-start.11 = (bf16[3,384,256]{2,1,0:T(8,128)(2,1)S(1)}, bf16[3,384,256]{2,1,0:T(8,128)(2,1)S(1)}, u32[]{:S(2)}, u32[]{:S(2)}) collective-permute-start(bf16[3,384,256]{2,1,0:T(8,128)(2,1)S(1)} %shard_map.90.mine), channel_id=1, source_target_pairs={{0,8},{1,9},{2,10},{3,11},{4,12},{5,13},{6,14},{7,15},{8,0},{9,1},... | collective-permute-start | bytes 1769480 | tf_op jit(solution)/shard_map/ppermute | solution.py:37
  59.2 1.5 collective-permute-start.21
  60.9 1.4 shard_map.94
  62.3 2.7 %collective-permute-start.20 = (bf16[384,256]{1,0:T(8,128)(2,1)S(1)}, bf16[384,256]{1,0:T(8,128)(2,1)S(1)}, u32[]{:S(2)}, u32[]{:S(2)}) collective-permute-start(bf16[384,256]{1,0:T(8,128)(2,1)S(1)} %get-tuple-element.105), channel_id=1, source_target_pairs={{0,96},{1,97},{2,98},{3,99},{4,100},{5,101},{6,102},{7,103},{8,104... | collective-permute-start | bytes 589832 | tf_op jit(solution)/shard_map/ppermute | solution.py:37
  65.0 4.9 %collective-permute-done.21.nxt = bf16[768,256]{1,0:T(8,128)(2,1)S(1)} collective-permute-done((bf16[768,256]{1,0:T(8,128)(2,1)S(1)}, bf16[768,256]{1,0:T(8,128)(2,1)S(1)}, u32[]{:S(2)}, u32[]{:S(2)}) %collective-permute-start.21) | collective-permute-done | bytes 393248 | tf_op jit(solution)/shard_map/ppermute | solution.py:37
  69.9 2.4 %collective-permute-done.22.prev = bf16[768,256]{1,0:T(8,128)(2,1)S(1)} collective-permute-done((bf16[768,256]{1,0:T(8,128)(2,1)S(1)}, bf16[768,256]{1,0:T(8,128)(2,1)S(1)}, u32[]{:S(2)}, u32[]{:S(2)}) %collective-permute-start.22) | collective-permute-done | bytes 393248 | tf_op jit(solution)/shard_map/ppermute | solution.py:37
  72.7 1.1 collective-permute-start.24
  73.9 3.5 %collective-permute-done.25.refs_3_ = bf16[3,384,384]{2,1,0:T(8,128)(2,1)S(1)} collective-permute-done((bf16[3,384,384]{2,1,0:T(8,128)(2,1)S(1)}, bf16[3,384,384]{2,1,0:T(8,128)(2,1)S(1)}, u32[]{:S(2)}, u32[]{:S(2)}) %collective-permute-start.25) | collective-permute-done | bytes 884768 | tf_op jit(solution)/shard_map/ppermute | solution.py:37
  77.4 0.6 shard_map.99.mine
  78.0 2.0 %collective-permute-start.26 = (bf16[3,384,384]{2,1,0:T(8,128)(2,1)S(1)}, bf16[3,384,384]{2,1,0:T(8,128)(2,1)S(1)}, u32[]{:S(2)}, u32[]{:S(2)}) collective-permute-start(bf16[3,384,384]{2,1,0:T(8,128)(2,1)S(1)} %shard_map.99.mine), channel_id=1, source_target_pairs={{0,8},{1,9},{2,10},{3,11},{4,12},{5,13},{6,14},{7,15},{8,0},{9,1},... | collective-permute-start | bytes 2654216 | tf_op jit(solution)/shard_map/ppermute | solution.py:37
  80.0 1.6 %shard_map.96.refs_0_ = f32[4,768,256]{2,1,0:T(8,128)S(1)} custom-call(s32[26]{0:T(128)S(1)} %stack.123.numbers, bf16[3,384,256]{2,1,0:T(8,128)(2,1)S(1)} %shard_map.90.mine, bf16[3,384,256]{2,1,0:T(8,128)(2,1)S(1)} %collective-permute-done.11.theirs, bf16[768,256]{1,0:T(8,128)(2,1)S(1)} %get-tuple-element.85.own, ...), custom_call_target="tpu_custom_call" | custom-call | flops 1100000000 | bytes 1000 | tf_op jit(solution)/shard_map/pallas_call | solution.py:69
  81.8 1.4 shard_map.98
  84.1 0.8 collective-permute-done.27.refs_0_
  85.0 1.6 %collective-permute-start.31 = (bf16[768,256]{1,0:T(8,128)(2,1)S(1)}, bf16[768,256]{1,0:T(8,128)(2,1)S(1)}, u32[]{:S(2)}, u32[]{:S(2)}) collective-permute-start(bf16[768,256]{1,0:T(8,128)(2,1)S(1)} %get-tuple-element.121), channel_id=1, source_target_pairs={{0,96},{1,97},{2,98},{3,99},{4,100},{5,101},{6,102},{7,103},{8,104... | collective-permute-start | bytes 1179656 | tf_op jit(solution)/shard_map/ppermute | solution.py:37
  86.7 1.6 %collective-permute-start.34 = (bf16[3,384,256]{2,1,0:T(8,128)(2,1)S(1)}, bf16[3,384,256]{2,1,0:T(8,128)(2,1)S(1)}, u32[]{:S(2)}, u32[]{:S(2)}) collective-permute-start(bf16[3,384,256]{2,1,0:T(8,128)(2,1)S(1)} %shard_map.100), channel_id=1, source_target_pairs={{0,16},{1,17},{2,18},{3,19},{4,20},{5,21},{6,22},{7,23},{8,24},{9,... | collective-permute-start | bytes 1769480 | tf_op jit(solution)/shard_map/ppermute | solution.py:37
  88.2 2.7 %shard_map.101 = (f32[768,384]{1,0:T(8,128)S(1)}, f32[768,384]{1,0:T(8,128)S(1)}, bf16[384,384]{1,0:T(8,128)(2,1)S(1)}, bf16[384,384]{1,0:T(8,128)(2,1)S(1)}, f32[768,384]{1,0:T(8,128)S(1)}) custom-call(bf16[1024,768]{1,0:T(8,128)(2,1)S(1)} %get-tuple-element.82.tokens, bf16[1024,768]{1,0:T(8,128)(2,1)S(1)} %get-tuple-element.83.cotangents, ...), custom_call_target="tpu_custom_call" | custom-call | flops 1100000000 | bytes 1000 | tf_op jit(solution)/shard_map/pallas_call | solution.py:69
  91.0 2.7 %collective-permute-start.33 = (bf16[384,384]{1,0:T(8,128)(2,1)S(1)}, bf16[384,384]{1,0:T(8,128)(2,1)S(1)}, u32[]{:S(2)}, u32[]{:S(2)}) collective-permute-start(bf16[384,384]{1,0:T(8,128)(2,1)S(1)} %get-tuple-element.125), channel_id=1, source_target_pairs={{0,96},{1,97},{2,98},{3,99},{4,100},{5,101},{6,102},{7,103},{8,104... | collective-permute-start | bytes 884744 | tf_op jit(solution)/shard_map/ppermute | solution.py:37
  93.7 1.8 %collective-permute-done.30.refs_1_ = bf16[768,256]{1,0:T(8,128)(2,1)S(1)} collective-permute-done((bf16[768,256]{1,0:T(8,128)(2,1)S(1)}, bf16[768,256]{1,0:T(8,128)(2,1)S(1)}, u32[]{:S(2)}, u32[]{:S(2)}) %collective-permute-start.30) | collective-permute-done | bytes 393248 | tf_op jit(solution)/shard_map/ppermute | solution.py:37
  95.5 2.6 %shard_map.103.refs_0_ = f32[4,768,256]{2,1,0:T(8,128)S(1)} custom-call(s32[26]{0:T(128)S(1)} %stack.123.numbers, bf16[3,384,384]{2,1,0:T(8,128)(2,1)S(1)} %shard_map.99.mine, bf16[3,384,384]{2,1,0:T(8,128)(2,1)S(1)} %collective-permute-done.26.theirs, bf16[768,384]{1,0:T(8,128)(2,1)S(1)} %get-tuple-element.93.own, ...), custom_call_target="tpu_custom_call" | custom-call | flops 1100000000 | bytes 1000 | tf_op jit(solution)/shard_map/pallas_call | solution.py:69
  98.1 3.6 %collective-permute-done.32.low = bf16[384,384]{1,0:T(8,128)(2,1)S(1)} collective-permute-done((bf16[384,384]{1,0:T(8,128)(2,1)S(1)}, bf16[384,384]{1,0:T(8,128)(2,1)S(1)}, u32[]{:S(2)}, u32[]{:S(2)}) %collective-permute-start.32) | collective-permute-done | bytes 294944 | tf_op jit(solution)/shard_map/ppermute | solution.py:37
  102.5 1.2 collective-permute-start.35
  103.9 2.5 %collective-permute-start.44 = (bf16[768,384]{1,0:T(8,128)(2,1)S(1)}, bf16[768,384]{1,0:T(8,128)(2,1)S(1)}, u32[]{:S(2)}, u32[]{:S(2)}) collective-permute-start(bf16[768,384]{1,0:T(8,128)(2,1)S(1)} %get-tuple-element.139), channel_id=1, source_target_pairs={{0,96},{1,97},{2,98},{3,99},{4,100},{5,101},{6,102},{7,103},{8,104... | collective-permute-start | bytes 1769480 | tf_op jit(solution)/shard_map/ppermute | solution.py:37
  106.4 1.7 %shard_map.105 = (f32[768,256]{1,0:T(8,128)S(1)}, bf16[768,256]{1,0:T(8,128)(2,1)S(1)}, bf16[768,256]{1,0:T(8,128)(2,1)S(1)}, bf16[768,256]{1,0:T(8,128)(2,1)S(1)}) custom-call(s32[26]{0:T(128)S(1)} %stack.123.numbers, bf16[3,384,256]{2,1,0:T(8,128)(2,1)S(1)} %shard_map.104.mine, bf16[3,384,256]{2,1,0:T(8,128)(2,1)S(1)} %collective-permute-done.35.theirs, ...), custom_call_target="tpu_custom_call" | custom-call | flops 1100000000 | bytes 1000 | tf_op jit(solution)/shard_map/pallas_call | solution.py:69
  108.1 1.3 collective-permute-start.36
  109.3 2.4 %collective-permute-start.37 = (bf16[768,256]{1,0:T(8,128)(2,1)S(1)}, bf16[768,256]{1,0:T(8,128)(2,1)S(1)}, u32[]{:S(2)}, u32[]{:S(2)}) collective-permute-start(bf16[768,256]{1,0:T(8,128)(2,1)S(1)} %get-tuple-element.131), channel_id=1, source_target_pairs={{0,4},{1,5},{2,6},{3,7},{4,0},{5,1},{6,2},{7,3},{8,12},{9,13},{10,... | collective-permute-start | bytes 1179656 | tf_op jit(solution)/shard_map/ppermute | solution.py:37
  111.8 1.2 collective-permute-start.38
  112.9 1.4 shard_map.108
  114.3 5.5 %collective-permute-done.43.refs_4_ = bf16[768,384]{1,0:T(8,128)(2,1)S(1)} collective-permute-done((bf16[768,384]{1,0:T(8,128)(2,1)S(1)}, bf16[768,384]{1,0:T(8,128)(2,1)S(1)}, u32[]{:S(2)}, u32[]{:S(2)}) %collective-permute-start.43) | collective-permute-done | bytes 589856 | tf_op jit(solution)/shard_map/ppermute | solution.py:37
  119.8 2.7 %collective-permute-start.46 = (bf16[384,256]{1,0:T(8,128)(2,1)S(1)}, bf16[384,256]{1,0:T(8,128)(2,1)S(1)}, u32[]{:S(2)}, u32[]{:S(2)}) collective-permute-start(bf16[384,256]{1,0:T(8,128)(2,1)S(1)} %get-tuple-element.146), channel_id=1, source_target_pairs={{0,96},{1,97},{2,98},{3,99},{4,100},{5,101},{6,102},{7,103},{8,104... | collective-permute-start | bytes 589832 | tf_op jit(solution)/shard_map/ppermute | solution.py:37
  122.5 6.3 %collective-permute-done.37.r2 = bf16[768,256]{1,0:T(8,128)(2,1)S(1)} collective-permute-done((bf16[768,256]{1,0:T(8,128)(2,1)S(1)}, bf16[768,256]{1,0:T(8,128)(2,1)S(1)}, u32[]{:S(2)}, u32[]{:S(2)}) %collective-permute-start.37) | collective-permute-done | bytes 393248 | tf_op jit(solution)/shard_map/ppermute | solution.py:37
  128.8 0.7 shard_map.106
  129.5 0.7 collective-permute-start.39
  130.4 2.7 %collective-permute-start.48 = (bf16[768,256]{1,0:T(8,128)(2,1)S(1)}, bf16[768,256]{1,0:T(8,128)(2,1)S(1)}, u32[]{:S(2)}, u32[]{:S(2)}) collective-permute-start(bf16[768,256]{1,0:T(8,128)(2,1)S(1)} %get-tuple-element.148), channel_id=1, source_target_pairs={{0,96},{1,97},{2,98},{3,99},{4,100},{5,101},{6,102},{7,103},{8,104... | collective-permute-start | bytes 1179656 | tf_op jit(solution)/shard_map/ppermute | solution.py:37
  133.1 3.8 %collective-permute-start.40 = (f32[192,256]{1,0:T(8,128)S(1)}, f32[192,256]{1,0:T(8,128)S(1)}, u32[]{:S(2)}, u32[]{:S(2)}) collective-permute-start(f32[192,256]{1,0:T(8,128)S(1)} %get-tuple-element.134), channel_id=1, source_target_pairs={{0,16},{1,0},{2,18},{3,2},{4,20},{5,4},{6,22},{7,6},{8,24},{9,8},{... | collective-permute-start | bytes 589832 | tf_op jit(solution)/shard_map/ppermute | solution.py:37
  136.9 2.6 %collective-permute-start.41 = (f32[192,256]{1,0:T(8,128)S(1)}, f32[192,256]{1,0:T(8,128)S(1)}, u32[]{:S(2)}, u32[]{:S(2)}) collective-permute-start(f32[192,256]{1,0:T(8,128)S(1)} %get-tuple-element.135), channel_id=1, source_target_pairs={{0,8},{1,24},{2,10},{3,26},{4,12},{5,28},{6,14},{7,30},{8,0},{9,16... | collective-permute-start | bytes 589832 | tf_op jit(solution)/shard_map/ppermute | solution.py:37
  139.5 0.6 collective-permute-start.42
  140.1 0.5 collective-permute-done.40.a1
  140.6 6.9 %collective-permute-done.42.b1 = f32[192,256]{1,0:T(8,128)S(1)} collective-permute-done((f32[192,256]{1,0:T(8,128)S(1)}, f32[192,256]{1,0:T(8,128)S(1)}, u32[]{:S(2)}, u32[]{:S(2)}) %collective-permute-start.42) | collective-permute-done | bytes 196640 | tf_op jit(solution)/shard_map/ppermute | solution.py:37
  147.5 1.3 shard_map.107
  148.9 1.8 %shard_map.110 = (f32[256,896]{1,0:T(8,128)}, f32[256,896]{1,0:T(8,128)}, f32[256,896]{1,0:T(8,128)}) custom-call(f32[768,256]{1,0:T(8,128)S(1)} %get-tuple-element.137.refs_0_, bf16[768,256]{1,0:T(8,128)(2,1)S(1)} %collective-permute-done.30.refs_1_, bf16[768,256]{1,0:T(8,128)(2,1)S(1)} %collective-permute-done.31.refs_2_, ...), custom_call_target="tpu_custom_call" | custom-call | flops 1100000000 | bytes 1000 | tf_op jit(solution)/shard_map/pallas_call | solution.py:69
  (62 shorter events, 5.7 us)
Async XLA Ops:
  2.1 13.6 %collective-permute-start.3 = (bf16[768,256]{1,0:T(8,128)(2,1)S(1)}, bf16[768,256]{1,0:T(8,128)(2,1)S(1)}, u32[]{:S(2)}, u32[]{:S(2)}) collective-permute-start(bf16[768,256]{1,0:T(8,128)(2,1)S(1)} %get-tuple-element.85.own), channel_id=1, source_target_pairs={{0,96},{1,97},{2,98},{3,99},{4,100},{5,101},{6,102},{7,103},{8,104... | collective-permute-start | bytes 1179656 | tf_op jit(solution)/shard_map/ppermute | solution.py:37
  6.8 10.9 %collective-permute-start.4 = (bf16[768,256]{1,0:T(8,128)(2,1)S(1)}, bf16[768,256]{1,0:T(8,128)(2,1)S(1)}, u32[]{:S(2)}, u32[]{:S(2)}) collective-permute-start(bf16[768,256]{1,0:T(8,128)(2,1)S(1)} %get-tuple-element.85.own), channel_id=1, source_target_pairs={{0,32},{1,33},{2,34},{3,35},{4,36},{5,37},{6,38},{7,39},{8,40},{9,... | collective-permute-start | bytes 1179656 | tf_op jit(solution)/shard_map/ppermute | solution.py:37
  11.3 18.2 %collective-permute-start = (bf16[2,4,192,256]{3,2,1,0:T(8,128)(2,1)S(1)}, bf16[2,4,192,256]{3,2,1,0:T(8,128)(2,1)S(1)}, u32[]{:S(2)}, u32[]{:S(2)}) collective-permute-start(bf16[2,4,192,256]{3,2,1,0:T(8,128)(2,1)S(1)} %get-tuple-element.79), channel_id=1, source_target_pairs={{0,16},{1,17},{2,18},{3,19},{4,20},{5,21},{6,22},{7,23},{8,24},{9,... | collective-permute-start | bytes 2359304 | tf_op jit(solution)/shard_map/ppermute | solution.py:37
  12.7 16.8 %collective-permute-start.1 = (bf16[2,4,192,256]{3,2,1,0:T(8,128)(2,1)S(1)}, bf16[2,4,192,256]{3,2,1,0:T(8,128)(2,1)S(1)}, u32[]{:S(2)}, u32[]{:S(2)}) collective-permute-start(bf16[2,4,192,256]{3,2,1,0:T(8,128)(2,1)S(1)} %get-tuple-element.80), channel_id=1, source_target_pairs={{0,8},{1,9},{2,10},{3,11},{4,12},{5,13},{6,14},{7,15},{8,0},{9,1},... | collective-permute-start | bytes 2359304 | tf_op jit(solution)/shard_map/ppermute | solution.py:37
  13.9 20.7 %collective-permute-start.2 = (bf16[2,4,192,256]{3,2,1,0:T(8,128)(2,1)S(1)}, bf16[2,4,192,256]{3,2,1,0:T(8,128)(2,1)S(1)}, u32[]{:S(2)}, u32[]{:S(2)}) collective-permute-start(bf16[2,4,192,256]{3,2,1,0:T(8,128)(2,1)S(1)} %get-tuple-element.81), channel_id=1, source_target_pairs={{0,25},{1,24},{2,27},{3,26},{4,29},{5,28},{6,31},{7,30},{8,17},{9,... | collective-permute-start | bytes 2359304 | tf_op jit(solution)/shard_map/ppermute | solution.py:37
  17.7 4.9 %collective-permute-start.5 = (bf16[384,256]{1,0:T(8,128)(2,1)S(1)}, bf16[384,256]{1,0:T(8,128)(2,1)S(1)}, u32[]{:S(2)}, u32[]{:S(2)}) collective-permute-start(bf16[384,256]{1,0:T(8,128)(2,1)S(1)} %get-tuple-element.86), channel_id=1, source_target_pairs={{0,96},{1,97},{2,98},{3,99},{4,100},{5,101},{6,102},{7,103},{8,104... | collective-permute-start | bytes 589832 | tf_op jit(solution)/shard_map/ppermute | solution.py:37
  18.8 6.8 %collective-permute-start.6 = (bf16[384,256]{1,0:T(8,128)(2,1)S(1)}, bf16[384,256]{1,0:T(8,128)(2,1)S(1)}, u32[]{:S(2)}, u32[]{:S(2)}) collective-permute-start(bf16[384,256]{1,0:T(8,128)(2,1)S(1)} %get-tuple-element.87), channel_id=1, source_target_pairs={{0,32},{1,33},{2,34},{3,35},{4,36},{5,37},{6,38},{7,39},{8,40},{9,... | collective-permute-start | bytes 589832 | tf_op jit(solution)/shard_map/ppermute | solution.py:37
  22.6 14.1 %collective-permute-start.12 = (bf16[768,384]{1,0:T(8,128)(2,1)S(1)}, bf16[768,384]{1,0:T(8,128)(2,1)S(1)}, u32[]{:S(2)}, u32[]{:S(2)}) collective-permute-start(bf16[768,384]{1,0:T(8,128)(2,1)S(1)} %get-tuple-element.93.own), channel_id=1, source_target_pairs={{0,96},{1,97},{2,98},{3,99},{4,100},{5,101},{6,102},{7,103},{8,104... | collective-permute-start | bytes 1769480 | tf_op jit(solution)/shard_map/ppermute | solution.py:37
  25.5 14.0 %collective-permute-start.13 = (bf16[768,384]{1,0:T(8,128)(2,1)S(1)}, bf16[768,384]{1,0:T(8,128)(2,1)S(1)}, u32[]{:S(2)}, u32[]{:S(2)}) collective-permute-start(bf16[768,384]{1,0:T(8,128)(2,1)S(1)} %get-tuple-element.93.own), channel_id=1, source_target_pairs={{0,32},{1,33},{2,34},{3,35},{4,36},{5,37},{6,38},{7,39},{8,40},{9,... | collective-permute-start | bytes 1769480 | tf_op jit(solution)/shard_map/ppermute | solution.py:37
  36.0 6.0 %collective-permute-start.7 = (f32[1,384,256]{2,1,0:T(8,128)S(1)}, f32[1,384,256]{2,1,0:T(8,128)S(1)}, u32[]{:S(2)}, u32[]{:S(2)}) collective-permute-start(f32[1,384,256]{2,1,0:T(8,128)S(1)} %get-tuple-element.89), channel_id=1, source_target_pairs={{0,8},{1,9},{2,10},{3,11},{4,12},{5,13},{6,14},{7,15},{8,0},{9,1},... | collective-permute-start | bytes 1179656 | tf_op jit(solution)/shard_map/ppermute | solution.py:37
  36.1 5.9 %collective-permute-start.8 = (f32[1,384,256]{2,1,0:T(8,128)S(1)}, f32[1,384,256]{2,1,0:T(8,128)S(1)}, u32[]{:S(2)}, u32[]{:S(2)}) collective-permute-start(f32[1,384,256]{2,1,0:T(8,128)S(1)} %get-tuple-element.90), channel_id=1, source_target_pairs={{0,8},{1,9},{2,10},{3,11},{4,12},{5,13},{6,14},{7,15},{8,0},{9,1},... | collective-permute-start | bytes 1179656 | tf_op jit(solution)/shard_map/ppermute | solution.py:37
  36.6 5.4 %collective-permute-start.9 = (f32[1,384,256]{2,1,0:T(8,128)S(1)}, f32[1,384,256]{2,1,0:T(8,128)S(1)}, u32[]{:S(2)}, u32[]{:S(2)}) collective-permute-start(f32[1,384,256]{2,1,0:T(8,128)S(1)} %get-tuple-element.91), channel_id=1, source_target_pairs={{0,8},{1,9},{2,10},{3,11},{4,12},{5,13},{6,14},{7,15},{8,0},{9,1},... | collective-permute-start | bytes 1179656 | tf_op jit(solution)/shard_map/ppermute | solution.py:37
  39.6 5.6 %collective-permute-start.14 = (bf16[384,384]{1,0:T(8,128)(2,1)S(1)}, bf16[384,384]{1,0:T(8,128)(2,1)S(1)}, u32[]{:S(2)}, u32[]{:S(2)}) collective-permute-start(bf16[384,384]{1,0:T(8,128)(2,1)S(1)} %get-tuple-element.94), channel_id=1, source_target_pairs={{0,96},{1,97},{2,98},{3,99},{4,100},{5,101},{6,102},{7,103},{8,104... | collective-permute-start | bytes 884744 | tf_op jit(solution)/shard_map/ppermute | solution.py:37
  39.9 6.8 %collective-permute-start.15 = (bf16[384,384]{1,0:T(8,128)(2,1)S(1)}, bf16[384,384]{1,0:T(8,128)(2,1)S(1)}, u32[]{:S(2)}, u32[]{:S(2)}) collective-permute-start(bf16[384,384]{1,0:T(8,128)(2,1)S(1)} %get-tuple-element.95), channel_id=1, source_target_pairs={{0,32},{1,33},{2,34},{3,35},{4,36},{5,37},{6,38},{7,39},{8,40},{9,... | collective-permute-start | bytes 884744 | tf_op jit(solution)/shard_map/ppermute | solution.py:37
  42.1 12.0 %collective-permute-start.10 = (bf16[3,384,256]{2,1,0:T(8,128)(2,1)S(1)}, bf16[3,384,256]{2,1,0:T(8,128)(2,1)S(1)}, u32[]{:S(2)}, u32[]{:S(2)}) collective-permute-start(bf16[3,384,256]{2,1,0:T(8,128)(2,1)S(1)} %shard_map.89), channel_id=1, source_target_pairs={{0,16},{1,17},{2,18},{3,19},{4,20},{5,21},{6,22},{7,23},{8,24},{9,... | collective-permute-start | bytes 1769480 | tf_op jit(solution)/shard_map/ppermute | solution.py:37
  49.5 5.8 %collective-permute-start.16 = (f32[1,384,384]{2,1,0:T(8,128)S(1)}, f32[1,384,384]{2,1,0:T(8,128)S(1)}, u32[]{:S(2)}, u32[]{:S(2)}) collective-permute-start(f32[1,384,384]{2,1,0:T(8,128)S(1)} %get-tuple-element.98), channel_id=1, source_target_pairs={{0,8},{1,9},{2,10},{3,11},{4,12},{5,13},{6,14},{7,15},{8,0},{9,1},... | collective-permute-start | bytes 1769480 | tf_op jit(solution)/shard_map/ppermute | solution.py:37
  53.7 2.5 %collective-permute-start.17 = (f32[1,384,384]{2,1,0:T(8,128)S(1)}, f32[1,384,384]{2,1,0:T(8,128)S(1)}, u32[]{:S(2)}, u32[]{:S(2)}) collective-permute-start(f32[1,384,384]{2,1,0:T(8,128)S(1)} %get-tuple-element.99), channel_id=1, source_target_pairs={{0,8},{1,9},{2,10},{3,11},{4,12},{5,13},{6,14},{7,15},{8,0},{9,1},... | collective-permute-start | bytes 1769480 | tf_op jit(solution)/shard_map/ppermute | solution.py:37
  53.7 3.2 %collective-permute-start.18 = (f32[1,384,384]{2,1,0:T(8,128)S(1)}, f32[1,384,384]{2,1,0:T(8,128)S(1)}, u32[]{:S(2)}, u32[]{:S(2)}) collective-permute-start(f32[1,384,384]{2,1,0:T(8,128)S(1)} %get-tuple-element.100), channel_id=1, source_target_pairs={{0,8},{1,9},{2,10},{3,11},{4,12},{5,13},{6,14},{7,15},{8,0},{9,1},... | collective-permute-start | bytes 1769480 | tf_op jit(solution)/shard_map/ppermute | solution.py:37
  57.1 20.2 %collective-permute-start.25 = (bf16[3,384,384]{2,1,0:T(8,128)(2,1)S(1)}, bf16[3,384,384]{2,1,0:T(8,128)(2,1)S(1)}, u32[]{:S(2)}, u32[]{:S(2)}) collective-permute-start(bf16[3,384,384]{2,1,0:T(8,128)(2,1)S(1)} %shard_map.93), channel_id=1, source_target_pairs={{0,16},{1,17},{2,18},{3,19},{4,20},{5,21},{6,22},{7,23},{8,24},{9,... | collective-permute-start | bytes 2654216 | tf_op jit(solution)/shard_map/ppermute | solution.py:37
  57.7 3.2 %collective-permute-start.11 = (bf16[3,384,256]{2,1,0:T(8,128)(2,1)S(1)}, bf16[3,384,256]{2,1,0:T(8,128)(2,1)S(1)}, u32[]{:S(2)}, u32[]{:S(2)}) collective-permute-start(bf16[3,384,256]{2,1,0:T(8,128)(2,1)S(1)} %shard_map.90.mine), channel_id=1, source_target_pairs={{0,8},{1,9},{2,10},{3,11},{4,12},{5,13},{6,14},{7,15},{8,0},{9,1},... | collective-permute-start | bytes 1769480 | tf_op jit(solution)/shard_map/ppermute | solution.py:37
  59.2 10.7 %collective-permute-start.21 = (bf16[768,256]{1,0:T(8,128)(2,1)S(1)}, bf16[768,256]{1,0:T(8,128)(2,1)S(1)}, u32[]{:S(2)}, u32[]{:S(2)}) collective-permute-start(bf16[768,256]{1,0:T(8,128)(2,1)S(1)} %get-tuple-element.110.own), channel_id=1, source_target_pairs={{0,96},{1,97},{2,98},{3,99},{4,100},{5,101},{6,102},{7,103},{8,104... | collective-permute-start | bytes 1179656 | tf_op jit(solution)/shard_map/ppermute | solution.py:37
  60.7 11.6 %collective-permute-start.22 = (bf16[768,256]{1,0:T(8,128)(2,1)S(1)}, bf16[768,256]{1,0:T(8,128)(2,1)S(1)}, u32[]{:S(2)}, u32[]{:S(2)}) collective-permute-start(bf16[768,256]{1,0:T(8,128)(2,1)S(1)} %get-tuple-element.110.own), channel_id=1, source_target_pairs={{0,32},{1,33},{2,34},{3,35},{4,36},{5,37},{6,38},{7,39},{8,40},{9,... | collective-permute-start | bytes 1179656 | tf_op jit(solution)/shard_map/ppermute | solution.py:37
  62.3 19.4 %collective-permute-start.19 = (bf16[384,256]{1,0:T(8,128)(2,1)S(1)}, bf16[384,256]{1,0:T(8,128)(2,1)S(1)}, u32[]{:S(2)}, u32[]{:S(2)}) collective-permute-start(bf16[384,256]{1,0:T(8,128)(2,1)S(1)} %get-tuple-element.104), channel_id=1, source_target_pairs={{0,32},{1,33},{2,34},{3,35},{4,36},{5,37},{6,38},{7,39},{8,40},{9,... | collective-permute-start | bytes 589832 | tf_op jit(solution)/shard_map/ppermute | solution.py:37
  62.3 19.3 %collective-permute-start.20 = (bf16[384,256]{1,0:T(8,128)(2,1)S(1)}, bf16[384,256]{1,0:T(8,128)(2,1)S(1)}, u32[]{:S(2)}, u32[]{:S(2)}) collective-permute-start(bf16[384,256]{1,0:T(8,128)(2,1)S(1)} %get-tuple-element.105), channel_id=1, source_target_pairs={{0,96},{1,97},{2,98},{3,99},{4,100},{5,101},{6,102},{7,103},{8,104... | collective-permute-start | bytes 589832 | tf_op jit(solution)/shard_map/ppermute | solution.py:37
  72.3 9.4 %collective-permute-start.23 = (bf16[384,256]{1,0:T(8,128)(2,1)S(1)}, bf16[384,256]{1,0:T(8,128)(2,1)S(1)}, u32[]{:S(2)}, u32[]{:S(2)}) collective-permute-start(bf16[384,256]{1,0:T(8,128)(2,1)S(1)} %get-tuple-element.112), channel_id=1, source_target_pairs={{0,96},{1,97},{2,98},{3,99},{4,100},{5,101},{6,102},{7,103},{8,104... | collective-permute-start | bytes 589832 | tf_op jit(solution)/shard_map/ppermute | solution.py:37
  72.7 9.0 %collective-permute-start.24 = (bf16[384,256]{1,0:T(8,128)(2,1)S(1)}, bf16[384,256]{1,0:T(8,128)(2,1)S(1)}, u32[]{:S(2)}, u32[]{:S(2)}) collective-permute-start(bf16[384,256]{1,0:T(8,128)(2,1)S(1)} %get-tuple-element.113), channel_id=1, source_target_pairs={{0,32},{1,33},{2,34},{3,35},{4,36},{5,37},{6,38},{7,39},{8,40},{9,... | collective-permute-start | bytes 589832 | tf_op jit(solution)/shard_map/ppermute | solution.py:37
  78.0 10.3 %collective-permute-start.26 = (bf16[3,384,384]{2,1,0:T(8,128)(2,1)S(1)}, bf16[3,384,384]{2,1,0:T(8,128)(2,1)S(1)}, u32[]{:S(2)}, u32[]{:S(2)}) collective-permute-start(bf16[3,384,384]{2,1,0:T(8,128)(2,1)S(1)} %shard_map.99.mine), channel_id=1, source_target_pairs={{0,8},{1,9},{2,10},{3,11},{4,12},{5,13},{6,14},{7,15},{8,0},{9,1},... | collective-permute-start | bytes 2654216 | tf_op jit(solution)/shard_map/ppermute | solution.py:37
  83.2 1.8 %collective-permute-start.27 = (f32[1,384,256]{2,1,0:T(8,128)S(1)}, f32[1,384,256]{2,1,0:T(8,128)S(1)}, u32[]{:S(2)}, u32[]{:S(2)}) collective-permute-start(f32[1,384,256]{2,1,0:T(8,128)S(1)} %get-tuple-element.116), channel_id=1, source_target_pairs={{0,8},{1,9},{2,10},{3,11},{4,12},{5,13},{6,14},{7,15},{8,0},{9,1},... | collective-permute-start | bytes 1179656 | tf_op jit(solution)/shard_map/ppermute | solution.py:37
  83.4 3.2 %collective-permute-start.28 = (f32[1,384,256]{2,1,0:T(8,128)S(1)}, f32[1,384,256]{2,1,0:T(8,128)S(1)}, u32[]{:S(2)}, u32[]{:S(2)}) collective-permute-start(f32[1,384,256]{2,1,0:T(8,128)S(1)} %get-tuple-element.117), channel_id=1, source_target_pairs={{0,8},{1,9},{2,10},{3,11},{4,12},{5,13},{6,14},{7,15},{8,0},{9,1},... | collective-permute-start | bytes 1179656 | tf_op jit(solution)/shard_map/ppermute | solution.py:37
  83.8 2.8 %collective-permute-start.29 = (f32[1,384,256]{2,1,0:T(8,128)S(1)}, f32[1,384,256]{2,1,0:T(8,128)S(1)}, u32[]{:S(2)}, u32[]{:S(2)}) collective-permute-start(f32[1,384,256]{2,1,0:T(8,128)S(1)} %get-tuple-element.118), channel_id=1, source_target_pairs={{0,8},{1,9},{2,10},{3,11},{4,12},{5,13},{6,14},{7,15},{8,0},{9,1},... | collective-permute-start | bytes 1179656 | tf_op jit(solution)/shard_map/ppermute | solution.py:37
  83.9 11.5 %collective-permute-start.30 = (bf16[768,256]{1,0:T(8,128)(2,1)S(1)}, bf16[768,256]{1,0:T(8,128)(2,1)S(1)}, u32[]{:S(2)}, u32[]{:S(2)}) collective-permute-start(bf16[768,256]{1,0:T(8,128)(2,1)S(1)} %get-tuple-element.106), channel_id=1, source_target_pairs={{0,32},{1,33},{2,34},{3,35},{4,36},{5,37},{6,38},{7,39},{8,40},{9,... | collective-permute-start | bytes 1179656 | tf_op jit(solution)/shard_map/ppermute | solution.py:37
  85.0 10.6 %collective-permute-start.31 = (bf16[768,256]{1,0:T(8,128)(2,1)S(1)}, bf16[768,256]{1,0:T(8,128)(2,1)S(1)}, u32[]{:S(2)}, u32[]{:S(2)}) collective-permute-start(bf16[768,256]{1,0:T(8,128)(2,1)S(1)} %get-tuple-element.121), channel_id=1, source_target_pairs={{0,96},{1,97},{2,98},{3,99},{4,100},{5,101},{6,102},{7,103},{8,104... | collective-permute-start | bytes 1179656 | tf_op jit(solution)/shard_map/ppermute | solution.py:37
  86.7 15.3 %collective-permute-start.34 = (bf16[3,384,256]{2,1,0:T(8,128)(2,1)S(1)}, bf16[3,384,256]{2,1,0:T(8,128)(2,1)S(1)}, u32[]{:S(2)}, u32[]{:S(2)}) collective-permute-start(bf16[3,384,256]{2,1,0:T(8,128)(2,1)S(1)} %shard_map.100), channel_id=1, source_target_pairs={{0,16},{1,17},{2,18},{3,19},{4,20},{5,21},{6,22},{7,23},{8,24},{9,... | collective-permute-start | bytes 1769480 | tf_op jit(solution)/shard_map/ppermute | solution.py:37
  90.9 10.8 %collective-permute-start.32 = (bf16[384,384]{1,0:T(8,128)(2,1)S(1)}, bf16[384,384]{1,0:T(8,128)(2,1)S(1)}, u32[]{:S(2)}, u32[]{:S(2)}) collective-permute-start(bf16[384,384]{1,0:T(8,128)(2,1)S(1)} %get-tuple-element.124), channel_id=1, source_target_pairs={{0,32},{1,33},{2,34},{3,35},{4,36},{5,37},{6,38},{7,39},{8,40},{9,... | collective-permute-start | bytes 884744 | tf_op jit(solution)/shard_map/ppermute | solution.py:37
  91.0 10.9 %collective-permute-start.33 = (bf16[384,384]{1,0:T(8,128)(2,1)S(1)}, bf16[384,384]{1,0:T(8,128)(2,1)S(1)}, u32[]{:S(2)}, u32[]{:S(2)}) collective-permute-start(bf16[384,384]{1,0:T(8,128)(2,1)S(1)} %get-tuple-element.125), channel_id=1, source_target_pairs={{0,96},{1,97},{2,98},{3,99},{4,100},{5,101},{6,102},{7,103},{8,104... | collective-permute-start | bytes 884744 | tf_op jit(solution)/shard_map/ppermute | solution.py:37
  102.5 3.9 %collective-permute-start.35 = (bf16[3,384,256]{2,1,0:T(8,128)(2,1)S(1)}, bf16[3,384,256]{2,1,0:T(8,128)(2,1)S(1)}, u32[]{:S(2)}, u32[]{:S(2)}) collective-permute-start(bf16[3,384,256]{2,1,0:T(8,128)(2,1)S(1)} %shard_map.104.mine), channel_id=1, source_target_pairs={{0,8},{1,9},{2,10},{3,11},{4,12},{5,13},{6,14},{7,15},{8,0},{9,1},... | collective-permute-start | bytes 1769480 | tf_op jit(solution)/shard_map/ppermute | solution.py:37
  103.7 16.1 %collective-permute-start.43 = (bf16[768,384]{1,0:T(8,128)(2,1)S(1)}, bf16[768,384]{1,0:T(8,128)(2,1)S(1)}, u32[]{:S(2)}, u32[]{:S(2)}) collective-permute-start(bf16[768,384]{1,0:T(8,128)(2,1)S(1)} %get-tuple-element.126), channel_id=1, source_target_pairs={{0,32},{1,33},{2,34},{3,35},{4,36},{5,37},{6,38},{7,39},{8,40},{9,... | collective-permute-start | bytes 1769480 | tf_op jit(solution)/shard_map/ppermute | solution.py:37
  103.9 16.0 %collective-permute-start.44 = (bf16[768,384]{1,0:T(8,128)(2,1)S(1)}, bf16[768,384]{1,0:T(8,128)(2,1)S(1)}, u32[]{:S(2)}, u32[]{:S(2)}) collective-permute-start(bf16[768,384]{1,0:T(8,128)(2,1)S(1)} %get-tuple-element.139), channel_id=1, source_target_pairs={{0,96},{1,97},{2,98},{3,99},{4,100},{5,101},{6,102},{7,103},{8,104... | collective-permute-start | bytes 1769480 | tf_op jit(solution)/shard_map/ppermute | solution.py:37
  108.1 14.4 %collective-permute-start.36 = (bf16[768,256]{1,0:T(8,128)(2,1)S(1)}, bf16[768,256]{1,0:T(8,128)(2,1)S(1)}, u32[]{:S(2)}, u32[]{:S(2)}) collective-permute-start(bf16[768,256]{1,0:T(8,128)(2,1)S(1)} %get-tuple-element.130), channel_id=1, source_target_pairs={{0,2},{1,3},{2,4},{3,5},{4,6},{5,7},{6,0},{7,1},{8,10},{9,11},{10,... | collective-permute-start | bytes 1179656 | tf_op jit(solution)/shard_map/ppermute | solution.py:37
  109.3 19.4 %collective-permute-start.37 = (bf16[768,256]{1,0:T(8,128)(2,1)S(1)}, bf16[768,256]{1,0:T(8,128)(2,1)S(1)}, u32[]{:S(2)}, u32[]{:S(2)}) collective-permute-start(bf16[768,256]{1,0:T(8,128)(2,1)S(1)} %get-tuple-element.131), channel_id=1, source_target_pairs={{0,4},{1,5},{2,6},{3,7},{4,0},{5,1},{6,2},{7,3},{8,12},{9,13},{10,... | collective-permute-start | bytes 1179656 | tf_op jit(solution)/shard_map/ppermute | solution.py:37
  111.8 17.0 %collective-permute-start.38 = (bf16[768,256]{1,0:T(8,128)(2,1)S(1)}, bf16[768,256]{1,0:T(8,128)(2,1)S(1)}, u32[]{:S(2)}, u32[]{:S(2)}) collective-permute-start(bf16[768,256]{1,0:T(8,128)(2,1)S(1)} %get-tuple-element.132), channel_id=1, source_target_pairs={{0,6},{1,7},{2,0},{3,1},{4,2},{5,3},{6,4},{7,5},{8,14},{9,15},{10,... | collective-permute-start | bytes 1179656 | tf_op jit(solution)/shard_map/ppermute | solution.py:37
  119.8 10.4 %collective-permute-start.45 = (bf16[384,256]{1,0:T(8,128)(2,1)S(1)}, bf16[384,256]{1,0:T(8,128)(2,1)S(1)}, u32[]{:S(2)}, u32[]{:S(2)}) collective-permute-start(bf16[384,256]{1,0:T(8,128)(2,1)S(1)} %get-tuple-element.145), channel_id=1, source_target_pairs={{0,32},{1,33},{2,34},{3,35},{4,36},{5,37},{6,38},{7,39},{8,40},{9,... | collective-permute-start | bytes 589832 | tf_op jit(solution)/shard_map/ppermute | solution.py:37
  119.8 10.4 %collective-permute-start.46 = (bf16[384,256]{1,0:T(8,128)(2,1)S(1)}, bf16[384,256]{1,0:T(8,128)(2,1)S(1)}, u32[]{:S(2)}, u32[]{:S(2)}) collective-permute-start(bf16[384,256]{1,0:T(8,128)(2,1)S(1)} %get-tuple-element.146), channel_id=1, source_target_pairs={{0,96},{1,97},{2,98},{3,99},{4,100},{5,101},{6,102},{7,103},{8,104... | collective-permute-start | bytes 589832 | tf_op jit(solution)/shard_map/ppermute | solution.py:37
  129.5 10.0 %collective-permute-start.39 = (f32[192,256]{1,0:T(8,128)S(1)}, f32[192,256]{1,0:T(8,128)S(1)}, u32[]{:S(2)}, u32[]{:S(2)}) collective-permute-start(f32[192,256]{1,0:T(8,128)S(1)} %get-tuple-element.133), channel_id=1, source_target_pairs={{0,0},{1,16},{2,2},{3,18},{4,4},{5,20},{6,6},{7,22},{8,8},{9,24},{... | collective-permute-start | bytes 589832 | tf_op jit(solution)/shard_map/ppermute | solution.py:37
  130.3 18.6 %collective-permute-start.47 = (bf16[768,256]{1,0:T(8,128)(2,1)S(1)}, bf16[768,256]{1,0:T(8,128)(2,1)S(1)}, u32[]{:S(2)}, u32[]{:S(2)}) collective-permute-start(bf16[768,256]{1,0:T(8,128)(2,1)S(1)} %get-tuple-element.147), channel_id=1, source_target_pairs={{0,32},{1,33},{2,34},{3,35},{4,36},{5,37},{6,38},{7,39},{8,40},{9,... | collective-permute-start | bytes 1179656 | tf_op jit(solution)/shard_map/ppermute | solution.py:37
  130.4 18.5 %collective-permute-start.48 = (bf16[768,256]{1,0:T(8,128)(2,1)S(1)}, bf16[768,256]{1,0:T(8,128)(2,1)S(1)}, u32[]{:S(2)}, u32[]{:S(2)}) collective-permute-start(bf16[768,256]{1,0:T(8,128)(2,1)S(1)} %get-tuple-element.148), channel_id=1, source_target_pairs={{0,96},{1,97},{2,98},{3,99},{4,100},{5,101},{6,102},{7,103},{8,104... | collective-permute-start | bytes 1179656 | tf_op jit(solution)/shard_map/ppermute | solution.py:37
  133.1 7.6 %collective-permute-start.40 = (f32[192,256]{1,0:T(8,128)S(1)}, f32[192,256]{1,0:T(8,128)S(1)}, u32[]{:S(2)}, u32[]{:S(2)}) collective-permute-start(f32[192,256]{1,0:T(8,128)S(1)} %get-tuple-element.134), channel_id=1, source_target_pairs={{0,16},{1,0},{2,18},{3,2},{4,20},{5,4},{6,22},{7,6},{8,24},{9,8},{... | collective-permute-start | bytes 589832 | tf_op jit(solution)/shard_map/ppermute | solution.py:37
  136.9 3.7 %collective-permute-start.41 = (f32[192,256]{1,0:T(8,128)S(1)}, f32[192,256]{1,0:T(8,128)S(1)}, u32[]{:S(2)}, u32[]{:S(2)}) collective-permute-start(f32[192,256]{1,0:T(8,128)S(1)} %get-tuple-element.135), channel_id=1, source_target_pairs={{0,8},{1,24},{2,10},{3,26},{4,12},{5,28},{6,14},{7,30},{8,0},{9,16... | collective-permute-start | bytes 589832 | tf_op jit(solution)/shard_map/ppermute | solution.py:37
  139.5 8.0 %collective-permute-start.42 = (f32[192,256]{1,0:T(8,128)S(1)}, f32[192,256]{1,0:T(8,128)S(1)}, u32[]{:S(2)}, u32[]{:S(2)}) collective-permute-start(f32[192,256]{1,0:T(8,128)S(1)} %get-tuple-element.136), channel_id=1, source_target_pairs={{0,24},{1,8},{2,26},{3,10},{4,28},{5,12},{6,30},{7,14},{8,16},{9,0... | collective-permute-start | bytes 589832 | tf_op jit(solution)/shard_map/ppermute | solution.py:37

commit v5 on v4

--- a/solution.py
+++ b/solution.py
@@ -12,7 +12,8 @@
 BF16 = jnp.bfloat16
 CHUNKS = (256, 384, 256)
 COSTS = {}
-ORDER = {"own1": ["nxt0"], "own2": ["nxt1"], "pre2": ["ahead0", "total0"], "half1": ["other0"], "half2": ["other1"], "grad0": ["sent1"], "grad1": ["sent2"], "delta2": ["ahead1", "total1"], "middle1": ["r10", "r30"], "middle2": ["r11", "r31"], "cut2": ["low0"]}
+MIX = BF16
+ORDER = {"own1": ["nxt0"], "own2": ["nxt1"], "pre2": ["ahead0", "total0"], "half1": ["other0"], "half2": ["other1"], "grad0": ["sent1"], "grad1": ["sent2"], "delta2": ["ahead1", "total1"], "middle1": ["r10", "r30"], "middle2": ["r11", "r31"], "cut2": ["low0"], "cut1": ["turned"], "delta1": ["sent2"]}
 PARTS = 4
 CSPLIT = (1, 1, 1)
 YSPLIT = (3,)
@@ -222,18 +223,21 @@
         for i in range(2):
             block = (i + numbers[24]) % 2
             rows = pl.ds(pl.multiple_of(j * 384 + block * 192, 192), 192)
-            outs[2 * j + i][...] = (
+            total = (
                 own[rows]
                 + r1[rows].astype(F32)
                 + r2[rows].astype(F32)
                 + r3[rows].astype(F32)
             )
+            outs[2 * j + i][...] = total.astype(MIX)
 
 
 def place_kernel(numbers, a0, a1, b0, b1, out):
     for j, (first, second) in enumerate(((a0, a1), (b0, b1))):
         side = (j + numbers[25]) % 2
-        out[:, pl.ds(pl.multiple_of(side * 256, 256), 256)] = first[...] + second[...]
+        out[:, pl.ds(pl.multiple_of(side * 256, 256), 256)] = first[...].astype(
+            F32
+        ) + second[...].astype(F32)
 
 
 def delta_kernel(keep, *refs):
@@ -289,16 +293,34 @@
     behind[384:768] = (b3[384:768] + high[...].astype(F32)).astype(BF16)
 
 
-def finish_kernel(*refs):
-    parts, outs = refs[:-3], refs[-3:]
+def finish_kernel(first, b0, r1, r3, *refs):
+    outs, total, sem = refs[-5:-2], refs[-2], refs[-1]
+    copies = []
     for m, out in enumerate(outs):
         rows = slice(m * 256, (m + 1) * 256)
-        first = 0
-        for i in range(len(parts) // 3):
-            b0, r1, r3 = parts[3 * i : 3 * i + 3]
-            last = first + b0.shape[1]
-            out[:, first:last] = b0[rows] + r1[rows].astype(F32) + r3[rows].astype(F32)
-            first = last
+        total[m] = b0[rows] + r1[rows].astype(F32) + r3[rows].astype(F32)
+        copies.append(
+            pltpu.make_async_copy(
+                total.at[m], out.at[:, pl.ds(first, total.shape[2])], sem.at[m]
+            )
+        )
+        copies[-1].start()
+    for copy in copies:
+        copy.wait()
+
+
+def finish(first, parts, base):
+    width = parts[0].shape[1]
+    return pl.pallas_call(
+        functools.partial(finish_kernel, first),
+        in_specs=[VMEM] * 3 + [HBM] * len(base),
+        out_specs=[HBM] * 3,
+        out_shape=[shape(256, sum(CHUNKS))] * 3,
+        input_output_aliases={3 + m: m for m in range(len(base))},
+        scratch_shapes=[pltpu.VMEM((3, 256, width), F32), pltpu.SemaphoreType.DMA((3,))],
+        compiler_params=PARAMS,
+        cost_estimate=cost("finish"),
+    )(*parts, *base)
 
 
 def input_kernel(last, has_total, numbers, mine, theirs, own, nxt, low, high, prev, *refs):
@@ -357,7 +379,8 @@
     pieces = spread(*arrange(numbers, activations, cotangents))
     turned = local_kernel(turn_kernel, [shape(1024, 768, dtype=BF16)] * 2, "turn", *pieces)
 
-    known, rows, halves = {}, [], []
+    known, rows, halves = {f"t{i}": piece for i, piece in enumerate(pieces)}, [], []
+    known["turned"] = turned[0]
 
     def hold(stage, value):
         names = ORDER.get(stage, ())
@@ -371,7 +394,8 @@
         rows.append(second_step(own, hold(f"cut{i}", nxt), prev))
         if i + 1 < len(CHUNKS):
             near[0] = first_step(hold(f"own{i + 1}", stacks[i + 1]))
-        late = pieces[0] if i == 0 else after(pieces[0], *turned)
+            known[f"nxt{i + 1}"], known[f"prev{i + 1}"] = near[0][1:]
+        late = pieces[0] if i != 1 else after(pieces[0], *turned)
         keep, *send = local_kernel(
             pre_kernel,
             [shape(3, 384, width)] + [shape(count, 384, width) for count in CSPLIT],
@@ -474,7 +498,7 @@
 
     blocks = local_kernel(
         column_kernel,
-        [shape(192, 256)] * 4,
+        [shape(192, 256, dtype=MIX)] * 4,
         "column",
         numbers,
         partial[0],
@@ -494,9 +518,10 @@
     (input_grad,) = local_kernel(
         place_kernel, [shape(192, 512)], "place", numbers, *moved, scalars=1
     )
-    gate_grad, up_grad, down_grad = local_kernel(
-        finish_kernel, [shape(256, sum(CHUNKS))] * 3, "finish", *finished
-    )
+    grads = ()
+    for i in range(len(CHUNKS)):
+        grads = finish(sum(CHUNKS[:i]), finished[3 * i : 3 * i + 3], grads)
+    gate_grad, up_grad, down_grad = grads
     return (input_grad, gate_grad, up_grad, down_grad)
 
 

time: 151 us -> 147 us (0.974)
  waiting for transfers between devices: 61.2 us -> 56.3 us
    ppermute x49, waiting for transfers between devices: 61.2 us -> 56.3 us  [_move(): return lax.ppermute(value, ('dp', 'tensor'), pairs)]
    pallas_call x0 -> x3, Pallas kernels: none -> 2.98 us  [finish(): pl.pallas_call(functools.partial(finish_kernel, first), in_specs=[VMEM] *...]
    pallas_call x25 -> x24, Pallas kernels: 24 us -> 22.2 us  [local_kernel(): pl.pallas_call(kernel, in_specs=[SMEM] * scalars + [VMEM] * (len(args) -...]
  transfers between devices with their start and end apart: 49 -> 49, of which waited for: 23 -> 24; matrix products, arithmetic and copies ran while one was open for 0% -> 0% of each run, Pallas kernels for 17% -> 19%
where the time goes in v5:
time: 147 us
  starting transfers between devices  58.3 us (40%)
  waiting for transfers between devices  56.3 us (38%)
  Pallas kernels  31 us (21%)
    ppermute x49, starting transfers between devices, _move(): return lax.ppermute(value, ('dp', 'tensor'), pairs)  58.3 us
    ppermute x49, waiting for transfers between devices, _move(): return lax.ppermute(value, ('dp', 'tensor'), pairs)  56.3 us
    pallas_call x24, Pallas kernels, local_kernel(): pl.pallas_call(kernel, in_specs=[SMEM] * scalars + [VMEM] * (len(args) -...  22.2 us
    pallas_call x1, Pallas kernels, arrange(): pl.pallas_call(arrange_kernel, in_specs=[SMEM, HBM, HBM], out_specs=[VMEM...  4.4 us
    pallas_call x3, Pallas kernels, finish(): pl.pallas_call(functools.partial(finish_kernel, first), in_specs=[VMEM] *...  2.98 us
  transfers between devices with their start and end apart: 49, of which 24 were waited for; matrix products, arithmetic and copies ran while one was open for 0% of the time, Pallas kernels for 19%

profile of v5, /device:TPU:1, one launch (start us, length us, event | category | flops | bytes accessed | tf_op | source)
XLA Modules:
  0.0 146.9 jit_solution(15670037517847394799)
XLA Ops:
  0.6 1.5 %shard_map.86 = (bf16[768,256]{1,0:T(8,128)(2,1)S(1)}, bf16[768,384]{1,0:T(8,128)(2,1)S(1)}, bf16[768,256]{1,0:T(8,128)(2,1)S(1)}) custom-call(bf16[256,896]{1,0:T(8,128)(2,1)} %refs_0_.1, bf16[256,896]{1,0:T(8,128)(2,1)} %refs_1_.1, bf16[256,896]{1,0:T(8,128)(2,1)} %refs_2_.1), custom_call_target="tpu_custom_call" | custom-call | flops 1100000000 | bytes 1000 | tf_op jit(solution)/shard_map/pallas_call | solution.py:170
  2.1 4.7 %collective-permute-start.3 = (bf16[768,256]{1,0:T(8,128)(2,1)S(1)}, bf16[768,256]{1,0:T(8,128)(2,1)S(1)}, u32[]{:S(2)}, u32[]{:S(2)}) collective-permute-start(bf16[768,256]{1,0:T(8,128)(2,1)S(1)} %get-tuple-element.92.own), channel_id=1, source_target_pairs={{0,96},{1,97},{2,98},{3,99},{4,100},{5,101},{6,102},{7,103},{8,104... | collective-permute-start | bytes 1179656 | tf_op jit(solution)/shard_map/ppermute | solution.py:38
  6.9 4.4 %shard_map.84 = (bf16[2,4,192,256]{3,2,1,0:T(8,128)(2,1)S(1)}, bf16[2,4,192,256]{3,2,1,0:T(8,128)(2,1)S(1)}, bf16[2,4,192,256]{3,2,1,0:T(8,128)(2,1)S(1)}, bf16[2,4,192,256]{3,2,1,0:T(8,128)(2,1)S(1)}) custom-call(s32[26]{0:T(128)S(1)} %stack.123.numbers, bf16[192,4096]{1,0:T(8,128)(2,1)} %activations.1, bf16[4,192,4096]{2,1,0:T(8,128)(2,1)} %cotangents.1), custom_call_target="tpu_custom_call" | custom-call | flops 1100000000 | bytes 1000 | tf_op jit(solution)/shard_map/pallas_call | solution.py:121
  11.3 1.4 collective-permute-start
  12.7 1.2 collective-permute-start.1
  13.9 1.8 %collective-permute-start.2 = (bf16[2,4,192,256]{3,2,1,0:T(8,128)(2,1)S(1)}, bf16[2,4,192,256]{3,2,1,0:T(8,128)(2,1)S(1)}, u32[]{:S(2)}, u32[]{:S(2)}) collective-permute-start(bf16[2,4,192,256]{3,2,1,0:T(8,128)(2,1)S(1)} %get-tuple-element.89), channel_id=1, source_target_pairs={{0,25},{1,24},{2,27},{3,26},{4,29},{5,28},{6,31},{7,30},{8,17},{9,... | collective-permute-start | bytes 2359304 | tf_op jit(solution)/shard_map/ppermute | solution.py:38
  15.7 1.9 %collective-permute-done.4.prev = bf16[768,256]{1,0:T(8,128)(2,1)S(1)} collective-permute-done((bf16[768,256]{1,0:T(8,128)(2,1)S(1)}, bf16[768,256]{1,0:T(8,128)(2,1)S(1)}, u32[]{:S(2)}, u32[]{:S(2)}) %collective-permute-start.4) | collective-permute-done | bytes 393248 | tf_op jit(solution)/shard_map/ppermute | solution.py:38
  17.7 1.1 collective-permute-start.5
  19.2 3.3 %collective-permute-done.5.low = bf16[384,256]{1,0:T(8,128)(2,1)S(1)} collective-permute-done((bf16[384,256]{1,0:T(8,128)(2,1)S(1)}, bf16[384,256]{1,0:T(8,128)(2,1)S(1)}, u32[]{:S(2)}, u32[]{:S(2)}) %collective-permute-start.5) | collective-permute-done | bytes 196640 | tf_op jit(solution)/shard_map/ppermute | solution.py:38
  22.6 3.0 %collective-permute-start.12 = (bf16[768,384]{1,0:T(8,128)(2,1)S(1)}, bf16[768,384]{1,0:T(8,128)(2,1)S(1)}, u32[]{:S(2)}, u32[]{:S(2)}) collective-permute-start(bf16[768,384]{1,0:T(8,128)(2,1)S(1)} %get-tuple-element.101.own), channel_id=1, source_target_pairs={{0,96},{1,97},{2,98},{3,99},{4,100},{5,101},{6,102},{7,103},{8,104... | collective-permute-start | bytes 1769480 | tf_op jit(solution)/shard_map/ppermute | solution.py:38
  25.5 3.9 %collective-permute-done.t1 = bf16[2,4,192,256]{3,2,1,0:T(8,128)(2,1)S(1)} collective-permute-done((bf16[2,4,192,256]{3,2,1,0:T(8,128)(2,1)S(1)}, bf16[2,4,192,256]{3,2,1,0:T(8,128)(2,1)S(1)}, u32[]{:S(2)}, u32[]{:S(2)}) %collective-permute-start) | collective-permute-done | bytes 786464 | tf_op jit(solution)/shard_map/ppermute | solution.py:38
  29.5 5.1 %collective-permute-done.2.t3 = bf16[2,4,192,256]{3,2,1,0:T(8,128)(2,1)S(1)} collective-permute-done((bf16[2,4,192,256]{3,2,1,0:T(8,128)(2,1)S(1)}, bf16[2,4,192,256]{3,2,1,0:T(8,128)(2,1)S(1)}, u32[]{:S(2)}, u32[]{:S(2)}) %collective-permute-start.2) | collective-permute-done | bytes 786464 | tf_op jit(solution)/shard_map/ppermute | solution.py:38
  34.6 1.4 shard_map.88
  36.7 0.9 shard_map.85
  37.8 0.6 collective-permute-done.8.refs_1_
  38.3 0.6 collective-permute-done.9.refs_2_
  39.6 2.6 %collective-permute-start.14 = (bf16[384,384]{1,0:T(8,128)(2,1)S(1)}, bf16[384,384]{1,0:T(8,128)(2,1)S(1)}, u32[]{:S(2)}, u32[]{:S(2)}) collective-permute-start(bf16[384,384]{1,0:T(8,128)(2,1)S(1)} %get-tuple-element.103), channel_id=1, source_target_pairs={{0,96},{1,97},{2,98},{3,99},{4,100},{5,101},{6,102},{7,103},{8,104... | collective-permute-start | bytes 884744 | tf_op jit(solution)/shard_map/ppermute | solution.py:38
  42.2 5.5 %collective-permute-done.14.low = bf16[384,384]{1,0:T(8,128)(2,1)S(1)} collective-permute-done((bf16[384,384]{1,0:T(8,128)(2,1)S(1)}, bf16[384,384]{1,0:T(8,128)(2,1)S(1)}, u32[]{:S(2)}, u32[]{:S(2)}) %collective-permute-start.14) | collective-permute-done | bytes 294944 | tf_op jit(solution)/shard_map/ppermute | solution.py:38
  47.7 3.1 %collective-permute-done.15.high = bf16[384,384]{1,0:T(8,128)(2,1)S(1)} collective-permute-done((bf16[384,384]{1,0:T(8,128)(2,1)S(1)}, bf16[384,384]{1,0:T(8,128)(2,1)S(1)}, u32[]{:S(2)}, u32[]{:S(2)}) %collective-permute-start.15) | collective-permute-done | bytes 294944 | tf_op jit(solution)/shard_map/ppermute | solution.py:38
  50.8 2.7 %shard_map.92 = (f32[3,384,384]{2,1,0:T(8,128)S(1)}, f32[1,384,384]{2,1,0:T(8,128)S(1)}, f32[1,384,384]{2,1,0:T(8,128)S(1)}, f32[1,384,384]{2,1,0:T(8,128)S(1)}) custom-call(bf16[2,4,192,256]{3,2,1,0:T(8,128)(2,1)S(1)} %get-tuple-element.117.t0, bf16[2,4,192,256]{3,2,1,0:T(8,128)(2,1)S(1)} %collective-permute-done.t1, ...), custom_call_target="tpu_custom_call" | custom-call | flops 1100000000 | bytes 1000 | tf_op jit(solution)/shard_map/pallas_call | solution.py:70
  53.6 2.1 %collective-permute-start.16 = (f32[1,384,384]{2,1,0:T(8,128)S(1)}, f32[1,384,384]{2,1,0:T(8,128)S(1)}, u32[]{:S(2)}, u32[]{:S(2)}) collective-permute-start(f32[1,384,384]{2,1,0:T(8,128)S(1)} %get-tuple-element.107), channel_id=1, source_target_pairs={{0,8},{1,9},{2,10},{3,11},{4,12},{5,13},{6,14},{7,15},{8,0},{9,1},... | collective-permute-start | bytes 1769480 | tf_op jit(solution)/shard_map/ppermute | solution.py:38
  56.8 1.5 %collective-permute-start.21 = (bf16[768,256]{1,0:T(8,128)(2,1)S(1)}, bf16[768,256]{1,0:T(8,128)(2,1)S(1)}, u32[]{:S(2)}, u32[]{:S(2)}) collective-permute-start(bf16[768,256]{1,0:T(8,128)(2,1)S(1)} %get-tuple-element.119.own), channel_id=1, source_target_pairs={{0,96},{1,97},{2,98},{3,99},{4,100},{5,101},{6,102},{7,103},{8,104... | collective-permute-start | bytes 1179656 | tf_op jit(solution)/shard_map/ppermute | solution.py:38
  59.1 1.5 %collective-permute-start.25 = (bf16[3,384,384]{2,1,0:T(8,128)(2,1)S(1)}, bf16[3,384,384]{2,1,0:T(8,128)(2,1)S(1)}, u32[]{:S(2)}, u32[]{:S(2)}) collective-permute-start(bf16[3,384,384]{2,1,0:T(8,128)(2,1)S(1)} %shard_map.93), channel_id=1, source_target_pairs={{0,16},{1,17},{2,18},{3,19},{4,20},{5,21},{6,22},{7,23},{8,24},{9,... | collective-permute-start | bytes 2654216 | tf_op jit(solution)/shard_map/ppermute | solution.py:38
  60.7 1.4 shard_map.94
  62.1 2.7 %collective-permute-start.20 = (bf16[384,256]{1,0:T(8,128)(2,1)S(1)}, bf16[384,256]{1,0:T(8,128)(2,1)S(1)}, u32[]{:S(2)}, u32[]{:S(2)}) collective-permute-start(bf16[384,256]{1,0:T(8,128)(2,1)S(1)} %get-tuple-element.114), channel_id=1, source_target_pairs={{0,96},{1,97},{2,98},{3,99},{4,100},{5,101},{6,102},{7,103},{8,104... | collective-permute-start | bytes 589832 | tf_op jit(solution)/shard_map/ppermute | solution.py:38
  64.8 2.7 %collective-permute-done.21.nxt = bf16[768,256]{1,0:T(8,128)(2,1)S(1)} collective-permute-done((bf16[768,256]{1,0:T(8,128)(2,1)S(1)}, bf16[768,256]{1,0:T(8,128)(2,1)S(1)}, u32[]{:S(2)}, u32[]{:S(2)}) %collective-permute-start.21) | collective-permute-done | bytes 393248 | tf_op jit(solution)/shard_map/ppermute | solution.py:38
  67.5 2.2 %collective-permute-done.22.prev = bf16[768,256]{1,0:T(8,128)(2,1)S(1)} collective-permute-done((bf16[768,256]{1,0:T(8,128)(2,1)S(1)}, bf16[768,256]{1,0:T(8,128)(2,1)S(1)}, u32[]{:S(2)}, u32[]{:S(2)}) %collective-permute-start.22) | collective-permute-done | bytes 393248 | tf_op jit(solution)/shard_map/ppermute | solution.py:38
  70.1 1.1 collective-permute-start.24
  71.3 1.6 %shard_map.96.refs_0_ = f32[4,768,256]{2,1,0:T(8,128)S(1)} custom-call(s32[26]{0:T(128)S(1)} %stack.123.numbers, bf16[3,384,256]{2,1,0:T(8,128)(2,1)S(1)} %shard_map.90.mine, bf16[3,384,256]{2,1,0:T(8,128)(2,1)S(1)} %collective-permute-done.11.theirs, bf16[768,256]{1,0:T(8,128)(2,1)S(1)} %get-tuple-element.92.own, ...), custom_call_target="tpu_custom_call" | custom-call | flops 1100000000 | bytes 1000 | tf_op jit(solution)/shard_map/pallas_call | solution.py:70
  72.9 1.0 collective-permute-done.19.low
  74.0 0.6 collective-permute-done.23.low
  74.6 2.7 %collective-permute-done.24.high = bf16[384,256]{1,0:T(8,128)(2,1)S(1)} collective-permute-done((bf16[384,256]{1,0:T(8,128)(2,1)S(1)}, bf16[384,256]{1,0:T(8,128)(2,1)S(1)}, u32[]{:S(2)}, u32[]{:S(2)}) %collective-permute-start.24) | collective-permute-done | bytes 196640 | tf_op jit(solution)/shard_map/ppermute | solution.py:38
  77.3 1.4 shard_map.98
  78.7 2.3 %collective-permute-start.26 = (f32[1,384,256]{2,1,0:T(8,128)S(1)}, f32[1,384,256]{2,1,0:T(8,128)S(1)}, u32[]{:S(2)}, u32[]{:S(2)}) collective-permute-start(f32[1,384,256]{2,1,0:T(8,128)S(1)} %get-tuple-element.125), channel_id=1, source_target_pairs={{0,8},{1,9},{2,10},{3,11},{4,12},{5,13},{6,14},{7,15},{8,0},{9,1},... | collective-permute-start | bytes 1179656 | tf_op jit(solution)/shard_map/ppermute | solution.py:38
  81.5 0.8 collective-permute-done.26.refs_0_
  82.3 0.6 collective-permute-done.27.refs_1_
  83.6 0.6 shard_map.100.mine
  84.8 2.6 %collective-permute-start.31 = (bf16[768,256]{1,0:T(8,128)(2,1)S(1)}, bf16[768,256]{1,0:T(8,128)(2,1)S(1)}, u32[]{:S(2)}, u32[]{:S(2)}) collective-permute-start(bf16[768,256]{1,0:T(8,128)(2,1)S(1)} %get-tuple-element.131), channel_id=1, source_target_pairs={{0,96},{1,97},{2,98},{3,99},{4,100},{5,101},{6,102},{7,103},{8,104... | collective-permute-start | bytes 1179656 | tf_op jit(solution)/shard_map/ppermute | solution.py:38
  87.7 2.7 %shard_map.101 = (f32[768,384]{1,0:T(8,128)S(1)}, f32[768,384]{1,0:T(8,128)S(1)}, bf16[384,384]{1,0:T(8,128)(2,1)S(1)}, bf16[384,384]{1,0:T(8,128)(2,1)S(1)}, f32[768,384]{1,0:T(8,128)S(1)}) custom-call(bf16[1024,768]{1,0:T(8,128)(2,1)S(1)} %get-tuple-element.90.tokens, bf16[1024,768]{1,0:T(8,128)(2,1)S(1)} %get-tuple-element.91.cotangents, ...), custom_call_target="tpu_custom_call" | custom-call | flops 1100000000 | bytes 1000 | tf_op jit(solution)/shard_map/pallas_call | solution.py:70
  90.5 2.7 %collective-permute-start.33 = (bf16[384,384]{1,0:T(8,128)(2,1)S(1)}, bf16[384,384]{1,0:T(8,128)(2,1)S(1)}, u32[]{:S(2)}, u32[]{:S(2)}) collective-permute-start(bf16[384,384]{1,0:T(8,128)(2,1)S(1)} %get-tuple-element.135), channel_id=1, source_target_pairs={{0,96},{1,97},{2,98},{3,99},{4,100},{5,101},{6,102},{7,103},{8,104... | collective-permute-start | bytes 884744 | tf_op jit(solution)/shard_map/ppermute | solution.py:38
  93.1 3.3 %collective-permute-done.30.r1 = bf16[768,256]{1,0:T(8,128)(2,1)S(1)} collective-permute-done((bf16[768,256]{1,0:T(8,128)(2,1)S(1)}, bf16[768,256]{1,0:T(8,128)(2,1)S(1)}, u32[]{:S(2)}, u32[]{:S(2)}) %collective-permute-start.30) | collective-permute-done | bytes 393248 | tf_op jit(solution)/shard_map/ppermute | solution.py:38
  96.5 2.6 %shard_map.103.refs_0_ = f32[4,768,256]{2,1,0:T(8,128)S(1)} custom-call(s32[26]{0:T(128)S(1)} %stack.123.numbers, bf16[3,384,384]{2,1,0:T(8,128)(2,1)S(1)} %shard_map.100.mine, bf16[3,384,384]{2,1,0:T(8,128)(2,1)S(1)} %collective-permute-done.29.theirs, bf16[768,384]{1,0:T(8,128)(2,1)S(1)} %get-tuple-element.101.own, ...), custom_call_target="tpu_custom_call" | custom-call | flops 1100000000 | bytes 1000 | tf_op jit(solution)/shard_map/pallas_call | solution.py:70
  99.0 3.7 %collective-permute-done.32.low = bf16[384,384]{1,0:T(8,128)(2,1)S(1)} collective-permute-done((bf16[384,384]{1,0:T(8,128)(2,1)S(1)}, bf16[384,384]{1,0:T(8,128)(2,1)S(1)}, u32[]{:S(2)}, u32[]{:S(2)}) %collective-permute-start.32) | collective-permute-done | bytes 294944 | tf_op jit(solution)/shard_map/ppermute | solution.py:38
  103.5 1.0 collective-permute-start.35
  104.5 2.7 %collective-permute-start.44 = (bf16[768,384]{1,0:T(8,128)(2,1)S(1)}, bf16[768,384]{1,0:T(8,128)(2,1)S(1)}, u32[]{:S(2)}, u32[]{:S(2)}) collective-permute-start(bf16[768,384]{1,0:T(8,128)(2,1)S(1)} %get-tuple-element.150), channel_id=1, source_target_pairs={{0,96},{1,97},{2,98},{3,99},{4,100},{5,101},{6,102},{7,103},{8,104... | collective-permute-start | bytes 1769480 | tf_op jit(solution)/shard_map/ppermute | solution.py:38
  107.2 1.7 %shard_map.105 = (f32[768,256]{1,0:T(8,128)S(1)}, bf16[768,256]{1,0:T(8,128)(2,1)S(1)}, bf16[768,256]{1,0:T(8,128)(2,1)S(1)}, bf16[768,256]{1,0:T(8,128)(2,1)S(1)}) custom-call(s32[26]{0:T(128)S(1)} %stack.123.numbers, bf16[3,384,256]{2,1,0:T(8,128)(2,1)S(1)} %shard_map.104.mine, bf16[3,384,256]{2,1,0:T(8,128)(2,1)S(1)} %collective-permute-done.35.theirs, ...), custom_call_target="tpu_custom_call" | custom-call | flops 1100000000 | bytes 1000 | tf_op jit(solution)/shard_map/pallas_call | solution.py:70
  108.9 1.3 collective-permute-start.36
  110.1 2.5 %collective-permute-start.37 = (bf16[768,256]{1,0:T(8,128)(2,1)S(1)}, bf16[768,256]{1,0:T(8,128)(2,1)S(1)}, u32[]{:S(2)}, u32[]{:S(2)}) collective-permute-start(bf16[768,256]{1,0:T(8,128)(2,1)S(1)} %get-tuple-element.141), channel_id=1, source_target_pairs={{0,4},{1,5},{2,6},{3,7},{4,0},{5,1},{6,2},{7,3},{8,12},{9,13},{10,... | collective-permute-start | bytes 1179656 | tf_op jit(solution)/shard_map/ppermute | solution.py:38
  112.6 1.1 collective-permute-start.38
  113.7 1.4 shard_map.108
  115.1 5.5 %collective-permute-done.43.r1 = bf16[768,384]{1,0:T(8,128)(2,1)S(1)} collective-permute-done((bf16[768,384]{1,0:T(8,128)(2,1)S(1)}, bf16[768,384]{1,0:T(8,128)(2,1)S(1)}, u32[]{:S(2)}, u32[]{:S(2)}) %collective-permute-start.43) | collective-permute-done | bytes 589856 | tf_op jit(solution)/shard_map/ppermute | solution.py:38
  120.6 2.7 %collective-permute-start.46 = (bf16[384,256]{1,0:T(8,128)(2,1)S(1)}, bf16[384,256]{1,0:T(8,128)(2,1)S(1)}, u32[]{:S(2)}, u32[]{:S(2)}) collective-permute-start(bf16[384,256]{1,0:T(8,128)(2,1)S(1)} %get-tuple-element.154), channel_id=1, source_target_pairs={{0,96},{1,97},{2,98},{3,99},{4,100},{5,101},{6,102},{7,103},{8,104... | collective-permute-start | bytes 589832 | tf_op jit(solution)/shard_map/ppermute | solution.py:38
  123.3 4.1 %collective-permute-done.45.low = bf16[384,256]{1,0:T(8,128)(2,1)S(1)} collective-permute-done((bf16[384,256]{1,0:T(8,128)(2,1)S(1)}, bf16[384,256]{1,0:T(8,128)(2,1)S(1)}, u32[]{:S(2)}, u32[]{:S(2)}) %collective-permute-start.45) | collective-permute-done | bytes 196640 | tf_op jit(solution)/shard_map/ppermute | solution.py:38
  127.6 2.7 %collective-permute-start.48 = (bf16[768,256]{1,0:T(8,128)(2,1)S(1)}, bf16[768,256]{1,0:T(8,128)(2,1)S(1)}, u32[]{:S(2)}, u32[]{:S(2)}) collective-permute-start(bf16[768,256]{1,0:T(8,128)(2,1)S(1)} %get-tuple-element.156), channel_id=1, source_target_pairs={{0,96},{1,97},{2,98},{3,99},{4,100},{5,101},{6,102},{7,103},{8,104... | collective-permute-start | bytes 1179656 | tf_op jit(solution)/shard_map/ppermute | solution.py:38
  130.2 0.7 shard_map.106
  131.0 0.7 collective-permute-start.39
  131.6 1.0 shard_map.110
  132.6 3.0 %collective-permute-start.40 = (bf16[192,256]{1,0:T(8,128)(2,1)S(1)}, bf16[192,256]{1,0:T(8,128)(2,1)S(1)}, u32[]{:S(2)}, u32[]{:S(2)}) collective-permute-start(bf16[192,256]{1,0:T(8,128)(2,1)S(1)} %get-tuple-element.144), channel_id=1, source_target_pairs={{0,16},{1,0},{2,18},{3,2},{4,20},{5,4},{6,22},{7,6},{8,24},{9,8},{... | collective-permute-start | bytes 294920 | tf_op jit(solution)/shard_map/ppermute | solution.py:38
  135.6 2.9 %collective-permute-start.41 = (bf16[192,256]{1,0:T(8,128)(2,1)S(1)}, bf16[192,256]{1,0:T(8,128)(2,1)S(1)}, u32[]{:S(2)}, u32[]{:S(2)}) collective-permute-start(bf16[192,256]{1,0:T(8,128)(2,1)S(1)} %get-tuple-element.145), channel_id=1, source_target_pairs={{0,8},{1,24},{2,10},{3,26},{4,12},{5,28},{6,14},{7,30},{8,0},{9,16... | collective-permute-start | bytes 294920 | tf_op jit(solution)/shard_map/ppermute | solution.py:38
  138.5 1.6 %collective-permute-start.42 = (bf16[192,256]{1,0:T(8,128)(2,1)S(1)}, bf16[192,256]{1,0:T(8,128)(2,1)S(1)}, u32[]{:S(2)}, u32[]{:S(2)}) collective-permute-start(bf16[192,256]{1,0:T(8,128)(2,1)S(1)} %get-tuple-element.146), channel_id=1, source_target_pairs={{0,24},{1,8},{2,26},{3,10},{4,28},{5,12},{6,30},{7,14},{8,16},{9,0... | collective-permute-start | bytes 294920 | tf_op jit(solution)/shard_map/ppermute | solution.py:38
  140.1 1.1 shard_map.111
  141.2 3.2 %collective-permute-done.42.b1 = bf16[192,256]{1,0:T(8,128)(2,1)S(1)} collective-permute-done((bf16[192,256]{1,0:T(8,128)(2,1)S(1)}, bf16[192,256]{1,0:T(8,128)(2,1)S(1)}, u32[]{:S(2)}, u32[]{:S(2)}) %collective-permute-start.42) | collective-permute-done | bytes 98336 | tf_op jit(solution)/shard_map/ppermute | solution.py:38
  144.4 1.3 shard_map.107
  145.7 0.9 shard_map.112
  (64 shorter events, 7.8 us)
Async XLA Ops:
  2.1 13.6 %collective-permute-start.3 = (bf16[768,256]{1,0:T(8,128)(2,1)S(1)}, bf16[768,256]{1,0:T(8,128)(2,1)S(1)}, u32[]{:S(2)}, u32[]{:S(2)}) collective-permute-start(bf16[768,256]{1,0:T(8,128)(2,1)S(1)} %get-tuple-element.92.own), channel_id=1, source_target_pairs={{0,96},{1,97},{2,98},{3,99},{4,100},{5,101},{6,102},{7,103},{8,104... | collective-permute-start | bytes 1179656 | tf_op jit(solution)/shard_map/ppermute | solution.py:38
  6.8 10.9 %collective-permute-start.4 = (bf16[768,256]{1,0:T(8,128)(2,1)S(1)}, bf16[768,256]{1,0:T(8,128)(2,1)S(1)}, u32[]{:S(2)}, u32[]{:S(2)}) collective-permute-start(bf16[768,256]{1,0:T(8,128)(2,1)S(1)} %get-tuple-element.92.own), channel_id=1, source_target_pairs={{0,32},{1,33},{2,34},{3,35},{4,36},{5,37},{6,38},{7,39},{8,40},{9,... | collective-permute-start | bytes 1179656 | tf_op jit(solution)/shard_map/ppermute | solution.py:38
  11.3 18.2 %collective-permute-start = (bf16[2,4,192,256]{3,2,1,0:T(8,128)(2,1)S(1)}, bf16[2,4,192,256]{3,2,1,0:T(8,128)(2,1)S(1)}, u32[]{:S(2)}, u32[]{:S(2)}) collective-permute-start(bf16[2,4,192,256]{3,2,1,0:T(8,128)(2,1)S(1)} %get-tuple-element.87), channel_id=1, source_target_pairs={{0,16},{1,17},{2,18},{3,19},{4,20},{5,21},{6,22},{7,23},{8,24},{9,... | collective-permute-start | bytes 2359304 | tf_op jit(solution)/shard_map/ppermute | solution.py:38
  12.7 16.8 %collective-permute-start.1 = (bf16[2,4,192,256]{3,2,1,0:T(8,128)(2,1)S(1)}, bf16[2,4,192,256]{3,2,1,0:T(8,128)(2,1)S(1)}, u32[]{:S(2)}, u32[]{:S(2)}) collective-permute-start(bf16[2,4,192,256]{3,2,1,0:T(8,128)(2,1)S(1)} %get-tuple-element.88), channel_id=1, source_target_pairs={{0,8},{1,9},{2,10},{3,11},{4,12},{5,13},{6,14},{7,15},{8,0},{9,1},... | collective-permute-start | bytes 2359304 | tf_op jit(solution)/shard_map/ppermute | solution.py:38
  13.9 20.7 %collective-permute-start.2 = (bf16[2,4,192,256]{3,2,1,0:T(8,128)(2,1)S(1)}, bf16[2,4,192,256]{3,2,1,0:T(8,128)(2,1)S(1)}, u32[]{:S(2)}, u32[]{:S(2)}) collective-permute-start(bf16[2,4,192,256]{3,2,1,0:T(8,128)(2,1)S(1)} %get-tuple-element.89), channel_id=1, source_target_pairs={{0,25},{1,24},{2,27},{3,26},{4,29},{5,28},{6,31},{7,30},{8,17},{9,... | collective-permute-start | bytes 2359304 | tf_op jit(solution)/shard_map/ppermute | solution.py:38
  17.7 4.9 %collective-permute-start.5 = (bf16[384,256]{1,0:T(8,128)(2,1)S(1)}, bf16[384,256]{1,0:T(8,128)(2,1)S(1)}, u32[]{:S(2)}, u32[]{:S(2)}) collective-permute-start(bf16[384,256]{1,0:T(8,128)(2,1)S(1)} %get-tuple-element.93), channel_id=1, source_target_pairs={{0,96},{1,97},{2,98},{3,99},{4,100},{5,101},{6,102},{7,103},{8,104... | collective-permute-start | bytes 589832 | tf_op jit(solution)/shard_map/ppermute | solution.py:38
  18.8 6.8 %collective-permute-start.6 = (bf16[384,256]{1,0:T(8,128)(2,1)S(1)}, bf16[384,256]{1,0:T(8,128)(2,1)S(1)}, u32[]{:S(2)}, u32[]{:S(2)}) collective-permute-start(bf16[384,256]{1,0:T(8,128)(2,1)S(1)} %get-tuple-element.94), channel_id=1, source_target_pairs={{0,32},{1,33},{2,34},{3,35},{4,36},{5,37},{6,38},{7,39},{8,40},{9,... | collective-permute-start | bytes 589832 | tf_op jit(solution)/shard_map/ppermute | solution.py:38
  22.6 14.9 %collective-permute-start.12 = (bf16[768,384]{1,0:T(8,128)(2,1)S(1)}, bf16[768,384]{1,0:T(8,128)(2,1)S(1)}, u32[]{:S(2)}, u32[]{:S(2)}) collective-permute-start(bf16[768,384]{1,0:T(8,128)(2,1)S(1)} %get-tuple-element.101.own), channel_id=1, source_target_pairs={{0,96},{1,97},{2,98},{3,99},{4,100},{5,101},{6,102},{7,103},{8,104... | collective-permute-start | bytes 1769480 | tf_op jit(solution)/shard_map/ppermute | solution.py:38
  25.5 14.0 %collective-permute-start.13 = (bf16[768,384]{1,0:T(8,128)(2,1)S(1)}, bf16[768,384]{1,0:T(8,128)(2,1)S(1)}, u32[]{:S(2)}, u32[]{:S(2)}) collective-permute-start(bf16[768,384]{1,0:T(8,128)(2,1)S(1)} %get-tuple-element.101.own), channel_id=1, source_target_pairs={{0,32},{1,33},{2,34},{3,35},{4,36},{5,37},{6,38},{7,39},{8,40},{9,... | collective-permute-start | bytes 1769480 | tf_op jit(solution)/shard_map/ppermute | solution.py:38
  36.0 1.8 %collective-permute-start.7 = (f32[1,384,256]{2,1,0:T(8,128)S(1)}, f32[1,384,256]{2,1,0:T(8,128)S(1)}, u32[]{:S(2)}, u32[]{:S(2)}) collective-permute-start(f32[1,384,256]{2,1,0:T(8,128)S(1)} %get-tuple-element.96), channel_id=1, source_target_pairs={{0,8},{1,9},{2,10},{3,11},{4,12},{5,13},{6,14},{7,15},{8,0},{9,1},... | collective-permute-start | bytes 1179656 | tf_op jit(solution)/shard_map/ppermute | solution.py:38
  36.1 2.3 %collective-permute-start.8 = (f32[1,384,256]{2,1,0:T(8,128)S(1)}, f32[1,384,256]{2,1,0:T(8,128)S(1)}, u32[]{:S(2)}, u32[]{:S(2)}) collective-permute-start(f32[1,384,256]{2,1,0:T(8,128)S(1)} %get-tuple-element.97), channel_id=1, source_target_pairs={{0,8},{1,9},{2,10},{3,11},{4,12},{5,13},{6,14},{7,15},{8,0},{9,1},... | collective-permute-start | bytes 1179656 | tf_op jit(solution)/shard_map/ppermute | solution.py:38
  36.6 2.3 %collective-permute-start.9 = (f32[1,384,256]{2,1,0:T(8,128)S(1)}, f32[1,384,256]{2,1,0:T(8,128)S(1)}, u32[]{:S(2)}, u32[]{:S(2)}) collective-permute-start(f32[1,384,256]{2,1,0:T(8,128)S(1)} %get-tuple-element.98), channel_id=1, source_target_pairs={{0,8},{1,9},{2,10},{3,11},{4,12},{5,13},{6,14},{7,15},{8,0},{9,1},... | collective-permute-start | bytes 1179656 | tf_op jit(solution)/shard_map/ppermute | solution.py:38
  39.0 17.2 %collective-permute-start.10 = (bf16[3,384,256]{2,1,0:T(8,128)(2,1)S(1)}, bf16[3,384,256]{2,1,0:T(8,128)(2,1)S(1)}, u32[]{:S(2)}, u32[]{:S(2)}) collective-permute-start(bf16[3,384,256]{2,1,0:T(8,128)(2,1)S(1)} %shard_map.89), channel_id=1, source_target_pairs={{0,16},{1,17},{2,18},{3,19},{4,20},{5,21},{6,22},{7,23},{8,24},{9,... | collective-permute-start | bytes 1769480 | tf_op jit(solution)/shard_map/ppermute | solution.py:38
  39.6 8.1 %collective-permute-start.14 = (bf16[384,384]{1,0:T(8,128)(2,1)S(1)}, bf16[384,384]{1,0:T(8,128)(2,1)S(1)}, u32[]{:S(2)}, u32[]{:S(2)}) collective-permute-start(bf16[384,384]{1,0:T(8,128)(2,1)S(1)} %get-tuple-element.103), channel_id=1, source_target_pairs={{0,96},{1,97},{2,98},{3,99},{4,100},{5,101},{6,102},{7,103},{8,104... | collective-permute-start | bytes 884744 | tf_op jit(solution)/shard_map/ppermute | solution.py:38
  42.2 8.6 %collective-permute-start.15 = (bf16[384,384]{1,0:T(8,128)(2,1)S(1)}, bf16[384,384]{1,0:T(8,128)(2,1)S(1)}, u32[]{:S(2)}, u32[]{:S(2)}) collective-permute-start(bf16[384,384]{1,0:T(8,128)(2,1)S(1)} %get-tuple-element.104), channel_id=1, source_target_pairs={{0,32},{1,33},{2,34},{3,35},{4,36},{5,37},{6,38},{7,39},{8,40},{9,... | collective-permute-start | bytes 884744 | tf_op jit(solution)/shard_map/ppermute | solution.py:38
  53.6 4.8 %collective-permute-start.16 = (f32[1,384,384]{2,1,0:T(8,128)S(1)}, f32[1,384,384]{2,1,0:T(8,128)S(1)}, u32[]{:S(2)}, u32[]{:S(2)}) collective-permute-start(f32[1,384,384]{2,1,0:T(8,128)S(1)} %get-tuple-element.107), channel_id=1, source_target_pairs={{0,8},{1,9},{2,10},{3,11},{4,12},{5,13},{6,14},{7,15},{8,0},{9,1},... | collective-permute-start | bytes 1769480 | tf_op jit(solution)/shard_map/ppermute | solution.py:38
  55.7 2.8 %collective-permute-start.17 = (f32[1,384,384]{2,1,0:T(8,128)S(1)}, f32[1,384,384]{2,1,0:T(8,128)S(1)}, u32[]{:S(2)}, u32[]{:S(2)}) collective-permute-start(f32[1,384,384]{2,1,0:T(8,128)S(1)} %get-tuple-element.108), channel_id=1, source_target_pairs={{0,8},{1,9},{2,10},{3,11},{4,12},{5,13},{6,14},{7,15},{8,0},{9,1},... | collective-permute-start | bytes 1769480 | tf_op jit(solution)/shard_map/ppermute | solution.py:38
  55.7 3.2 %collective-permute-start.18 = (f32[1,384,384]{2,1,0:T(8,128)S(1)}, f32[1,384,384]{2,1,0:T(8,128)S(1)}, u32[]{:S(2)}, u32[]{:S(2)}) collective-permute-start(f32[1,384,384]{2,1,0:T(8,128)S(1)} %get-tuple-element.109), channel_id=1, source_target_pairs={{0,8},{1,9},{2,10},{3,11},{4,12},{5,13},{6,14},{7,15},{8,0},{9,1},... | collective-permute-start | bytes 1769480 | tf_op jit(solution)/shard_map/ppermute | solution.py:38
  56.6 4.0 %collective-permute-start.11 = (bf16[3,384,256]{2,1,0:T(8,128)(2,1)S(1)}, bf16[3,384,256]{2,1,0:T(8,128)(2,1)S(1)}, u32[]{:S(2)}, u32[]{:S(2)}) collective-permute-start(bf16[3,384,256]{2,1,0:T(8,128)(2,1)S(1)} %shard_map.90.mine), channel_id=1, source_target_pairs={{0,8},{1,9},{2,10},{3,11},{4,12},{5,13},{6,14},{7,15},{8,0},{9,1},... | collective-permute-start | bytes 1769480 | tf_op jit(solution)/shard_map/ppermute | solution.py:38
  56.8 10.6 %collective-permute-start.21 = (bf16[768,256]{1,0:T(8,128)(2,1)S(1)}, bf16[768,256]{1,0:T(8,128)(2,1)S(1)}, u32[]{:S(2)}, u32[]{:S(2)}) collective-permute-start(bf16[768,256]{1,0:T(8,128)(2,1)S(1)} %get-tuple-element.119.own), channel_id=1, source_target_pairs={{0,96},{1,97},{2,98},{3,99},{4,100},{5,101},{6,102},{7,103},{8,104... | collective-permute-start | bytes 1179656 | tf_op jit(solution)/shard_map/ppermute | solution.py:38
  58.3 11.3 %collective-permute-start.22 = (bf16[768,256]{1,0:T(8,128)(2,1)S(1)}, bf16[768,256]{1,0:T(8,128)(2,1)S(1)}, u32[]{:S(2)}, u32[]{:S(2)}) collective-permute-start(bf16[768,256]{1,0:T(8,128)(2,1)S(1)} %get-tuple-element.119.own), channel_id=1, source_target_pairs={{0,32},{1,33},{2,34},{3,35},{4,36},{5,37},{6,38},{7,39},{8,40},{9,... | collective-permute-start | bytes 1179656 | tf_op jit(solution)/shard_map/ppermute | solution.py:38
  59.1 22.4 %collective-permute-start.25 = (bf16[3,384,384]{2,1,0:T(8,128)(2,1)S(1)}, bf16[3,384,384]{2,1,0:T(8,128)(2,1)S(1)}, u32[]{:S(2)}, u32[]{:S(2)}) collective-permute-start(bf16[3,384,384]{2,1,0:T(8,128)(2,1)S(1)} %shard_map.93), channel_id=1, source_target_pairs={{0,16},{1,17},{2,18},{3,19},{4,20},{5,21},{6,22},{7,23},{8,24},{9,... | collective-permute-start | bytes 2654216 | tf_op jit(solution)/shard_map/ppermute | solution.py:38
  62.0 11.9 %collective-permute-start.19 = (bf16[384,256]{1,0:T(8,128)(2,1)S(1)}, bf16[384,256]{1,0:T(8,128)(2,1)S(1)}, u32[]{:S(2)}, u32[]{:S(2)}) collective-permute-start(bf16[384,256]{1,0:T(8,128)(2,1)S(1)} %get-tuple-element.113), channel_id=1, source_target_pairs={{0,32},{1,33},{2,34},{3,35},{4,36},{5,37},{6,38},{7,39},{8,40},{9,... | collective-permute-start | bytes 589832 | tf_op jit(solution)/shard_map/ppermute | solution.py:38
  62.1 11.8 %collective-permute-start.20 = (bf16[384,256]{1,0:T(8,128)(2,1)S(1)}, bf16[384,256]{1,0:T(8,128)(2,1)S(1)}, u32[]{:S(2)}, u32[]{:S(2)}) collective-permute-start(bf16[384,256]{1,0:T(8,128)(2,1)S(1)} %get-tuple-element.114), channel_id=1, source_target_pairs={{0,96},{1,97},{2,98},{3,99},{4,100},{5,101},{6,102},{7,103},{8,104... | collective-permute-start | bytes 589832 | tf_op jit(solution)/shard_map/ppermute | solution.py:38
  69.7 4.9 %collective-permute-start.23 = (bf16[384,256]{1,0:T(8,128)(2,1)S(1)}, bf16[384,256]{1,0:T(8,128)(2,1)S(1)}, u32[]{:S(2)}, u32[]{:S(2)}) collective-permute-start(bf16[384,256]{1,0:T(8,128)(2,1)S(1)} %get-tuple-element.121), channel_id=1, source_target_pairs={{0,96},{1,97},{2,98},{3,99},{4,100},{5,101},{6,102},{7,103},{8,104... | collective-permute-start | bytes 589832 | tf_op jit(solution)/shard_map/ppermute | solution.py:38
  70.1 7.2 %collective-permute-start.24 = (bf16[384,256]{1,0:T(8,128)(2,1)S(1)}, bf16[384,256]{1,0:T(8,128)(2,1)S(1)}, u32[]{:S(2)}, u32[]{:S(2)}) collective-permute-start(bf16[384,256]{1,0:T(8,128)(2,1)S(1)} %get-tuple-element.122), channel_id=1, source_target_pairs={{0,32},{1,33},{2,34},{3,35},{4,36},{5,37},{6,38},{7,39},{8,40},{9,... | collective-permute-start | bytes 589832 | tf_op jit(solution)/shard_map/ppermute | solution.py:38
  78.7 3.6 %collective-permute-start.26 = (f32[1,384,256]{2,1,0:T(8,128)S(1)}, f32[1,384,256]{2,1,0:T(8,128)S(1)}, u32[]{:S(2)}, u32[]{:S(2)}) collective-permute-start(f32[1,384,256]{2,1,0:T(8,128)S(1)} %get-tuple-element.125), channel_id=1, source_target_pairs={{0,8},{1,9},{2,10},{3,11},{4,12},{5,13},{6,14},{7,15},{8,0},{9,1},... | collective-permute-start | bytes 1179656 | tf_op jit(solution)/shard_map/ppermute | solution.py:38
  81.0 1.9 %collective-permute-start.27 = (f32[1,384,256]{2,1,0:T(8,128)S(1)}, f32[1,384,256]{2,1,0:T(8,128)S(1)}, u32[]{:S(2)}, u32[]{:S(2)}) collective-permute-start(f32[1,384,256]{2,1,0:T(8,128)S(1)} %get-tuple-element.126), channel_id=1, source_target_pairs={{0,8},{1,9},{2,10},{3,11},{4,12},{5,13},{6,14},{7,15},{8,0},{9,1},... | collective-permute-start | bytes 1179656 | tf_op jit(solution)/shard_map/ppermute | solution.py:38
  81.1 2.4 %collective-permute-start.28 = (f32[1,384,256]{2,1,0:T(8,128)S(1)}, f32[1,384,256]{2,1,0:T(8,128)S(1)}, u32[]{:S(2)}, u32[]{:S(2)}) collective-permute-start(f32[1,384,256]{2,1,0:T(8,128)S(1)} %get-tuple-element.127), channel_id=1, source_target_pairs={{0,8},{1,9},{2,10},{3,11},{4,12},{5,13},{6,14},{7,15},{8,0},{9,1},... | collective-permute-start | bytes 1179656 | tf_op jit(solution)/shard_map/ppermute | solution.py:38
  84.2 3.5 %collective-permute-start.29 = (bf16[3,384,384]{2,1,0:T(8,128)(2,1)S(1)}, bf16[3,384,384]{2,1,0:T(8,128)(2,1)S(1)}, u32[]{:S(2)}, u32[]{:S(2)}) collective-permute-start(bf16[3,384,384]{2,1,0:T(8,128)(2,1)S(1)} %shard_map.100.mine), channel_id=1, source_target_pairs={{0,8},{1,9},{2,10},{3,11},{4,12},{5,13},{6,14},{7,15},{8,0},{9,1},... | collective-permute-start | bytes 2654216 | tf_op jit(solution)/shard_map/ppermute | solution.py:38
  84.7 11.8 %collective-permute-start.30 = (bf16[768,256]{1,0:T(8,128)(2,1)S(1)}, bf16[768,256]{1,0:T(8,128)(2,1)S(1)}, u32[]{:S(2)}, u32[]{:S(2)}) collective-permute-start(bf16[768,256]{1,0:T(8,128)(2,1)S(1)} %get-tuple-element.115), channel_id=1, source_target_pairs={{0,32},{1,33},{2,34},{3,35},{4,36},{5,37},{6,38},{7,39},{8,40},{9,... | collective-permute-start | bytes 1179656 | tf_op jit(solution)/shard_map/ppermute | solution.py:38
  84.8 11.7 %collective-permute-start.31 = (bf16[768,256]{1,0:T(8,128)(2,1)S(1)}, bf16[768,256]{1,0:T(8,128)(2,1)S(1)}, u32[]{:S(2)}, u32[]{:S(2)}) collective-permute-start(bf16[768,256]{1,0:T(8,128)(2,1)S(1)} %get-tuple-element.131), channel_id=1, source_target_pairs={{0,96},{1,97},{2,98},{3,99},{4,100},{5,101},{6,102},{7,103},{8,104... | collective-permute-start | bytes 1179656 | tf_op jit(solution)/shard_map/ppermute | solution.py:38
  87.3 15.6 %collective-permute-start.34 = (bf16[3,384,256]{2,1,0:T(8,128)(2,1)S(1)}, bf16[3,384,256]{2,1,0:T(8,128)(2,1)S(1)}, u32[]{:S(2)}, u32[]{:S(2)}) collective-permute-start(bf16[3,384,256]{2,1,0:T(8,128)(2,1)S(1)} %shard_map.99), channel_id=1, source_target_pairs={{0,16},{1,17},{2,18},{3,19},{4,20},{5,21},{6,22},{7,23},{8,24},{9,... | collective-permute-start | bytes 1769480 | tf_op jit(solution)/shard_map/ppermute | solution.py:38
  90.4 12.4 %collective-permute-start.32 = (bf16[384,384]{1,0:T(8,128)(2,1)S(1)}, bf16[384,384]{1,0:T(8,128)(2,1)S(1)}, u32[]{:S(2)}, u32[]{:S(2)}) collective-permute-start(bf16[384,384]{1,0:T(8,128)(2,1)S(1)} %get-tuple-element.134), channel_id=1, source_target_pairs={{0,32},{1,33},{2,34},{3,35},{4,36},{5,37},{6,38},{7,39},{8,40},{9,... | collective-permute-start | bytes 884744 | tf_op jit(solution)/shard_map/ppermute | solution.py:38
  90.5 12.3 %collective-permute-start.33 = (bf16[384,384]{1,0:T(8,128)(2,1)S(1)}, bf16[384,384]{1,0:T(8,128)(2,1)S(1)}, u32[]{:S(2)}, u32[]{:S(2)}) collective-permute-start(bf16[384,384]{1,0:T(8,128)(2,1)S(1)} %get-tuple-element.135), channel_id=1, source_target_pairs={{0,96},{1,97},{2,98},{3,99},{4,100},{5,101},{6,102},{7,103},{8,104... | collective-permute-start | bytes 884744 | tf_op jit(solution)/shard_map/ppermute | solution.py:38
  103.5 3.7 %collective-permute-start.35 = (bf16[3,384,256]{2,1,0:T(8,128)(2,1)S(1)}, bf16[3,384,256]{2,1,0:T(8,128)(2,1)S(1)}, u32[]{:S(2)}, u32[]{:S(2)}) collective-permute-start(bf16[3,384,256]{2,1,0:T(8,128)(2,1)S(1)} %shard_map.104.mine), channel_id=1, source_target_pairs={{0,8},{1,9},{2,10},{3,11},{4,12},{5,13},{6,14},{7,15},{8,0},{9,1},... | collective-permute-start | bytes 1769480 | tf_op jit(solution)/shard_map/ppermute | solution.py:38
  104.5 16.1 %collective-permute-start.43 = (bf16[768,384]{1,0:T(8,128)(2,1)S(1)}, bf16[768,384]{1,0:T(8,128)(2,1)S(1)}, u32[]{:S(2)}, u32[]{:S(2)}) collective-permute-start(bf16[768,384]{1,0:T(8,128)(2,1)S(1)} %get-tuple-element.136), channel_id=1, source_target_pairs={{0,32},{1,33},{2,34},{3,35},{4,36},{5,37},{6,38},{7,39},{8,40},{9,... | collective-permute-start | bytes 1769480 | tf_op jit(solution)/shard_map/ppermute | solution.py:38
  104.5 16.1 %collective-permute-start.44 = (bf16[768,384]{1,0:T(8,128)(2,1)S(1)}, bf16[768,384]{1,0:T(8,128)(2,1)S(1)}, u32[]{:S(2)}, u32[]{:S(2)}) collective-permute-start(bf16[768,384]{1,0:T(8,128)(2,1)S(1)} %get-tuple-element.150), channel_id=1, source_target_pairs={{0,96},{1,97},{2,98},{3,99},{4,100},{5,101},{6,102},{7,103},{8,104... | collective-permute-start | bytes 1769480 | tf_op jit(solution)/shard_map/ppermute | solution.py:38
  108.9 21.4 %collective-permute-start.36 = (bf16[768,256]{1,0:T(8,128)(2,1)S(1)}, bf16[768,256]{1,0:T(8,128)(2,1)S(1)}, u32[]{:S(2)}, u32[]{:S(2)}) collective-permute-start(bf16[768,256]{1,0:T(8,128)(2,1)S(1)} %get-tuple-element.140), channel_id=1, source_target_pairs={{0,2},{1,3},{2,4},{3,5},{4,6},{5,7},{6,0},{7,1},{8,10},{9,11},{10,... | collective-permute-start | bytes 1179656 | tf_op jit(solution)/shard_map/ppermute | solution.py:38
  110.1 20.1 %collective-permute-start.37 = (bf16[768,256]{1,0:T(8,128)(2,1)S(1)}, bf16[768,256]{1,0:T(8,128)(2,1)S(1)}, u32[]{:S(2)}, u32[]{:S(2)}) collective-permute-start(bf16[768,256]{1,0:T(8,128)(2,1)S(1)} %get-tuple-element.141), channel_id=1, source_target_pairs={{0,4},{1,5},{2,6},{3,7},{4,0},{5,1},{6,2},{7,3},{8,12},{9,13},{10,... | collective-permute-start | bytes 1179656 | tf_op jit(solution)/shard_map/ppermute | solution.py:38
  112.6 17.7 %collective-permute-start.38 = (bf16[768,256]{1,0:T(8,128)(2,1)S(1)}, bf16[768,256]{1,0:T(8,128)(2,1)S(1)}, u32[]{:S(2)}, u32[]{:S(2)}) collective-permute-start(bf16[768,256]{1,0:T(8,128)(2,1)S(1)} %get-tuple-element.142), channel_id=1, source_target_pairs={{0,6},{1,7},{2,0},{3,1},{4,2},{5,3},{6,4},{7,5},{8,14},{9,15},{10,... | collective-permute-start | bytes 1179656 | tf_op jit(solution)/shard_map/ppermute | solution.py:38
  120.6 6.8 %collective-permute-start.45 = (bf16[384,256]{1,0:T(8,128)(2,1)S(1)}, bf16[384,256]{1,0:T(8,128)(2,1)S(1)}, u32[]{:S(2)}, u32[]{:S(2)}) collective-permute-start(bf16[384,256]{1,0:T(8,128)(2,1)S(1)} %get-tuple-element.153), channel_id=1, source_target_pairs={{0,32},{1,33},{2,34},{3,35},{4,36},{5,37},{6,38},{7,39},{8,40},{9,... | collective-permute-start | bytes 589832 | tf_op jit(solution)/shard_map/ppermute | solution.py:38
  120.6 6.8 %collective-permute-start.46 = (bf16[384,256]{1,0:T(8,128)(2,1)S(1)}, bf16[384,256]{1,0:T(8,128)(2,1)S(1)}, u32[]{:S(2)}, u32[]{:S(2)}) collective-permute-start(bf16[384,256]{1,0:T(8,128)(2,1)S(1)} %get-tuple-element.154), channel_id=1, source_target_pairs={{0,96},{1,97},{2,98},{3,99},{4,100},{5,101},{6,102},{7,103},{8,104... | collective-permute-start | bytes 589832 | tf_op jit(solution)/shard_map/ppermute | solution.py:38
  127.5 18.2 %collective-permute-start.47 = (bf16[768,256]{1,0:T(8,128)(2,1)S(1)}, bf16[768,256]{1,0:T(8,128)(2,1)S(1)}, u32[]{:S(2)}, u32[]{:S(2)}) collective-permute-start(bf16[768,256]{1,0:T(8,128)(2,1)S(1)} %get-tuple-element.155), channel_id=1, source_target_pairs={{0,32},{1,33},{2,34},{3,35},{4,36},{5,37},{6,38},{7,39},{8,40},{9,... | collective-permute-start | bytes 1179656 | tf_op jit(solution)/shard_map/ppermute | solution.py:38
  127.6 18.2 %collective-permute-start.48 = (bf16[768,256]{1,0:T(8,128)(2,1)S(1)}, bf16[768,256]{1,0:T(8,128)(2,1)S(1)}, u32[]{:S(2)}, u32[]{:S(2)}) collective-permute-start(bf16[768,256]{1,0:T(8,128)(2,1)S(1)} %get-tuple-element.156), channel_id=1, source_target_pairs={{0,96},{1,97},{2,98},{3,99},{4,100},{5,101},{6,102},{7,103},{8,104... | collective-permute-start | bytes 1179656 | tf_op jit(solution)/shard_map/ppermute | solution.py:38
  131.0 7.5 %collective-permute-start.39 = (bf16[192,256]{1,0:T(8,128)(2,1)S(1)}, bf16[192,256]{1,0:T(8,128)(2,1)S(1)}, u32[]{:S(2)}, u32[]{:S(2)}) collective-permute-start(bf16[192,256]{1,0:T(8,128)(2,1)S(1)} %get-tuple-element.143), channel_id=1, source_target_pairs={{0,0},{1,16},{2,2},{3,18},{4,4},{5,20},{6,6},{7,22},{8,8},{9,24},{... | collective-permute-start | bytes 294920 | tf_op jit(solution)/shard_map/ppermute | solution.py:38
  132.6 8.6 %collective-permute-start.40 = (bf16[192,256]{1,0:T(8,128)(2,1)S(1)}, bf16[192,256]{1,0:T(8,128)(2,1)S(1)}, u32[]{:S(2)}, u32[]{:S(2)}) collective-permute-start(bf16[192,256]{1,0:T(8,128)(2,1)S(1)} %get-tuple-element.144), channel_id=1, source_target_pairs={{0,16},{1,0},{2,18},{3,2},{4,20},{5,4},{6,22},{7,6},{8,24},{9,8},{... | collective-permute-start | bytes 294920 | tf_op jit(solution)/shard_map/ppermute | solution.py:38
  135.6 5.6 %collective-permute-start.41 = (bf16[192,256]{1,0:T(8,128)(2,1)S(1)}, bf16[192,256]{1,0:T(8,128)(2,1)S(1)}, u32[]{:S(2)}, u32[]{:S(2)}) collective-permute-start(bf16[192,256]{1,0:T(8,128)(2,1)S(1)} %get-tuple-element.145), channel_id=1, source_target_pairs={{0,8},{1,24},{2,10},{3,26},{4,12},{5,28},{6,14},{7,30},{8,0},{9,16... | collective-permute-start | bytes 294920 | tf_op jit(solution)/shard_map/ppermute | solution.py:38
  138.5 5.9 %collective-permute-start.42 = (bf16[192,256]{1,0:T(8,128)(2,1)S(1)}, bf16[192,256]{1,0:T(8,128)(2,1)S(1)}, u32[]{:S(2)}, u32[]{:S(2)}) collective-permute-start(bf16[192,256]{1,0:T(8,128)(2,1)S(1)} %get-tuple-element.146), channel_id=1, source_target_pairs={{0,24},{1,8},{2,26},{3,10},{4,28},{5,12},{6,30},{7,14},{8,16},{9,0... | collective-permute-start | bytes 294920 | tf_op jit(solution)/shard_map/ppermute | solution.py:38
